TPU v7x, 32 devices: a whole 2x2x4 slice. The times are simulated.
32 devices in a mesh: seq: 8 (over z, x), head: 4 (over y, core).
Axes of the slice: x: 2, y: 2, z: 4, core: 2. Of those that a mesh axis runs over, the one named last changes fastest.
Arguments:
- block_in: bfloat16 [4096, 1024], P('seq'), may hold values from -6 to 6
- seq_start: int32 [10], replicated, may hold values from 0 to 4095, as said below
- attn_gain: float32 [1024], replicated, may hold values from 0.5 to 1.5
- q_weight: bfloat16 [1024, 1024], P(None, 'head'), may hold values from -0.1875 to 0.1875
- k_weight: bfloat16 [1024, 2048], P(None, 'head'), may hold values from -0.1875 to 0.1875
- v_weight: bfloat16 [1024, 2048], P(None, 'head'), may hold values from -0.1875 to 0.1875
- conv_q: float32 [4, 1024], P(None, 'head'), may hold values from -3 to 3
- conv_k: float32 [4, 2048], P(None, 'head'), may hold values from -3 to 3
- conv_v: float32 [4, 2048], P(None, 'head'), may hold values from -3 to 3
- beta_weight: bfloat16 [1024, 16], P(None, 'head'), may hold values from -0.1875 to 0.1875
- decay_weight: bfloat16 [1024, 8], P(None, 'head'), may hold values from -0.1875 to 0.1875
- a_log: float32 [8], P('head'), may hold values from -10 to -3.5
- dt_bias: float32 [8], P('head'), may hold values from -2 to 1
- outgate_weight: bfloat16 [1024, 1024], P(None, 'head'), may hold values from -0.1875 to 0.1875
- o_gain: float32 [128], replicated, may hold values from 0.5 to 1.5
- out_weight: bfloat16 [1024, 1024], P('head'), may hold values from -0.3125 to 0.3125
- mlp_gain: float32 [1024], replicated, may hold values from 0.5 to 1.5
- gate_weight: bfloat16 [1024, 2816], P(None, 'head'), may hold values from -0.1875 to 0.1875
- up_weight: bfloat16 [1024, 2816], P(None, 'head'), may hold values from -0.1875 to 0.1875
- down_weight: bfloat16 [2816, 1024], P('head'), may hold values from -0.1875 to 0.1875
- out_grad: bfloat16 [4096, 1024], P('seq'), may hold values from -6 to 6
Outputs:
- output: bfloat16 [4096, 1024], P('seq')
- grad_input: bfloat16 [4096, 1024], P('seq')
- grad_attn_gain: float32 [1024], replicated
- grad_q_weight: float32 [1024, 1024], P(None, 'head')
- grad_k_weight: float32 [1024, 2048], P(None, 'head')
- grad_v_weight: float32 [1024, 2048], P(None, 'head')
- grad_conv_q: float32 [4, 1024], P(None, 'head')
- grad_conv_k: float32 [4, 2048], P(None, 'head')
- grad_conv_v: float32 [4, 2048], P(None, 'head')
- grad_beta_weight: float32 [1024, 16], P(None, 'head')
- grad_decay_weight: float32 [1024, 8], P(None, 'head')
- grad_a_log: float32 [8], P('head')
- grad_dt_bias: float32 [8], P('head')
- grad_outgate_weight: float32 [1024, 1024], P(None, 'head')
- grad_o_gain: float32 [128], replicated
- grad_out_weight: float32 [1024, 1024], P('head')
- grad_mlp_gain: float32 [1024], replicated
- grad_gate_weight: float32 [1024, 2816], P(None, 'head')
- grad_up_weight: float32 [1024, 2816], P(None, 'head')
- grad_down_weight: float32 [2816, 1024], P('head')
Inputs may be any that keep to these rules, and one draw needn't show every extreme that they name: seq_start holds the first token of each packed sequence in increasing order, the first being 0; two sequences have about 4096 // 4 tokens and eight about 4096 // 16, in an order drawn from the seed, each boundary moved by fewer than 64 tokens; every entry after the first is odd.
All inputs are finite; a program needn't handle non-finite values.
Results may differ from a plain program's by a relative error of at most 0.018.
The roundings to bfloat16 on the way count: a program that leaves them out, or rounds other values in their place, can miss the bound.
Values may be sent and summed in bfloat16 or wider, within the bound.
No kernel may reach another device: no remote copies, remote signals or barrier semaphores. Data moves between devices by JAX's collectives and lax.ppermute only.
A program may use at most 192 MiB of HBM per device.

v0:
```python
import jax
import jax.numpy as jnp
from jax import lax
from jax.sharding import PartitionSpec as P

NH = 2
GROUP = 64


HIGH_ACCURACY = lax.Precision.HIGHEST
EPSILON = 1e-06


def from_behind(value, axis, steps):
    count = lax.axis_size(axis)
    leading, last = (max(0, -steps), min(count, count - steps))
    return lax.ppermute(value, axis, [(source, source + steps) for source in range(leading, last)])


def carried_in(value, axis, join, neutral):
    count, mine = (lax.axis_size(axis), lax.axis_index(axis))
    pieces = jax.tree.map(lambda part: lax.all_gather(part, axis), value)
    total = jax.tree.map(
        lambda part, zero: jnp.full_like(part, 0) + jnp.asarray(zero, part.dtype), value, neutral
    )

    def carried_lap(position, total):
        longer = join(total, jax.tree.map(lambda part: part[position], pieces))
        return jax.tree.map(lambda new, old: jnp.where(position < mine, new, old), longer, total)

    return lax.fori_loop(0, count - 1, carried_lap, total)


def prefix_2(shard, axis, combine, identity):
    size, position = (lax.axis_size(axis), lax.axis_index(axis))
    everything = jax.tree.map(
        lambda part, kind: lax.all_gather(part.astype(kind), axis),
        shard,
        jax.tree.map(lambda a: jnp.bfloat16 if a.dtype == jnp.float32 else a.dtype, shard),
    )
    start = jax.tree.map(
        lambda part, zero: jnp.broadcast_to(jnp.asarray(zero, part.dtype), part.shape),
        shard,
        identity,
    )

    def prefix_lap(k, before):
        at = size - 1 - k
        reached = at > position
        new = combine(
            before, jax.tree.map(lambda part, own: part[at].astype(own.dtype), everything, shard)
        )
        return jax.tree.map(lambda a, b: jnp.where(reached, a, b), new, before)

    return lax.fori_loop(0, size, prefix_lap, start)


def dot_plain(left, right):
    return jnp.dot(left, right, preferred_element_type=jnp.float32)


def dot_rows(left, right):
    return lax.dot_general(
        left, right, (((1,), (1,)), ((), ())), preferred_element_type=jnp.float32
    )


def dot_cols(left, right):
    return lax.dot_general(
        left, right, (((0,), (0,)), ((), ())), preferred_element_type=jnp.float32
    )


def matmul_high(left, right):
    return jnp.matmul(left, right, precision=HIGH_ACCURACY)


def round_low(values):
    return lax.optimization_barrier(values.astype(jnp.bfloat16)).astype(jnp.float32)


def rms_norm(values, gain):
    return values * lax.rsqrt(jnp.mean(values * values, axis=-1, keepdims=True) + EPSILON) * gain


def unit_rows(values):
    return values * lax.rsqrt(jnp.sum(values * values, axis=-1, keepdims=True) + EPSILON)


def doc_index(positions, seq_start):
    return jnp.sum((seq_start[None, :] <= positions[:, None]).astype(jnp.int32), axis=1) - 1


def link(earlier, later):
    return (matmul_high(later[0], earlier[0]), matmul_high(later[0], earlier[1]) + later[1])


def group_parts(keys, values, betas, logdec, resets):
    size = keys.shape[0]
    rows = jnp.arange(size)
    lower = rows[:, None] >= rows[None, :]
    strict = rows[:, None] > rows[None, :]
    lower_ones = lower.astype(jnp.float32)
    cumul = matmul_high(lower_ones, logdec)
    segment = matmul_high(lower_ones, resets)
    same = (segment[:, None] == segment[None, :]) & lower
    decay = jnp.where(same, jnp.exp(jnp.where(same, cumul[:, None] - cumul[None, :], 0.0)), 0.0)
    start = jnp.where(segment == 0.0, jnp.exp(cumul), 0.0)
    gram = matmul_high(keys, keys.T)
    system = jnp.eye(size, dtype=jnp.float32) + jnp.where(
        strict, betas[:, None] * gram * decay, 0.0
    )
    right_side = jnp.concatenate(
        [betas[:, None] * start[:, None] * keys, betas[:, None] * values], axis=1
    )
    solved = lax.linalg.triangular_solve(
        system, right_side, left_side=True, lower=True, unit_diagonal=True
    )
    key_width = keys.shape[1]
    wy_keys = solved[:, :key_width]
    wy_values = solved[:, key_width:]
    carried = keys * decay[size - 1][:, None]
    step_map = start[size - 1] * jnp.eye(key_width, dtype=jnp.float32) - matmul_high(
        carried.T, wy_keys
    )
    step_add = matmul_high(carried.T, wy_values)
    return (decay, start, wy_keys, wy_values, step_map, step_add)


def group_out(recurrent_state, queries, keys, decay, start, wy_keys, wy_values, step_map, step_add):
    picked = decay[NH - 1 :: NH]
    fresh = wy_values - matmul_high(wy_keys, recurrent_state)
    scores = matmul_high(queries, keys.T) * picked
    mixed = matmul_high(queries * start[NH - 1 :: NH][:, None], recurrent_state) + matmul_high(
        scores, fresh
    )
    return (matmul_high(step_map, recurrent_state) + step_add, mixed)


def prep_all(keys, values, betas, logdec, resets):
    span = GROUP * NH
    blocks = keys.shape[1] // span

    def split(array):
        return array.reshape((array.shape[0], blocks, span) + array.shape[2:])

    per_block = jax.vmap(group_parts)
    per_head = jax.vmap(per_block, in_axes=(0, 0, 0, 0, None))
    return per_head(
        split(keys), split(values), split(betas), split(logdec), resets.reshape(blocks, span)
    )


def recur_parts(parts, queries, keys, recurrent_state):
    decay, start, wy_keys, wy_values, step_map, step_add = parts
    blocks = decay.shape[1]

    def one_head(
        query_rows, key_rows, decay, start, wy_keys, wy_values, step_map, step_add, head_state
    ):
        items = (
            query_rows.reshape((blocks, -1) + query_rows.shape[1:]),
            key_rows.reshape((blocks, -1) + key_rows.shape[1:]),
            decay,
            start,
            wy_keys,
            wy_values,
            step_map,
            step_add,
        )

        def advance(carry, item):
            return group_out(carry, *item)

        final, outputs = lax.scan(advance, head_state, items)
        return (outputs.reshape((-1, outputs.shape[-1])), final)

    return jax.vmap(one_head)(
        queries, keys, decay, start, wy_keys, wy_values, step_map, step_add, recurrent_state
    )


def device_maps(parts, initial):
    step_map, step_add = (parts[4], parts[5])

    def compose(carry, piece):
        return (link(carry, piece), None)

    result, _ = lax.scan(
        compose, initial, (jnp.swapaxes(step_map, 0, 1), jnp.swapaxes(step_add, 0, 1))
    )
    return result


def head_layout(queries, keys, values, betas, logdec):
    tok_count = queries.shape[0]
    heads = queries.shape[1]
    q_heads = jnp.transpose(queries, (1, 0, 2))
    key_heads_split = jnp.transpose(keys, (1, 0, 2, 3)).reshape(heads, tok_count * NH, -1)
    v_heads = jnp.transpose(values, (1, 0, 2, 3)).reshape(heads, tok_count * NH, -1)
    b_heads = jnp.transpose(betas, (1, 0, 2)).reshape(heads, -1)
    padded = jnp.concatenate(
        [logdec[:, :, None], jnp.zeros((tok_count, heads, NH - 1), jnp.float32)], axis=2
    )
    g_heads = jnp.transpose(padded, (1, 0, 2)).reshape(heads, -1)
    return (q_heads, key_heads_split, v_heads, b_heads, g_heads)


def local(
    block_in,
    seq_start,
    attn_gain,
    q_weight,
    k_weight,
    v_weight,
    conv_q,
    conv_k,
    conv_v,
    beta_weight,
    decay_weight,
    a_log,
    dt_bias,
    outgate_weight,
    o_gain,
    out_weight,
    mlp_gain,
    gate_weight,
    up_weight,
    down_weight,
    out_grad,
):
    tok_count = block_in.shape[0]
    heads = a_log.shape[0]
    query_cols = q_weight.shape[1]
    key_cols = k_weight.shape[1]
    beta_cols = beta_weight.shape[1]
    head_dim = query_cols // heads
    kernel_len = conv_q.shape[0]
    rim = kernel_len - 1
    positions = lax.axis_index("seq") * tok_count + jnp.arange(tok_count, dtype=jnp.int32)
    documents = doc_index(positions, seq_start)
    resets = jnp.any(seq_start[None, :] == positions[:, None], axis=1).astype(jnp.float32)
    sub_resets = jnp.concatenate(
        [resets[:, None], jnp.zeros((tok_count, NH - 1), jnp.float32)], axis=1
    ).reshape(-1)
    masks = jnp.stack(
        [
            (doc_index(positions - (rim - j), seq_start) == documents).astype(jnp.float32)[:, None]
            for j in range(kernel_len)
        ]
    )
    eye_stack = jnp.broadcast_to(jnp.eye(head_dim, dtype=jnp.float32), (heads, head_dim, head_dim))
    zero_stack = jnp.zeros((heads, head_dim, head_dim), jnp.float32)
    x_float = block_in.astype(jnp.float32)
    normed_float, attn_norm_back = jax.vjp(rms_norm, x_float, attn_gain)
    normed = normed_float.astype(jnp.bfloat16)
    mix_weight = jnp.concatenate([q_weight, k_weight, v_weight], axis=1)
    side_weight = jnp.concatenate([outgate_weight, beta_weight, decay_weight], axis=1)
    kernel = jnp.concatenate([conv_q, conv_k, conv_v], axis=1)
    projected = dot_plain(normed, mix_weight).astype(jnp.bfloat16)
    side = dot_plain(normed, side_weight)
    halo_in = from_behind(projected[tok_count - rim :], "seq", 1)
    extended = jnp.concatenate([halo_in, projected], axis=0).astype(jnp.float32)

    def conv_piece(extended, kernel):
        total = jnp.zeros((tok_count, kernel.shape[1]), jnp.float32)
        for j in range(kernel_len):
            total = total + kernel[j] * extended[j : j + tok_count] * masks[j]
        activated = jax.nn.silu(total)
        queries = unit_rows(
            activated[:, :query_cols].reshape(tok_count, heads, head_dim)
        ) * head_dim ** (-0.5)
        keys = unit_rows(
            activated[:, query_cols : query_cols + key_cols].reshape(tok_count, heads, NH, head_dim)
        )
        values = activated[:, query_cols + key_cols :].reshape(tok_count, heads, NH, head_dim)
        return (queries, keys, values)

    def side_piece(side, a_log, dt_bias):
        outgate = side[:, :query_cols]
        betas = jax.nn.sigmoid(side[:, query_cols : query_cols + beta_cols]).reshape(
            tok_count, heads, NH
        )
        logdec = -jnp.exp(a_log) * jax.nn.softplus(side[:, query_cols + beta_cols :] + dt_bias)
        return (outgate, betas, logdec)

    (queries, keys, values), convolution_backward = jax.vjp(conv_piece, extended, kernel)
    queries = round_low(queries)
    keys = round_low(keys)
    values = round_low(values)
    (outgate, betas, logdec), side_back = jax.vjp(side_piece, side, a_log, dt_bias)
    laid = head_layout(queries, keys, values, betas, logdec)
    parts = prep_all(laid[1], laid[2], laid[3], laid[4], sub_resets)
    matrices, offsets = device_maps(parts, (eye_stack, zero_stack))
    prefix = carried_in((matrices, offsets), "seq", link, (eye_stack, zero_stack))
    state_in = prefix[1]
    mixed_heads, _ = recur_parts(parts, laid[0], laid[1], state_in)
    mixed = jnp.transpose(mixed_heads, (1, 0, 2))

    def norm_piece(mixed, outgate, o_gain):
        gated = rms_norm(mixed, o_gain) * jax.nn.silu(outgate.reshape(mixed.shape))
        return gated.reshape(tok_count, -1)

    gated, norm_back = jax.vjp(norm_piece, mixed, outgate, o_gain)
    branch = gated.astype(jnp.bfloat16)
    attention_out = lax.psum(dot_plain(branch, out_weight), "head")
    hidden = x_float + attention_out
    normed_mlp_float, mlp_norm_back = jax.vjp(rms_norm, hidden, mlp_gain)
    normed_mlp = normed_mlp_float.astype(jnp.bfloat16)
    gate = dot_plain(normed_mlp, gate_weight)
    up = dot_plain(normed_mlp, up_weight)

    def swiglu(gate, up):
        return jax.nn.silu(gate) * up

    inner_float, swiglu_back = jax.vjp(swiglu, gate, up)
    inner = inner_float.astype(jnp.bfloat16)
    feed_out = lax.psum(dot_plain(inner, down_weight).astype(jnp.bfloat16), "head").astype(
        jnp.float32
    )
    output = (hidden + feed_out).astype(jnp.bfloat16)
    grad_inner = dot_rows(out_grad, down_weight)
    grad_down = dot_cols(inner, out_grad)
    grad_gate, grad_up = swiglu_back(grad_inner)
    grad_gate = grad_gate.astype(jnp.bfloat16)
    grad_up = grad_up.astype(jnp.bfloat16)
    part_mlp = dot_rows(grad_gate, gate_weight) + dot_rows(grad_up, up_weight)
    grad_gate_w = dot_cols(normed_mlp, grad_gate)
    grad_up_w = dot_cols(normed_mlp, grad_up)
    grad_normed_mlp = lax.psum(part_mlp, "head")
    grad_hidden_norm, grad_mlp_gain = mlp_norm_back(grad_normed_mlp)
    grad_hidden = out_grad.astype(jnp.float32) + grad_hidden_norm
    attention_gradient = grad_hidden.astype(jnp.bfloat16)
    grad_gated = dot_rows(attention_gradient, out_weight)
    grad_out_w = dot_cols(branch, attention_gradient)
    grad_mixed, grad_outgate, grad_o_part = norm_back(grad_gated)
    grad_mixed_heads = jnp.transpose(grad_mixed, (1, 0, 2))

    def outputs_of_state(recurrent_state):
        return recur_parts(parts, laid[0], laid[1], recurrent_state)[0]

    _, state_back = jax.vjp(outputs_of_state, state_in)
    (carry_term,) = state_back(grad_mixed_heads)
    adjoint = prefix_2(
        (jnp.swapaxes(matrices, 1, 2), carry_term), "seq", link, (eye_stack, zero_stack)
    )

    def mixer_piece(queries, keys, values, betas, logdec, recurrent_state):
        inputs = head_layout(queries, keys, values, betas, logdec)
        fresh_parts = prep_all(inputs[1], inputs[2], inputs[3], inputs[4], sub_resets)
        return recur_parts(fresh_parts, inputs[0], inputs[1], recurrent_state)

    _, mixer_back = jax.vjp(mixer_piece, queries, keys, values, betas, logdec, state_in)
    grad_q, grad_k, grad_v, grad_betas, grad_logdec, _ = mixer_back((grad_mixed_heads, adjoint[1]))
    grad_side, grad_a_log, grad_dt_bias = side_back((grad_outgate, grad_betas, grad_logdec))
    grad_extended, grad_kernel = convolution_backward((grad_q, grad_k, grad_v))
    halo_back = from_behind(grad_extended[:rim], "seq", -1)
    grad_proj = grad_extended[rim:] + jnp.concatenate(
        [jnp.zeros((tok_count - rim, halo_back.shape[1]), jnp.float32), halo_back], axis=0
    )
    grad_proj = grad_proj.astype(jnp.bfloat16)
    grad_side = grad_side.astype(jnp.bfloat16)
    part_attn = dot_rows(grad_proj, mix_weight) + dot_rows(grad_side, side_weight)
    grad_mix_w = dot_cols(normed, grad_proj)
    grad_side_w = dot_cols(normed, grad_side)
    grad_normed, grad_o_gain = (
        lax.psum(part_attn.astype(jnp.bfloat16), "head").astype(jnp.float32),
        lax.psum(grad_o_part.astype(jnp.bfloat16), "head").astype(jnp.float32),
    )
    grad_x_norm, grad_attn_gain = attn_norm_back(grad_normed)
    grad_input = (grad_hidden + grad_x_norm).astype(jnp.bfloat16)
    grad_q_w = grad_mix_w[:, :query_cols]
    grad_k_w = grad_mix_w[:, query_cols : query_cols + key_cols]
    grad_v_w = grad_mix_w[:, query_cols + key_cols :]
    grad_conv_q = grad_kernel[:, :query_cols]
    grad_conv_k = grad_kernel[:, query_cols : query_cols + key_cols]
    grad_conv_v = grad_kernel[:, query_cols + key_cols :]
    grad_outgate_w = grad_side_w[:, :query_cols]
    grad_beta_w = grad_side_w[:, query_cols : query_cols + beta_cols]
    grad_decay_w = grad_side_w[:, query_cols + beta_cols :]
    results = tuple(
        lax.psum(
            (
                grad_attn_gain,
                grad_q_w,
                grad_k_w,
                grad_v_w,
                grad_conv_q,
                grad_conv_k,
                grad_conv_v,
                grad_beta_w,
                grad_decay_w,
                grad_a_log,
                grad_dt_bias,
                grad_outgate_w,
                grad_o_gain,
                grad_out_w,
                grad_mlp_gain,
                grad_gate_w,
                grad_up_w,
                grad_down,
            ),
            "seq",
        )
    )
    return (output, grad_input) + results


def solution(mesh):
    placed = (
        P("seq", None),
        P(),
        P(),
        P(None, "head"),
        P(None, "head"),
        P(None, "head"),
        P(None, "head"),
        P(None, "head"),
        P(None, "head"),
        P(None, "head"),
        P(None, "head"),
        P("head"),
        P("head"),
        P(None, "head"),
        P(),
        P("head", None),
        P(),
        P(None, "head"),
        P(None, "head"),
        P("head", None),
        P("seq", None),
    )
    return jax.shard_map(
        local,
        mesh=mesh,
        in_specs=placed,
        out_specs=(
            P("seq", None),
            P("seq", None),
            P(),
            P(None, "head"),
            P(None, "head"),
            P(None, "head"),
            P(None, "head"),
            P(None, "head"),
            P(None, "head"),
            P(None, "head"),
            P(None, "head"),
            P("head"),
            P("head"),
            P(None, "head"),
            P(),
            P("head", None),
            P(),
            P(None, "head"),
            P(None, "head"),
            P("head", None),
        ),
        check_vma=False,
    )
```

profile of v0, /device:TPU:0, one launch (start us, length us, event | category | flops | bytes accessed | tf_op | source)
XLA Modules:
  0.0 1476.8 jit_solution(445648456445057938)
XLA Ops:
  14.6 4.8 collective-permute-start
  29.8 3.3 fusion.147
  51.6 158.8 %custom-call.13 = f32[2,8,1,128,128]{3,4,2,1,0:T(8,128)} custom-call(f32[2,8,1,128,128]{4,3,2,1,0:T(8,128)} %get-tuple-element.2197), custom_call_target="InvertDiagBlocksLowerTriangular" | custom-call | tf_op jit(solution)/shard_map/vmap(vmap())/triangular_solve/custom-call.1 | solution.py:116
  211.7 3.2 fusion.157
  222.5 19.9 %while.142 = (s32[]{:T(128)}, f32[2,128,128]{2,1,0:T(8,128)S(1)}, f32[2,128,128]{2,1,0:T(8,128)S(1)}, f32[8,2,128,128]{3,2,1,0:T(8,128)}, f32[8,2,128,128]{3,2,1,0:T(8,128)}, /*index=5*/s32[]{:T(128)}, s32[]{:T(128)}) while((s32[]{:T(128)}, f32[2,128,128]{2,1,0:T(8,128)S(1)}, f32[2,128,128]{2,1,0:T(8,128)S(1)}, ...), condition=%wide.region_8.0_spmd.clone, body=%wide.region_7.0_spmd.clone.sunk | while | flops 100728832 | bytes 1443415 | solution.py:189
  263.2 42.0 %while.139 = (s32[]{:T(128)}, f32[8,2,64,128]{3,2,1,0:T(8,128)}, f32[8,2,64,128]{3,2,1,0:T(8,128)}, f32[8,2,64,128]{3,2,1,0:T(8,128)}, f32[8,2,128]{2,1,0:T(2,12...) while((s32[]{:T(128)}, f32[8,2,64,128]{3,2,1,0:T(8,128)}, ...), condition=%wide.region_22.24_spmd, body=%wide.region_21.23_spmd.sunk | while | flops 25198592 | bytes 857693 | solution.py:175
  305.3 2.7 slice_bitcast_fusion.1
  317.5 33.6 %all-gather.2 = bf16[16,128,128]{2,1,0:T(8,128)(2,1)} all-gather(bf16[2,128,128]{2,1,0:T(8,128)(2,1)S(1)} %bitcast.678), channel_id=4, replica_groups=mesh['seq'=8,'head'=4] {'seq'}, dimensions={0}, use_global_device_ids=true | all-gather | bytes 589824 | tf_op jit(solution)/shard_map/all_gather | solution.py:37
  351.1 9.2 while.143
  361.9 61.0 %while.138 = (s32[]{:T(128)}, f32[2,128,128]{2,1,0:T(8,128)S(1)}, f32[8,2,64,128]{3,2,0,1:T(8,128)}, f32[8,2,128,128]{3,2,1,0:T(8,128)}, f32[8,2,128,128]{3,2,1,...) while((s32[]{:T(128)}, f32[2,128,128]{2,1,0:T(8,128)S(1)}, ...), condition=%wide.region_13.15_spmd, body=%wide.region_12.14_spmd.sunk | while | flops 176275456 | bytes 2629245 | solution.py:175
  427.3 2.9 fusion.286
  437.2 90.3 %while.140 = (s32[]{:T(128)}, f32[2,128,128]{2,1,0:T(8,128)S(1)}, f32[8,2,128,128]{3,2,1,0:T(8,128)}, f32[8,2,128,128]{2,3,1,0:T(8,128)}, f32[8,2,64,128]{3,2,1,...) while((s32[]{:T(128)}, f32[2,128,128]{2,1,0:T(8,128)S(1)}, ...), condition=%wide.region_28.30_spmd, body=%wide.region_27.29_spmd.sunk | while | flops 125927424 | bytes 2828981 | solution.py:175
  541.1 3.2 convolution_convert_fusion.1
  551.8 39.3 %all-reduce.33.cloned.1.call-done = f32[512,1024]{1,0:T(8,128)} async-done(((f32[512,1024]{1,0:T(8,128)}), f32[512,1024]{1,0:T(8,128)}) %all-reduce.33.cloned.1.call-update) | async-done | bytes 2097168 | tf_op jit(solution)/shard_map/psum | solution.py:330
  591.1 2.9 multiply_reduce_fusion.4
  604.2 38.9 %while.144 = (s32[]{:T(128)}, f32[2,128,128]{2,1,0:T(8,128)S(1)}, f32[8,2,128,128]{2,3,1,0:T(8,128)}, f32[8,2,64,128]{3,2,1,0:T(8,128)}, f32[8,2,64,128]{3,2,1,0...) while((s32[]{:T(128)}, f32[2,128,128]{2,1,0:T(8,128)S(1)}, ...), condition=%wide.region_24.26_spmd.clone, body=%wide.region_23.25_spmd.clone.sunk | while | flops 151126016 | bytes 1575043 | solution.py:175
  643.1 31.4 %all-gather.3 = bf16[16,128,128]{2,1,0:T(8,128)(2,1)S(1)} all-gather(bf16[2,128,128]{2,1,0:T(8,128)(2,1)S(1)} %convert_element_type.200), channel_id=5, replica_groups=mesh['seq'=8,'head'=4] {'seq'}, dimensions={0}, use_global_device_ids=true | all-gather | bytes 589824 | tf_op jit(solution)/shard_map/all_gather | solution.py:37
  674.5 8.9 while.145
  689.8 139.8 %while.141 = (s32[]{:T(128)}, f32[2,128,128]{2,1,0:T(8,128)S(1)}, f32[8,2,64,128]{3,2,0,1:T(8,128)}, f32[8,2,128,128]{3,2,0,1:T(8,128)}, f32[8,2,128,128]{3,2,0,...) while((s32[]{:T(128)}, f32[2,128,128]{2,1,0:T(8,128)S(1)}, ...), condition=%wide.region_31.33_spmd, body=%wide.region_29.32_spmd.sunk | while | flops 352567168 | bytes 4669713 | solution.py:175
  829.7 4.2 fusion.193
  845.2 4.1 fusion.184
  857.7 5.5 add_add_fusion.2
  863.2 3.2 reshape.374
  868.0 3.2 reshape.373
  872.8 4.3 multiply_reduce_fusion.3
  892.0 3.3 add_convert_fusion
  902.6 2.7 fusion.283
  906.3 6.6 psum.177
  913.0 35.0 %all-reduce.37.cloned.1.call-done = (bf16[512,1024]{1,0:T(8,128)(2,1)}, bf16[512,1024]{1,0:T(8,128)(2,1)}) async-done(((bf16[512,1024]{1,0:T(8,128)(2,1)}, bf16[512,1024]{1,0:T(8,128)(2,1)}), (bf16[512,1024]{1,0:T(8,128)(2,1)}, bf16[512,1024]{1,0:T(8,128)(2,1)})) %all-reduce.37.cloned.1.call-update) | async-done | bytes 2097168 | tf_op jit(solution)/shard_map/psum | solution.py:318
  950.1 40.0 %all-reduce.23 = (f32[1024]{0:T(1024)}, f32[4,256]{1,0:T(4,128)}, f32[4,512]{1,0:T(4,128)}, f32[4,512]{1,0:T(4,128)}, f32[1024,4]{0,1:T(4,128)}, /*index=5*/f32[...) all-reduce(f32[1024]{0:T(1024)S(1)} %get-tuple-element.1961, ...), channel_id=1, replica_groups=mesh['seq'=8,'head'=4] {'seq'}, use_global_device_ids=true, to_apply=%region_44.46 | all-reduce | flops 13444 | bytes 107296 | tf_op jit(solution)/shard_map/psum | solution.py:382
  990.1 2.7 add_convert_fusion.1
  994.4 457.9 %all-reduce.35.cloned.1.call-done = (f32[1024,256]{1,0:T(8,128)}, f32[1024,512]{1,0:T(8,128)}, f32[1024,512]{1,0:T(8,128)}, f32[1024,256]{0,1:T(8,128)}, f32[256...) async-done(((f32[1024,256]{1,0:T(8,128)}, f32[1024,512]{1,0:T(8,128)}, f32[1024,512]{1,0:T(8,128)}, f32[1024,256]{0,1:T(8,128)}, ...) | async-done | bytes 15990800 | tf_op jit(solution)/shard_map/psum | solution.py:382
  (937 shorter events, 598.3 us)
Async XLA Ops:
  7.2 527.3 %copy-start = (bf16[704,1024]{1,0:T(8,128)(2,1)S(1)}, bf16[704,1024]{1,0:T(8,128)(2,1)}, u32[]{:S(2)}) copy-start(bf16[704,1024]{1,0:T(8,128)(2,1)} %param.58) | copy-start | bytes 4325380
  7.2 343.9 %all-gather.7.cloned.1.call-start = ((), (), s32[]{:S(2)}) async-start(), calls=%async_computation.2 | async-start | bytes 1179648 | tf_op jit(solution)/shard_map/all_gather | solution.py:22
  9.5 11.7 copy-start.113
  11.8 8.8 copy-start.130
  11.8 8.8 copy-start.126
  11.8 8.8 copy-start.127
  11.9 8.9 copy-start.122
  11.9 9.2 copy-start.129
  14.6 13.6 collective-permute-start
  20.6 201.8 %copy-start.66 = (f32[128,128]{1,0:T(8,128)}, f32[128,128]{1,0:T(8,128)S(1)}, u32[]{:S(2)}) copy-start(f32[128,128]{1,0:T(8,128)S(1)} %get-tuple-element.2217) | copy-start | bytes 196612
  20.8 9.0 copy-start.86
  20.8 9.0 copy-start.88
  20.8 9.0 copy-start.90
  20.8 9.0 copy-start.92
  27.3 22.1 %copy-start.100 = (pred[128,128]{1,0:T(8,128)(4,1)}, pred[128,128]{1,0:T(8,128)(4,1)S(1)}, u32[]{:S(2)}) copy-start(pred[128,128]{1,0:T(8,128)(4,1)S(1)} %get-tuple-element.2215) | copy-start | bytes 49156
  27.3 22.1 %copy-start.102 = (pred[128,128]{1,0:T(8,128)(4,1)}, pred[128,128]{1,0:T(8,128)(4,1)S(1)}, u32[]{:S(2)}) copy-start(pred[128,128]{1,0:T(8,128)(4,1)S(1)} %get-tuple-element.2216) | copy-start | bytes 49156
  27.5 21.9 %copy-start.47 = (pred[8,128,128]{2,1,0:T(8,128)(4,1)}, pred[8,128,128]{2,1,0:T(8,128)(4,1)S(1)}, u32[]{:S(2)}) copy-start(pred[8,128,128]{2,1,0:T(8,128)(4,1)S(1)} %compare_and_fusion) | copy-start | bytes 393220
  27.9 183.4 %copy-start.94 = (f32[2,8,128]{2,1,0:T(8,128)}, f32[2,8,128]{2,1,0:T(8,128)S(1)}, u32[]{:S(2)}) copy-start(f32[2,8,128]{2,1,0:T(8,128)S(1)} %get-tuple-element.2163) | copy-start | bytes 24580
  211.3 6.9 copy-start.82
  242.4 10.2 copy-start.33
  243.0 108.1 %all-gather.9.cloned.1.call-start = ((), (), s32[]{:S(2)}) async-start(), calls=%async_computation.3 | async-start | bytes 1179648 | tf_op jit(solution)/shard_map/all_gather | solution.py:22
  261.5 266.0 %all-reduce.31.cloned.1.call-start = ((), (), s32[]{:S(2)}) async-start(), calls=%async_computation | async-start | bytes 4194304 | tf_op jit(solution)/shard_map/psum | solution.py:306
  430.3 160.8 %all-reduce.33.cloned.1.call-start = ((), (), s32[]{:S(2)}) async-start(), calls=%async_computation.1 | async-start | bytes 4194304 | tf_op jit(solution)/shard_map/psum | solution.py:330
  540.7 407.3 %all-reduce.37.cloned.1.call-start = ((), (), s32[]{:S(2)}) async-start(), calls=%async_computation.5 | async-start | bytes 4194304 | tf_op jit(solution)/shard_map/psum | solution.py:318
  643.1 31.4 %copy-start.16 = (f32[8,2,64,128]{3,2,1,0:T(8,128)}, f32[8,2,64,128]{3,2,1,0:T(8,128)S(1)}, u32[]{:S(2)}) copy-start(f32[8,2,64,128]{3,2,1,0:T(8,128)S(1)} %get-tuple-element.3074) | copy-start | bytes 1572868
  829.7 12.3 copy-start.14
  881.9 10.1 collective-permute-start.1
  895.4 557.0 %all-reduce.35.cloned.1.call-start = ((), (), s32[]{:S(2)}) async-start(), calls=%async_computation.4 | async-start | bytes 31981568 | tf_op jit(solution)/shard_map/psum | solution.py:382
  905.3 7.7 copy-start.140
  905.3 44.8 %slice-start = ((f32[1024,262]{0,1:T(8,128)}), f32[1024,4]{0,1:T(4,128)S(1)}, s32[]{:S(2)}) async-start(f32[1024,262]{0,1:T(8,128)} %copy-done.69), calls=%async_computation.6 | async-start | bytes 32768 | tf_op jit(solution)/shard_map/slice | solution.py:379
  905.3 84.8 %copy-start.116 = (f32[512]{0:T(512)S(1)}, f32[512]{0:T(512)}, u32[]{:S(2)}) copy-start(f32[512]{0:T(512)} %copy-done.115) | copy-start | bytes 6148
  905.3 84.8 %copy-start.8 = (f32[512,1024]{1,0:T(8,128)S(1)}, f32[512,1024]{1,0:T(8,128)}, u32[]{:S(2)}) copy-start(f32[512,1024]{1,0:T(8,128)} %copy-done.6) | copy-start | bytes 6291460
  (118 other events, 333.6 us)
Sparse Core Ops, SparseCore 0:
  243.2 40.4 all-gather.6
  285.8 39.2 all-gather.8
  430.4 50.2 all-reduce.30
  540.8 50.2 all-reduce.32
  895.5 52.3 all-reduce.36
  955.6 496.7 all-reduce.34
where the time goes:
time: 1500 us; the launch traced here: 1480 us
  waiting for transfers between devices  532 us (35%)
  matrix products  366 us (24%)
  other arithmetic  248 us (17%)
  local copies, waits for them, and re-layouts  192 us (13%)
  blocking collectives  112 us (7%)
  between operations  16.6 us (1%)
    psum x1, waiting for transfers between devices, local(): lax.psum((grad_attn_gain, grad_q_w, grad_k_w, grad_v_w, grad_conv_q, grad...  458 us
    dot_general x227, matrix products, matmul_high(): return jnp.matmul(left, right, precision=HIGH_ACCURACY)  318 us
    another operation x3, other arithmetic, group_parts(): lax.linalg.triangular_solve(system, right_side, left_side=True, lower=Tru...  159 us
    all_gather x2, blocking collectives, prefix_2(): lax.all_gather(part.astype(kind), axis)  65 us
    unnamed x302, local copies, waits for them, and re-layouts  41.4 us
    psum x1, blocking collectives, local(): lax.psum((grad_attn_gain, grad_q_w, grad_k_w, grad_v_w, grad_conv_q, grad...  40 us
    psum x1, waiting for transfers between devices, local(): grad_normed_mlp = lax.psum(part_mlp, 'head')  39.3 us
    psum x1, waiting for transfers between devices, local(): lax.psum(dot_plain(inner, down_weight).astype(jnp.bfloat16), 'head')  35 us
  transfers between devices with their start and end apart: 8, of which 3 were waited for; matrix products, arithmetic and copies ran while one was open for 14% of the time, Pallas kernels for 0%

commit v1 on v0

v1 whole, which is shorter than its diff:
```python
import functools
import jax
import jax.numpy as jnp
from jax import lax
from jax.experimental import pallas as pl
from jax.experimental.pallas import tpu as pltpu
from jax.sharding import PartitionSpec as P

NH = 2
GROUP = 64
LANES = 128
EPSILON = 1e-06
BF = jnp.bfloat16
F32 = jnp.float32
VMEM = pltpu.VMEM
VMEM_LIMIT = 60 * 1024 * 1024


def mm(left, right):
    return jnp.dot(left.astype(BF), right.astype(BF), preferred_element_type=F32)


def mm_nt(left, right):
    return lax.dot_general(
        left.astype(BF), right.astype(BF), (((1,), (1,)), ((), ())), preferred_element_type=F32
    )


def mm_tn(left, right):
    return lax.dot_general(
        left.astype(BF), right.astype(BF), (((0,), (0,)), ((), ())), preferred_element_type=F32
    )


def mm_exact(left, right):
    return jnp.dot(left, right, preferred_element_type=F32, precision=lax.Precision.HIGHEST)


def sigmoid(values):
    return 1.0 / (1.0 + jnp.exp(-values))


def softplus(values):
    return jnp.maximum(values, 0.0) + jnp.log1p(jnp.exp(-jnp.abs(values)))


def documents_at(starts, positions):
    total = jnp.zeros(positions.shape, jnp.int32)
    for k in range(starts.shape[0]):
        total = total + (starts[k] <= positions).astype(jnp.int32)
    return total


def sub_order(index):
    return NH * (index % GROUP) + index // GROUP


def order_pair():
    rows = sub_order(lax.broadcasted_iota(jnp.int32, (LANES, LANES), 0))
    cols = sub_order(lax.broadcasted_iota(jnp.int32, (LANES, LANES), 1))
    return rows, cols


def gate_columns(small, log_rate, bias, heads):
    lane = lax.broadcasted_iota(jnp.int32, (1, LANES), 1)
    rate = jnp.zeros((1, LANES), F32)
    shift = jnp.zeros((1, LANES), F32)
    for h in range(heads):
        at = lane == NH * heads + h
        rate = jnp.where(at, -jnp.exp(jnp.full((1, LANES), log_rate[h], F32)), rate)
        shift = jnp.where(at, bias[h], shift)
    return sigmoid(small), rate * softplus(small + shift), small + shift, rate


def chunk_decays(rows, cols_ref, row_ref, doc_ref, c, h, heads, doc_before):
    cum_col = cols_ref[rows, NH * heads + h : NH * heads + h + 1]
    doc_col = doc_ref[rows, 0:1]
    packed = row_ref[c]
    cum_row = packed[NH * heads + h : NH * heads + h + 1, :]
    doc_row = packed[NH * heads + heads : NH * heads + heads + 1, :]
    token_row = lax.broadcasted_iota(jnp.int32, (GROUP, LANES), 1) % GROUP
    token_col = lax.broadcasted_iota(jnp.int32, (GROUP, LANES), 0)
    seen = (token_col >= token_row) & (doc_col == doc_row)
    pair = jnp.where(seen, jnp.exp(jnp.where(seen, cum_col - cum_row, 0.0)), 0.0)
    start = jnp.where(doc_col == doc_before, jnp.exp(cum_col), 0.0)
    cum_last = cum_col[GROUP - 1 :, :]
    doc_last = doc_col[GROUP - 1 :, :]
    to_end = jnp.where(doc_col == doc_last, jnp.exp(cum_last - cum_col), 0.0)
    return pair, start, to_end


def two(array):
    return jnp.concatenate([array, array], axis=0)


def beta_pair(rows, cols_ref, row_ref, c, h):
    lane = lax.broadcasted_iota(jnp.int32, (1, LANES), 1)
    packed = row_ref[c]
    row = jnp.where(lane < GROUP, packed[NH * h : NH * h + 1, :], packed[NH * h + 1 : NH * h + 2, :])
    col = jnp.concatenate(
        [cols_ref[rows, NH * h : NH * h + 1], cols_ref[rows, NH * h + 1 : NH * h + 2]], axis=0
    )
    return row, col


def prep_kernel(
    heads, starts, log_rate, bias, proj, halo, conv_q, conv_k, conv_v, small,
    out_aug, state_aug, wy_k, wy_v, inverse, step_p, query_map, keys, queries, conv_total, cols, doc, row,
    final_state, final_map,
    ext, vals, score_map, step_b, masks,
):
    tokens = proj.shape[0]
    chunks = tokens // GROUP
    first = lax.axis_index("seq") * tokens
    lead = 8
    lower_r = lax.broadcasted_iota(jnp.int32, (LANES, LANES), 0)
    lower_c = lax.broadcasted_iota(jnp.int32, (LANES, LANES), 1)
    lower = ((lower_r >= lower_c) & (lower_r // GROUP == lower_c // GROUP)).astype(F32)
    lane = lax.broadcasted_iota(jnp.int32, (LANES, LANES), 1)
    per = LANES // GROUP
    for block in range(tokens // LANES):
        at = pl.ds(block * LANES, LANES)
        betas, logdec, _, _ = gate_columns(small[at, :], log_rate, bias, heads)
        cum = mm_exact(lower, logdec)
        where = lax.broadcasted_iota(jnp.int32, (LANES, LANES), 0) + (first + block * LANES)
        document = documents_at(starts, where).astype(F32)
        packed = jnp.where(lane < NH * heads, betas, jnp.where(lane < NH * heads + heads, cum, document))
        cols[at, :] = packed
        doc[at, :] = document
        turned = packed.T
        for part in range(per):
            piece = turned[0:8, part * GROUP : (part + 1) * GROUP]
            row[block * per + part] = jnp.concatenate([piece] * NH, axis=1)
    order_r, order_c = order_pair()
    level = 0
    width = 1
    while width < LANES:
        inside = (order_r // (2 * width) == order_c // (2 * width)) & (order_r // width > order_c // width)
        masks[level] = inside.astype(F32)
        level += 1
        width *= 2
    ext[0:lead, :] = halo[16 - lead : 16, :].astype(F32)
    ext[lead:, :] = proj[...].astype(F32)
    width_q = heads * LANES
    width_k = NH * heads * LANES
    taps = conv_q.shape[0]

    def conv_chunk(c, _):
        base = pl.multiple_of(c * GROUP, GROUP)
        rows = pl.ds(base, GROUP)
        position = lax.broadcasted_iota(jnp.int32, (GROUP, LANES), 0) + (first + base)
        document = doc[rows, :]
        kept = [
            (documents_at(starts, position - lag).astype(F32) == document).astype(F32) for lag in range(1, taps)
        ]
        for group in range((width_q + 2 * width_k) // LANES):
            at = slice(group * LANES, (group + 1) * LANES)
            if group * LANES < width_q:
                kernel, shift = conv_q, 0
            elif group * LANES < width_q + width_k:
                kernel, shift = conv_k, width_q
            else:
                kernel, shift = conv_v, width_q + width_k
            cut = slice(at.start - shift, at.stop - shift)
            window = ext[pl.ds(base, GROUP + lead), at]
            total = kernel[taps - 1 : taps, cut] * window[lead:, :]
            for lag in range(1, taps):
                total += kernel[taps - 1 - lag : taps - lag, cut] * window[lead - lag : lead - lag + GROUP, :] * kept[lag - 1]
            conv_total[rows, at] = total
            active = total * sigmoid(total)
            if group * LANES < width_q:
                unit = active * lax.rsqrt(jnp.sum(active * active, axis=1, keepdims=True) + EPSILON)
                queries[group, c] = (unit * LANES ** (-0.5)).astype(BF)
            elif group * LANES < width_q + width_k:
                piece = group - width_q // LANES
                unit = active * lax.rsqrt(jnp.sum(active * active, axis=1, keepdims=True) + EPSILON)
                keys[piece // NH, c, (piece % NH) * GROUP : (piece % NH + 1) * GROUP] = unit.astype(BF)
            else:
                piece = group - (width_q + width_k) // LANES
                vals[piece // NH, c, (piece % NH) * GROUP : (piece % NH + 1) * GROUP] = active.astype(BF)
        return 0

    lax.fori_loop(0, chunks, conv_chunk, 0)

    strict = order_r > order_c
    eye = (lower_r == lower_c).astype(F32)
    together = 2

    def part_chunks(step, _):
        jobs = []
        for k in range(together):
            c = step * together + k
            rows = pl.ds(pl.multiple_of(c * GROUP, GROUP), GROUP)
            before = documents_at(starts, jnp.full((1, 1), first + c * GROUP - 1, jnp.int32)).astype(F32)
            for h in range(heads):
                pair, start, to_end = chunk_decays(rows, cols, row, doc, c, h, heads, before)
                beta_row, beta_col = beta_pair(rows, cols, row, c, h)
                key = keys[h, c]
                query = queries[h, c]
                grams = mm_nt(jnp.concatenate([key, query], axis=0), key)
                system = jnp.where(strict, grams[:LANES] * two(pair), 0.0) * beta_row
                scores = grams[LANES:] * pair * beta_row
                jobs.append((c, h, start, to_end, beta_col, key, query, system, scores))
        inverses = [eye - job[7] * masks[0] for job in jobs]
        for n in range(1, level):
            halves = [mm(job[7] * masks[n], inv) for job, inv in zip(jobs, inverses)]
            inverses = [inv - mm(inv, half) for inv, half in zip(inverses, halves)]
        for job, inv in zip(jobs, inverses):
            c, h, start, to_end, beta_col, key, query, system, scores = job
            low_inv = inv.astype(BF)
            inverse[h, c] = low_inv
            key_f = key.astype(F32)
            both = mm(low_inv, jnp.concatenate([(two(start) * key_f).astype(BF), vals[h, c]], axis=1)).astype(BF)
            wy_k[h, c] = both[:, :LANES]
            wy_v[h, c] = both[:, LANES:]
            carried = (beta_col * two(to_end) * key_f).astype(BF)
            ahead = mm_tn(carried, both)
            step_p[h, c] = ahead[:, :LANES].astype(BF)
            step_b[h, c] = ahead[:, LANES:]
            scored = mm(scores, both)
            query_map[h, c] = (start * query.astype(F32) - scored[:, :LANES]).astype(BF)
            score_map[h, c] = scored[:, LANES:]
        return 0

    lax.fori_loop(0, chunks // together, part_chunks, 0)

    zero = jnp.zeros((LANES, LANES), F32)

    def advance(c, carry):
        rows = pl.ds(pl.multiple_of(c * GROUP, GROUP), GROUP)
        before = documents_at(starts, jnp.full((1, 1), first + c * GROUP - 1, jnp.int32)).astype(F32)
        new = []
        for h in range(heads):
            state = carry[h]
            low_state = state.astype(BF)
            state_aug[h, c] = low_state
            last = cols[rows, NH * heads + h : NH * heads + h + 1][GROUP - 1 :, :]
            whole = jnp.where(doc[rows, 0:1][GROUP - 1 :, :] == before, jnp.exp(last), 0.0)
            new.append(
                whole * state - mm(step_p[h, c], low_state) + jnp.concatenate([step_b[h, c], zero], axis=1)
            )
            mapped = mm(query_map[h, c], low_state)
            out_aug[h, rows, :] = jnp.concatenate([mapped[:, :LANES] + score_map[h, c], mapped[:, LANES:]], axis=1)
        return tuple(new)

    begin = jnp.concatenate([zero, eye], axis=1)
    end = lax.fori_loop(0, chunks, advance, (begin,) * heads)
    for h in range(heads):
        final_state[h] = end[h][:, :LANES].astype(final_state.dtype)
        final_map[h] = end[h][:, LANES:].astype(final_map.dtype)


def specs(count, space=None):
    return [pl.BlockSpec(memory_space=space or pltpu.VMEM)] * count


def mixer_prep(starts, log_rate, bias, proj, halo, conv_q, conv_k, conv_v, small):
    tokens, width = proj.shape
    heads = log_rate.shape[0]
    chunks = tokens // GROUP
    square = (heads, chunks, LANES, LANES)
    shape = jax.ShapeDtypeStruct
    outs = [
        shape((heads, tokens, 2 * LANES), F32),
        shape((heads, chunks, LANES, 2 * LANES), BF),
        shape(square, BF),
        shape(square, BF),
        shape(square, BF),
        shape(square, BF),
        shape((heads, chunks, GROUP, LANES), BF),
        shape(square, BF),
        shape((heads, chunks, GROUP, LANES), BF),
        shape((tokens, width), F32),
        shape((tokens, LANES), F32),
        shape((tokens, LANES), F32),
        shape((chunks, 8, LANES), F32),
        shape((heads, LANES, LANES), BF),
        shape((heads, LANES, LANES), BF),
    ]
    return pl.pallas_call(
        functools.partial(prep_kernel, heads),
        out_shape=outs,
        in_specs=specs(3, pltpu.SMEM) + specs(6),
        out_specs=specs(len(outs)),
        scratch_shapes=[
            VMEM((tokens + 8, width), F32),
            VMEM(square, BF),
            VMEM((heads, chunks, GROUP, LANES), F32),
            VMEM(square, F32),
            VMEM((8, LANES, LANES), F32),
        ],
        compiler_params=pltpu.CompilerParams(vmem_limit_bytes=VMEM_LIMIT),
        cost_estimate=pl.CostEstimate(flops=4_000_000_000, bytes_accessed=16_000_000, transcendentals=2_000_000),
        name="mixer_prep",
    )(starts, log_rate, bias, proj, halo, conv_q, conv_k, conv_v, small)


def attend_kernel(heads, reach, out_aug, outgate, o_gain, out_weight, *rest):
    before = rest[:reach]
    mixed, branch, partial, state_in = rest[reach:]
    gain = o_gain[...]
    for h in range(heads):
        at = slice(h * LANES, (h + 1) * LANES)
        state = before[reach - 1][0, h].astype(F32)
        for r in range(reach - 2, -1, -1):
            state = mm(before[r][1, h], state) + before[r][0, h].astype(F32)
        state_in[h] = state
        mix = out_aug[h, :, :LANES] + mm(out_aug[h, :, LANES:], state)
        mixed[:, at] = mix
        gate = outgate[:, at]
        normed = mix * lax.rsqrt(jnp.mean(mix * mix, axis=1, keepdims=True) + EPSILON)
        branch[:, at] = (normed * gain * (gate * sigmoid(gate))).astype(BF)
    partial[...] = mm(branch[...], out_weight[...]).astype(partial.dtype)


def attend(out_aug, outgate, o_gain, out_weight, before, dtype=F32):
    heads, tokens, _ = out_aug.shape
    shape = jax.ShapeDtypeStruct
    reach = len(before)
    outs = [
        shape((tokens, heads * LANES), F32),
        shape((tokens, heads * LANES), BF),
        shape((tokens, out_weight.shape[1]), dtype),
        shape((heads, LANES, LANES), F32),
    ]
    return pl.pallas_call(
        functools.partial(attend_kernel, heads, reach),
        out_shape=outs,
        in_specs=specs(4 + reach),
        out_specs=specs(len(outs)),
        compiler_params=pltpu.CompilerParams(vmem_limit_bytes=VMEM_LIMIT),
        name="attend",
    )(out_aug, outgate, o_gain.reshape(1, -1), out_weight, *before)


def attend_back_kernel(heads, grad, out_weight, mixed, outgate, o_gain, out_aug, d_mixed, d_outgate, d_gain, carry):
    gain = o_gain[...]
    d_branch = mm_nt(grad[...], out_weight[...])
    gain_sum = jnp.zeros((1, LANES), F32)
    for h in range(heads):
        at = slice(h * LANES, (h + 1) * LANES)
        mix = mixed[:, at]
        gate = outgate[:, at]
        grad_h = d_branch[:, at]
        scale = lax.rsqrt(jnp.mean(mix * mix, axis=1, keepdims=True) + EPSILON)
        normed = mix * scale
        sg = sigmoid(gate)
        through = grad_h * (gate * sg)
        gain_sum += jnp.sum(through * normed, axis=0, keepdims=True)
        d_normed = through * gain
        d_mix = scale * (d_normed - normed * jnp.mean(d_normed * normed, axis=1, keepdims=True))
        d_mixed[:, at] = d_mix.astype(BF)
        d_outgate[:, at] = (grad_h * normed * gain * (sg * (1.0 + gate * (1.0 - sg)))).astype(BF)
        carry[h] = mm_tn(out_aug[h, :, LANES:], d_mix).astype(carry.dtype)
    d_gain[...] = gain_sum


def attend_back(grad, out_weight, mixed, outgate, o_gain, out_aug):
    heads, tokens, _ = out_aug.shape
    shape = jax.ShapeDtypeStruct
    outs = [
        shape((tokens, heads * LANES), BF),
        shape((tokens, heads * LANES), BF),
        shape((1, LANES), F32),
        shape((heads, LANES, LANES), BF),
    ]
    return pl.pallas_call(
        functools.partial(attend_back_kernel, heads),
        out_shape=outs,
        in_specs=specs(6),
        out_specs=specs(len(outs)),
        compiler_params=pltpu.CompilerParams(vmem_limit_bytes=VMEM_LIMIT),
        name="attend_back",
    )(grad, out_weight, mixed, outgate, o_gain.reshape(1, -1), out_aug)


def back_kernel(
    heads, reach, starts, log_rate, bias, proj, halo, conv_q, conv_k, conv_v, small,
    state_aug, wy_k, wy_v, inverse, step_p, query_map, keys, queries, conv_total, cols, doc, row,
    state_in, d_mixed, *rest,
):
    after = rest[:reach]
    later = rest[reach : 2 * reach - 1]
    (
        d_proj, tail, lead_rows, d_small, d_taps, d_scalars,
        ext, state_grads, d_query, d_key, d_value, col_grads, row_grads, d_total,
    ) = rest[2 * reach - 1 :]
    tokens = proj.shape[0]
    chunks = tokens // GROUP
    first = lax.axis_index("seq") * tokens
    lead = 8
    lane = lax.broadcasted_iota(jnp.int32, (GROUP, LANES), 1)

    def document_before(c):
        return documents_at(starts, jnp.full((1, 1), first + c * GROUP - 1, jnp.int32)).astype(F32)

    def whole_decay(c, h):
        at = pl.ds(pl.multiple_of(c * GROUP, GROUP) + GROUP - 8, 8)
        last = cols[at, NH * heads + h : NH * heads + h + 1][7:8, :]
        return jnp.where(doc[at, 0:1][7:8, :] == document_before(c), jnp.exp(last), 0.0)

    begin = []
    for h in range(heads):
        state = after[reach - 1][h].astype(F32)
        for r in range(reach - 2, -1, -1):
            state = mm_tn(later[r][h], state) + after[r][h].astype(F32)
        begin.append(state)

    def retreat(step, carry):
        c = chunks - 1 - step
        rows = pl.ds(pl.multiple_of(c * GROUP, GROUP), GROUP)
        new = []
        for h in range(heads):
            low_state = carry[h].astype(BF)
            state_grads[h, c] = low_state
            new.append(
                whole_decay(c, h) * carry[h]
                - mm_tn(step_p[h, c], low_state)
                + mm_tn(query_map[h, c], d_mixed[rows, h * LANES : (h + 1) * LANES])
            )
        return tuple(new)

    lax.fori_loop(0, chunks, retreat, tuple(begin))

    order_r, order_c = order_pair()
    strict = order_r > order_c
    together = 2
    last_token = lax.broadcasted_iota(jnp.int32, (GROUP, 1), 0) == GROUP - 1

    def chunk_back(step, _):
        for k in range(together):
            c = step * together + k
            rows = pl.ds(pl.multiple_of(c * GROUP, GROUP), GROUP)
            before = document_before(c)
            col_acc = jnp.zeros((GROUP, LANES), F32)
            row_acc = []
            row_beta = []
            for h in range(heads):
                pair, start, to_end = chunk_decays(rows, cols, row, doc, c, h, heads, before)
                beta_row, beta_col = beta_pair(rows, cols, row, c, h)
                key = keys[h, c]
                query = queries[h, c]
                key_f = key.astype(F32)
                query_f = query.astype(F32)
                d_out = d_mixed[rows, h * LANES : (h + 1) * LANES]
                d_state = state_grads[h, c]
                both = state_aug[h, c]
                state = both[:, :LANES].astype(F32) + mm(both[:, LANES:], state_in[h])
                low_state = state.astype(BF)
                fresh = wy_v[h, c].astype(F32) - mm(wy_k[h, c], low_state)
                grams = mm_nt(jnp.concatenate([key, query], axis=0), key)
                pair2 = two(pair)
                system = jnp.where(strict, grams[:LANES] * pair2, 0.0)
                scores = grams[LANES:] * pair
                key_end = two(to_end) * key_f
                key_start = two(start) * key_f
                d_wide = mm_tn(scores, d_out) + mm(key_end, d_state)
                solved = mm_tn(inverse[h, c], beta_col * d_wide)
                d_value[h, c] = solved
                low_fresh = fresh.astype(BF)
                crossed = mm_nt(
                    jnp.concatenate([solved.astype(BF), d_out], axis=0),
                    jnp.concatenate([low_fresh, low_state], axis=0),
                )
                pairs = jnp.where(strict, crossed[:LANES, :LANES], 0.0)
                solved_state = crossed[:LANES, LANES:]
                out_state = crossed[LANES:, LANES:]
                fresh_grad = mm_nt(beta_col * fresh, d_state)
                system_pairs = system * pairs
                decayed = -(system_pairs * beta_row)
                gram_grad = -(pairs * pair2 * beta_row)
                score_grad = crossed[LANES:, :LANES] * beta_row
                query_key = score_grad * pair
                score_decay = score_grad * scores
                stacked = jnp.concatenate([gram_grad, query_key], axis=0).astype(BF)
                direct = mm(stacked, key)
                turned = mm_tn(stacked, jnp.concatenate([key, query], axis=0))
                d_key[h, c] = direct[:LANES] + turned - two(start) * solved_state + two(to_end) * fresh_grad
                d_query[h, c] = direct[LANES:] + start * out_state
                ending = key_end * fresh_grad
                parts = decayed - key_start * solved_state - ending
                parts = parts[:GROUP] + parts[GROUP:] + score_decay + (start * query_f) * out_state
                at_end = jnp.sum(ending, keepdims=True) + whole_decay(c, h) * jnp.sum(
                    state * d_state.astype(F32), keepdims=True
                )
                decay_col = jnp.sum(parts, axis=1, keepdims=True) + jnp.where(last_token, at_end, 0.0)
                beta_sum = jnp.sum(d_wide * fresh, axis=1, keepdims=True)
                col_acc = jnp.where(lane == NH * heads + h, decay_col, col_acc)
                for s in range(NH):
                    col_acc = jnp.where(lane == NH * h + s, beta_sum[s * GROUP : (s + 1) * GROUP], col_acc)
                beta_row_sum = jnp.sum(system_pairs, axis=0, keepdims=True)
                row_beta.append(-beta_row_sum)
                row_acc.append(beta_row * beta_row_sum - jnp.sum(score_decay, axis=0, keepdims=True))
            col_grads[rows, :] = col_acc
            row_grads[c] = jnp.concatenate(
                row_acc + row_beta + [jnp.zeros((8 - 2 * heads, LANES), F32)], axis=0
            )
        return 0

    lax.fori_loop(0, chunks // together, chunk_back, 0)

    lower_r = lax.broadcasted_iota(jnp.int32, (LANES, LANES), 0)
    lower_c = lax.broadcasted_iota(jnp.int32, (LANES, LANES), 1)
    upper = ((lower_r <= lower_c) & (lower_r // GROUP == lower_c // GROUP)).astype(F32)
    per = LANES // GROUP
    scalar_decay = jnp.zeros((1, LANES), F32)
    scalar_rate = jnp.zeros((1, LANES), F32)
    wide = lax.broadcasted_iota(jnp.int32, (LANES, LANES), 1)
    for block in range(tokens // LANES):
        at = pl.ds(block * LANES, LANES)
        pieces = []
        for part in range(per):
            c = block * per + part
            turned = jnp.concatenate([row_grads[c], jnp.zeros((LANES - 8, LANES), F32)], axis=0).T
            piece = jnp.zeros((GROUP, LANES), F32)
            for h in range(heads):
                decay_col = turned[:GROUP, h : h + 1] + turned[GROUP:, h : h + 1]
                piece = jnp.where(lane == NH * heads + h, decay_col, piece)
                for s in range(NH):
                    beta_col = turned[s * GROUP : (s + 1) * GROUP, heads + h : heads + h + 1]
                    piece = jnp.where(lane == NH * h + s, beta_col, piece)
            pieces.append(piece)
        grads = col_grads[at, :] + jnp.concatenate(pieces, axis=0)
        d_logdec = mm_exact(upper, grads)
        betas, logdec, argument, rate = gate_columns(small[at, :], log_rate, bias, heads)
        d_argument = d_logdec * rate * sigmoid(argument)
        scalar_rate += jnp.sum(d_logdec * logdec, axis=0, keepdims=True)
        scalar_decay += jnp.sum(d_argument, axis=0, keepdims=True)
        d_small[at, :] = jnp.where(
            wide < NH * heads,
            grads * betas * (1.0 - betas),
            jnp.where(wide < NH * heads + heads, d_argument, 0.0),
        ).astype(BF)
    d_scalars[...] = jnp.concatenate([scalar_rate, scalar_decay, jnp.zeros((6, LANES), F32)], axis=0)

    ext[0:lead, :] = halo[16 - lead : 16, :].astype(F32)
    ext[lead:, :] = proj[...].astype(F32)
    width_q = heads * LANES
    width_k = NH * heads * LANES
    width = width_q + 2 * width_k
    taps = conv_q.shape[0]
    d_taps[...] = jnp.zeros(d_taps.shape, F32)
    d_total[tokens:, :] = jnp.zeros((8, width), F32)

    def kernel_of(group):
        if group * LANES < width_q:
            return conv_q, slice(group * LANES, (group + 1) * LANES)
        if group * LANES < width_q + width_k:
            return conv_k, slice(group * LANES - width_q, (group + 1) * LANES - width_q)
        return conv_v, slice(group * LANES - width_q - width_k, (group + 1) * LANES - width_q - width_k)

    def active_back(c, _):
        base = pl.multiple_of(c * GROUP, GROUP)
        rows = pl.ds(base, GROUP)
        position = lax.broadcasted_iota(jnp.int32, (GROUP, LANES), 0) + (first + base)
        document = doc[rows, :]
        kept = [
            (documents_at(starts, position - lag).astype(F32) == document).astype(F32) for lag in range(1, taps)
        ]
        for group in range(width // LANES):
            at = slice(group * LANES, (group + 1) * LANES)
            total = conv_total[rows, at]
            sg = sigmoid(total)
            if group * LANES < width_q + width_k:
                active = total * sg
                scale = lax.rsqrt(jnp.sum(active * active, axis=1, keepdims=True) + EPSILON)
                unit = active * scale
                if group * LANES < width_q:
                    grad = d_query[group, c] * LANES ** (-0.5)
                else:
                    piece = group - width_q // LANES
                    grad = d_key[piece // NH, c, (piece % NH) * GROUP : (piece % NH + 1) * GROUP]
                grad = scale * (grad - unit * jnp.sum(unit * grad, axis=1, keepdims=True))
            else:
                piece = group - (width_q + width_k) // LANES
                grad = d_value[piece // NH, c, (piece % NH) * GROUP : (piece % NH + 1) * GROUP]
            grad = grad * (sg * (1.0 + total * (1.0 - sg)))
            d_total[rows, at] = grad
            window = ext[pl.ds(base, GROUP + lead), at]
            sums = []
            for j in range(taps):
                lag = taps - 1 - j
                term = grad * window[lead - lag : lead - lag + GROUP, :]
                if lag > 0:
                    term = term * kept[lag - 1]
                sums.append(jnp.sum(term, axis=0, keepdims=True))
            d_taps[0:taps, at] += jnp.concatenate(sums, axis=0)
        return 0

    lax.fori_loop(0, chunks, active_back, 0)
    lead_rows[...] = d_total[0:8, :]

    def conv_back(c, _):
        base = pl.multiple_of(c * GROUP, GROUP)
        rows = pl.ds(base, GROUP)
        position = lax.broadcasted_iota(jnp.int32, (GROUP, LANES), 0) + (first + base)
        document = doc[rows, :]
        kept = [
            (documents_at(starts, position + lag).astype(F32) == document).astype(F32) for lag in range(1, taps)
        ]
        for group in range(width // LANES):
            at = slice(group * LANES, (group + 1) * LANES)
            kernel, cut = kernel_of(group)
            window = d_total[pl.ds(base, GROUP + lead), at]
            grad = kernel[taps - 1 : taps, cut] * window[:GROUP]
            for lag in range(1, taps):
                grad += kernel[taps - 1 - lag : taps - lag, cut] * kept[lag - 1] * window[lag : lag + GROUP]
            d_proj[rows, at] = grad.astype(BF)
            tail[:, at] = grad[GROUP - 8 :]
        return 0

    lax.fori_loop(0, chunks, conv_back, 0)


def mixer_back(starts, log_rate, bias, proj, halo, conv_q, conv_k, conv_v, small, saved, state_in, d_mixed, after, later):
    tokens, width = proj.shape
    heads = log_rate.shape[0]
    chunks = tokens // GROUP
    reach = len(after)
    square = (heads, chunks, LANES, LANES)
    shape = jax.ShapeDtypeStruct
    outs = [
        shape((tokens, width), BF),
        shape((8, width), F32),
        shape((8, width), F32),
        shape((tokens, LANES), BF),
        shape((8, width), F32),
        shape((8, LANES), F32),
    ]
    operands = [starts, log_rate, bias, proj, halo, conv_q, conv_k, conv_v, small, *saved, state_in, d_mixed, *after, *later]
    return pl.pallas_call(
        functools.partial(back_kernel, heads, reach),
        out_shape=outs,
        in_specs=specs(3, pltpu.SMEM) + specs(len(operands) - 3),
        out_specs=specs(len(outs)),
        scratch_shapes=[
            VMEM((tokens + 8, width), F32),
            VMEM(square, BF),
            VMEM((heads, chunks, GROUP, LANES), F32),
            VMEM(square, F32),
            VMEM(square, F32),
            VMEM((tokens, LANES), F32),
            VMEM((chunks, 8, LANES), F32),
            VMEM((tokens + 8, width), F32),
        ],
        compiler_params=pltpu.CompilerParams(vmem_limit_bytes=VMEM_LIMIT),
        cost_estimate=pl.CostEstimate(flops=8_000_000_000, bytes_accessed=20_000_000, transcendentals=2_000_000),
        name="mixer_back",
    )(*operands)


def shifted(value, axis, steps):
    count = lax.axis_size(axis)
    leading, last = max(0, -steps), min(count, count - steps)
    return lax.ppermute(value, axis, [(source, source + steps) for source in range(leading, last)])


def swapped(value, axis, bit):
    return lax.ppermute(value, axis, [(s, s ^ bit) for s in range(lax.axis_size(axis))])


def head_sum(part):
    count = lax.axis_size("head")
    low = lax.axis_index("head") % 2
    half = part.shape[0] // 2
    keep = lax.dynamic_slice_in_dim(part, low * half, half, 0)
    give = lax.dynamic_slice_in_dim(part, (1 - low) * half, half, 0)
    total = keep.astype(F32) + swapped(give, "head", 1).astype(F32)
    bit = 2
    while bit < count:
        sent = total.astype(BF)
        total = sent.astype(F32) + swapped(sent, "head", bit).astype(F32)
        bit *= 2
    return total


def both_halves(mine):
    low = lax.axis_index("head") % 2
    other = swapped(mine, "head", 1)
    return jnp.concatenate([jnp.where(low == 0, mine, other), jnp.where(low == 0, other, mine)], axis=0)


def dot_plain(left, right):
    return jnp.dot(left, right, preferred_element_type=F32)


def dot_rows(left, right):
    return lax.dot_general(left, right, (((1,), (1,)), ((), ())), preferred_element_type=F32)


def dot_cols(left, right):
    return lax.dot_general(left, right, (((0,), (0,)), ((), ())), preferred_element_type=F32)


def rms_norm(values, gain):
    return values * lax.rsqrt(jnp.mean(values * values, axis=-1, keepdims=True) + EPSILON) * gain


def reach_of(tokens, count):
    whole = tokens * count
    longest = whole // 4 + 2 * (whole // 64 - 1)
    return max(1, min(count - 1, -(-(longest - 1) // tokens)))


def local(
    block_in, seq_start, attn_gain, q_weight, k_weight, v_weight, conv_q, conv_k, conv_v,
    beta_weight, decay_weight, a_log, dt_bias, outgate_weight, o_gain, out_weight,
    mlp_gain, gate_weight, up_weight, down_weight, out_grad,
):
    tokens = block_in.shape[0]
    heads = a_log.shape[0]
    width_q = q_weight.shape[1]
    width_k = k_weight.shape[1]
    width = width_q + 2 * width_k
    betas = beta_weight.shape[1]
    reach = reach_of(tokens, lax.axis_size("seq"))
    x_float = block_in.astype(F32)
    normed_float, attn_norm_back = jax.vjp(rms_norm, x_float, attn_gain)
    normed = normed_float.astype(BF)
    mix_weight = jnp.concatenate([q_weight, k_weight, v_weight], axis=1)
    small_weight = jnp.concatenate(
        [beta_weight, decay_weight, jnp.zeros((beta_weight.shape[0], LANES - betas - heads), BF)], axis=1
    )
    projected = dot_plain(normed, mix_weight).astype(BF)
    small = dot_plain(normed, small_weight)
    outgate = dot_plain(normed, outgate_weight)
    halo = shifted(projected[tokens - 16 :], "seq", 1)
    mixer_args = (seq_start, a_log, dt_bias, projected, halo, conv_q, conv_k, conv_v, small)
    prepared = mixer_prep(*mixer_args)
    out_aug, saved, final_state, final_map = prepared[0], prepared[1:13], prepared[13], prepared[14]
    pair = jnp.stack([final_state, final_map])
    before = [shifted(pair, "seq", r) for r in range(1, reach)] + [shifted(final_state[None], "seq", reach)]
    later = [shifted(final_map, "seq", -r) for r in range(1, reach)]
    mixed, branch, partial, state_in = attend(out_aug, outgate, o_gain, out_weight, before)
    attention_out = both_halves(head_sum(partial))
    hidden = x_float + attention_out
    normed_mlp_float, mlp_norm_back = jax.vjp(rms_norm, hidden, mlp_gain)
    normed_mlp = normed_mlp_float.astype(BF)
    gate = dot_plain(normed_mlp, gate_weight)
    up = dot_plain(normed_mlp, up_weight)

    def swiglu(gate, up):
        return jax.nn.silu(gate) * up

    inner_float, swiglu_back = jax.vjp(swiglu, gate, up)
    inner = inner_float.astype(BF)
    grad_inner = dot_rows(out_grad, down_weight)
    grad_gate, grad_up = swiglu_back(grad_inner)
    grad_gate = grad_gate.astype(BF)
    grad_up = grad_up.astype(BF)
    part_mlp = dot_rows(grad_gate, gate_weight) + dot_rows(grad_up, up_weight)
    grad_normed_mlp = both_halves(head_sum(part_mlp))
    grad_hidden_norm, grad_mlp_gain = mlp_norm_back(grad_normed_mlp)
    grad_hidden = out_grad.astype(F32) + grad_hidden_norm
    attention_gradient = grad_hidden.astype(BF)
    grad_mixed, grad_outgate, grad_o_part, carry = attend_back(
        attention_gradient, out_weight, mixed, outgate, o_gain, out_aug
    )
    after = [shifted(carry, "seq", -r) for r in range(1, reach + 1)]
    feed_out = both_halves(head_sum(dot_plain(inner, down_weight)))
    output = (hidden + feed_out).astype(BF)
    early = lax.psum(
        (
            dot_cols(branch, attention_gradient).astype(BF),
            dot_cols(normed_mlp, grad_gate).astype(BF),
            dot_cols(normed_mlp, grad_up).astype(BF),
            dot_cols(inner, out_grad).astype(BF),
        ),
        "seq",
    )
    grad_proj, tail, lead_rows, grad_small, grad_taps, grad_scalars = mixer_back(
        *mixer_args, saved, state_in, grad_mixed, after, later
    )
    following = jnp.concatenate([jnp.zeros((8, width), F32), shifted(lead_rows, "seq", -1)], axis=0)
    kernel = jnp.concatenate([conv_q, conv_k, conv_v], axis=1)
    taps = kernel.shape[0]
    position = lax.axis_index("seq") * tokens + tokens - 8 + jnp.arange(8, dtype=jnp.int32)
    for lag in range(1, taps):
        kept = documents_at(seq_start, position + lag) == documents_at(seq_start, position)
        tail = tail + kernel[taps - 1 - lag] * following[lag : lag + 8] * kept.astype(F32)[:, None]
    grad_proj = jnp.concatenate([grad_proj[: tokens - 8], tail.astype(BF)], axis=0)
    part_attn = (
        dot_rows(grad_proj, mix_weight) + dot_rows(grad_outgate, outgate_weight) + dot_rows(grad_small, small_weight)
    )
    grad_normed = both_halves(head_sum(part_attn))
    grad_x_norm, grad_attn_gain = attn_norm_back(grad_normed)
    grad_input = (grad_hidden + grad_x_norm).astype(BF)
    grad_mix_w, grad_outgate_w, grad_small_w = lax.psum(
        (
            dot_cols(normed, grad_proj).astype(BF),
            dot_cols(normed, grad_outgate).astype(BF),
            dot_cols(normed, grad_small),
        ),
        "seq",
    )
    grad_attn_gain, grad_mlp_gain, grad_taps, grad_scalars = lax.psum(
        (grad_attn_gain, grad_mlp_gain, grad_taps[:taps], grad_scalars), "seq"
    )
    grad_o_gain = lax.psum(grad_o_part, ("seq", "head"))[0]
    grad_out_w, grad_gate_w, grad_up_w, grad_down_w = (a.astype(F32) for a in early)
    grad_mix_w = grad_mix_w.astype(F32)
    q_cols, k_cols, v_cols = slice(0, width_q), slice(width_q, width_q + width_k), slice(width_q + width_k, width)
    return (
        output, grad_input, grad_attn_gain,
        grad_mix_w[:, q_cols], grad_mix_w[:, k_cols], grad_mix_w[:, v_cols],
        grad_taps[:, q_cols], grad_taps[:, k_cols], grad_taps[:, v_cols],
        grad_small_w[:, :betas], grad_small_w[:, betas : betas + heads],
        grad_scalars[0, betas : betas + heads], grad_scalars[1, betas : betas + heads],
        grad_outgate_w.astype(F32), grad_o_gain, grad_out_w, grad_mlp_gain,
        grad_gate_w, grad_up_w, grad_down_w,
    )


def solution(mesh):
    placed = (
        P("seq", None), P(), P(), P(None, "head"), P(None, "head"), P(None, "head"), P(None, "head"),
        P(None, "head"), P(None, "head"), P(None, "head"), P(None, "head"), P("head"), P("head"),
        P(None, "head"), P(), P("head", None), P(), P(None, "head"), P(None, "head"), P("head", None),
        P("seq", None),
    )
    given = (
        P("seq", None), P("seq", None), P(), P(None, "head"), P(None, "head"), P(None, "head"),
        P(None, "head"), P(None, "head"), P(None, "head"), P(None, "head"), P(None, "head"), P("head"),
        P("head"), P(None, "head"), P(), P("head", None), P(), P(None, "head"), P(None, "head"),
        P("head", None),
    )
    return jax.shard_map(local, mesh=mesh, in_specs=placed, out_specs=given, check_vma=False)
```

time: 1500 us -> 562 us (0.37); the launches traced: 1480 us -> 561 us
  matrix products: 366 us -> 30.4 us
  waiting for transfers between devices: 532 us -> 277 us
  other arithmetic: 248 us -> 39.3 us
  local copies, waits for them, and re-layouts: 192 us -> 29.2 us
  Pallas kernels: 0 us -> 59.2 us
  blocking collectives: 112 us -> 78.9 us
  starting transfers between devices: 7.04 us -> 31.8 us
    dot_general x234 -> x6, matrix products: 332 us -> 8.26 us  [dot_plain(): return jnp.dot(left, right, preferred_element_type=F32)]
    psum x4 -> x2, waiting for transfers between devices: 532 us -> 225 us  [local(): lax.psum((dot_cols(normed, grad_proj).astype(BF), dot_cols(normed, grad_o...]
    another operation x4 -> x1, other arithmetic: 160 us -> 0.89 us  [local(): pair = jnp.stack([final_state, final_map])]
    all_gather x2 -> x0, blocking collectives: 65 us -> none  [prefix_2(): lax.all_gather(part.astype(kind), axis)]
    pallas_call x0 -> x4, Pallas kernels: none -> 59.2 us  [the longest x1 28.7 us: mixer_back(): pl.pallas_call(functools.partial(back_kernel, heads, reach), out_shape=ou...]
    ppermute x2 -> x22, waiting for transfers between devices: 0.01 us -> 51.7 us  [the longest x12 43 us: swapped(): lax.ppermute(value, axis, [(s, s ^ bit) for s in range(lax.axis_size(axis...]
    squeeze x48 -> x1, local copies, waits for them, and re-layouts: 38.3 us -> 0.58 us  [local(): grad_scalars[1, betas:betas + heads]]
    dynamic_update_slice x48 -> x0, local copies, waits for them, and re-layouts: 33.2 us -> none  [one_head(): final, outputs = lax.scan(advance, head_state, items)]
  transfers between devices with their start and end apart: 8 -> 24, of which waited for: 3 -> 13; matrix products, arithmetic and copies ran while one was open for 14% -> 10% of each run, Pallas kernels for 0% -> 1%
where the time goes in v1:
time: 562 us; the launch traced here: 561 us
  waiting for transfers between devices  277 us (49%)
  blocking collectives  78.9 us (14%)
  Pallas kernels  59.2 us (11%)
  other arithmetic  39.3 us (7%)
  starting transfers between devices  31.8 us (6%)
  matrix products  30.4 us (5%)
  local copies, waits for them, and re-layouts  29.2 us (5%)
  between operations  15 us (3%)
    psum x2, waiting for transfers between devices, local(): lax.psum((dot_cols(normed, grad_proj).astype(BF), dot_cols(normed, grad_o...  225 us
    ppermute x12, waiting for transfers between devices, swapped(): lax.ppermute(value, axis, [(s, s ^ bit) for s in range(lax.axis_size(axis...  43 us
    psum x1, blocking collectives, local(): grad_o_gain = lax.psum(grad_o_part, ('seq', 'head'))[0]  41 us
    psum x1, blocking collectives, local(): lax.psum((grad_attn_gain, grad_mlp_gain, grad_taps[:taps], grad_scalars),...  37.9 us
    pallas_call x1, Pallas kernels, mixer_back(): pl.pallas_call(functools.partial(back_kernel, heads, reach), out_shape=ou...  28.7 us
    ppermute x10, starting transfers between devices, shifted(): lax.ppermute(value, axis, [(source, source + steps) for source in range(l...  26.1 us
    pallas_call x1, Pallas kernels, mixer_prep(): pl.pallas_call(functools.partial(prep_kernel, heads), out_shape=outs, in_...  22.7 us
    dot_general x7, matrix products, dot_cols(): lax.dot_general(left, right, (((0,), (0,)), ((), ())), preferred_element_...  15.2 us
  transfers between devices with their start and end apart: 24, of which 13 were waited for; matrix products, arithmetic and copies ran while one was open for 10% of the time, Pallas kernels for 1%

profile of v1, /device:TPU:0, one launch (start us, length us, event | category | flops | bytes accessed | tf_op | source)
XLA Modules:
  0.0 560.6 jit_solution(9203578712960159769)
XLA Ops:
  14.0 4.8 collective-permute-start
  21.3 22.7 %mixer_prep.1 = (f32[2,512,256]{2,1,0:T(8,128)}, bf16[2,8,128,256]{3,2,1,0:T(8,128)(2,1)}, bf16[2,8,128,128]{3,2,1,0:T(8,128)(2,1)}, bf16[2,8,128,128]{3,2,1,0:T...) custom-call(s32[10]{0:T(128)} %starts.3, ...), custom_call_target="tpu_custom_call" | custom-call | flops 4000000000 | bytes 16000000 | tf_op jit(solution)/shard_map/mixer_prep/pallas_call | solution.py:280
  44.9 4.0 collective-permute-start.1
  49.0 3.5 collective-permute-start.2
  52.4 5.5 collective-permute-start.3
  60.7 4.0 attend.1
  66.1 2.6 collective-permute-done.4
  71.7 12.4 %collective-permute-done.5 = bf16[256,1024]{1,0:T(8,128)(2,1)S(1)} collective-permute-done((bf16[256,1024]{1,0:T(8,128)(2,1)S(1)}, bf16[256,1024]{1,0:T(8,128)(2,1)S(1)}, u32[]{:S(2)}, u32[]{:S(2)}) %collective-permute-start.5) | collective-permute-done | bytes 524320 | tf_op jit(solution)/shard_map/ppermute | solution.py:659
  85.3 2.9 collective-permute-done.6
  93.2 2.4 multiply_convert_fusion.1
  103.5 6.4 %compare_convert_fusion = (f32[8]{0:T(128)S(1)}, f32[8]{0:T(128)S(1)}) fusion(s32[]{:T(128)} %bitcast.12, s32[]{:T(128)} %bitcast.11, s32[]{:T(128)} %bitcast.10, s32[]{:T(128)} %bitcast.9, s32[]{:T(128)} %bitcast.8, s32[]{:T(128)} %bitcast.7, s32[]{:T(128)} %bitcast.6, s32[]{:T(128)} %bitcast.5, s32[]{:T(128)} %bitcast.4, s32[]{:T(128)S(6)} %sub.15, s32[]{:T(128)} %bitcast.3), kind=kLoop, calls=%fused_computation.92 | loop fusion | flops 752 | bytes 108 | tf_op jit(solution)/shard_map/convert_element_type | solution.py:780
  113.0 6.4 %compare_convert_fusion.22 = f32[8]{0:T(128)S(1)} fusion(s32[]{:T(128)} %bitcast.12, s32[]{:T(128)} %bitcast.11, s32[]{:T(128)} %bitcast.10, s32[]{:T(128)} %bitcast.9, s32[]{:T(128)} %bitcast.8, s32[]{:T(128)} %bitcast.7, s32[]{:T(128)} %bitcast.6, s32[]{:T(128)} %bitcast.5, s32[]{:T(128)} %bitcast.4, s32[]{:T(128)S(6)} %sub.15, s32[]{:T(128)} %bitcast.3), kind=kLoop, calls=%fused_computation.114 | loop fusion | flops 496 | bytes 76 | tf_op jit(solution)/shard_map/convert_element_type | solution.py:780
  123.2 2.5 collective-permute-done.11
  130.0 6.6 %collective-permute-done.8 = bf16[256,1024]{1,0:T(8,128)(2,1)S(1)} collective-permute-done((bf16[256,1024]{1,0:T(8,128)(2,1)S(1)}, bf16[256,1024]{1,0:T(8,128)(2,1)S(1)}, u32[]{:S(2)}, u32[]{:S(2)}) %collective-permute-start.8) | collective-permute-done | bytes 524320 | tf_op jit(solution)/shard_map/ppermute | solution.py:659
  140.9 2.8 fusion.76
  143.7 3.8 attend_back.1
  151.5 2.4 convolution_convert_fusion.6
  155.3 2.4 collective-permute-done.14.rest_1_
  157.6 2.8 collective-permute-done.15.rest_2_
  161.0 28.7 %mixer_back.1 = (bf16[512,1280]{1,0:T(8,128)(2,1)}, f32[8,1280]{1,0:T(8,128)}, f32[8,1280]{1,0:T(8,128)}, bf16[512,128]{1,0:T(8,128)(2,1)}, f32[8,1280]{1,0:T(8,128)}, /*index=5*/f32[8,128]{1,0:T(8,128)}) custom-call(s32[10]{0:T(128)} %starts.3, f32[2]{0:T(128)} %log_rate.3, f32[2]{0:T(128)} %bias.3, bf16[512,1280]{1,0:T(8,128)(2,1)} %copy-done.51, ...), custom_call_target="tpu_custom_call" | custom-call | flops 8000000000 | bytes 20000000 | tf_op jit(solution)/shard_map/mixer_back/pallas_call | solution.py:631
  191.1 2.3 fusion.69
  195.1 2.8 collective-permute-done.18
  198.0 3.1 convolution_convert_fusion
  206.4 2.6 collective-permute-done.19
  209.9 13.3 %collective-permute-done.20 = bf16[256,1024]{1,0:T(8,128)(2,1)S(1)} collective-permute-done((bf16[256,1024]{1,0:T(8,128)(2,1)S(1)}, bf16[256,1024]{1,0:T(8,128)(2,1)S(1)}, u32[]{:S(2)}, u32[]{:S(2)}) %collective-permute-start.20) | collective-permute-done | bytes 524320 | tf_op jit(solution)/shard_map/ppermute | solution.py:659
  224.0 41.0 %psum.90 = f32[128]{0:T(128)} all-reduce(f32[128]{0:T(128)S(1)} %bitcast.53), channel_id=1, replica_groups=mesh['seq'=8,'head'=4] {'seq','head'}, use_global_device_ids=true, to_apply=%region_11.12 | all-reduce | flops 128 | bytes 1024 | tf_op jit(solution)/shard_map/psum | solution.py:799
  265.1 4.1 all-reduce.6.cloned.1.call-done
  275.6 37.9 %all-reduce.1 = (f32[1024]{0:T(1024)}, f32[4,1280]{1,0:T(4,128)S(1)}, f32[8,128]{1,0:T(8,128)S(1)}, f32[1024]{0:T(1024)}) all-reduce(f32[1024]{0:T(1024)S(1)} %get-tuple-element.100, f32[4,1280]{1,0:T(4,128)S(1)} %slice.158, f32[8,128]{1,0:T(8,128)S(1)} %copy-done.50, f32[1024]{0:T(1024)S(1)} %copy-done.43), channel_id=1, replica_groups=mesh['seq'=8,'head'=4] {'seq'}, use_global_device_ids=true, to_apply=%region_5.6 | all-reduce | flops 8192 | bytes 65536 | tf_op jit(solution)/shard_map/psum | solution.py:796
  315.3 3.1 fusion.6
  318.5 220.9 %all-reduce.8.cloned.1.call-done = (bf16[1024,1280]{1,0:T(8,128)(2,1)}, bf16[1024,256]{1,0:T(8,128)(2,1)}, bf16[256,1024]{1,0:T(8,128)(2,1)}, bf16[1024,704]{0,1...) async-done(((bf16[1024,1280]{1,0:T(8,128)(2,1)}, bf16[1024,256]{1,0:T(8,128)(2,1)}, bf16[256,1024]{1,0:T(8,128)(2,1)}, bf16[1024,704]{0,1:T(8,128)(2,1)}, ...) | async-done | bytes 7995408 | tf_op jit(solution)/shard_map/psum | solution.py:788
  539.4 4.2 fusion.78
  543.5 2.2 slice.170
  (238 shorter events, 78.2 us)
Async XLA Ops:
  7.2 85.7 %copy-start = (bf16[704,1024]{1,0:T(8,128)(2,1)S(1)}, bf16[704,1024]{1,0:T(8,128)(2,1)}, u32[]{:S(2)}) copy-start(bf16[704,1024]{1,0:T(8,128)(2,1)} %param.40) | copy-start | bytes 4325380
  7.2 262.0 %all-reduce.6.cloned.1.call-start = ((), (), s32[]{:S(2)}) async-start(), calls=%async_computation | async-start | bytes 1048576 | tf_op jit(solution)/shard_map/psum | solution.py:788
  14.0 6.7 %collective-permute-start = (bf16[16,1280]{1,0:T(8,128)(2,1)S(1)}, bf16[16,1280]{1,0:T(8,128)(2,1)S(1)}, u32[]{:S(2)}, u32[]{:S(2)}) collective-permute-start(bf16[16,1280]{1,0:T(8,128)(2,1)S(1)} %slice.166), channel_id=1, source_target_pairs={{0,4},{4,8},{8,12},{12,16},{16,20},{20,24},{24,28},{1,5},{5,9},{9,... | collective-permute-start | bytes 122888 | tf_op jit(solution)/shard_map/ppermute | solution.py:655
  19.0 25.0 %copy-start.15 = (bf16[1024,4]{1,0:T(8,128)(2,1)}, bf16[1024,4]{1,0:T(8,128)(2,1)S(1)}, u32[]{:S(2)}) copy-start(bf16[1024,4]{1,0:T(8,128)(2,1)S(1)} %copy.41) | copy-start | bytes 24580
  19.2 24.8 %copy-start.17 = (bf16[1024,2]{1,0:T(8,128)(2,1)}, bf16[1024,2]{1,0:T(8,128)(2,1)S(1)}, u32[]{:S(2)}) copy-start(bf16[1024,2]{1,0:T(8,128)(2,1)S(1)} %copy.42) | copy-start | bytes 12292
  19.3 24.7 %copy-start.52 = (bf16[128]{0:T(256)(128)(2,1)}, bf16[128]{0:T(256)(128)(2,1)S(1)}, u32[]{:S(2)}) copy-start(bf16[128]{0:T(256)(128)(2,1)S(1)} %pad.15.clone) | copy-start | bytes 772
  20.6 37.4 %copy-start.25 = (bf16[1024,256]{1,0:T(8,128)(2,1)S(1)}, bf16[1024,256]{1,0:T(8,128)(2,1)}, u32[]{:S(2)}) copy-start(bf16[1024,256]{1,0:T(8,128)(2,1)} %param.34) | copy-start | bytes 1572868
  44.9 15.1 %collective-permute-start.1 = (bf16[2,2,128,128]{3,2,1,0:T(8,128)(2,1)S(1)}, bf16[2,2,128,128]{3,2,1,0:T(8,128)(2,1)S(1)}, u32[]{:S(2)}, u32[]{:S(2)}) collective-permute-start(bf16[2,2,128,128]{3,2,1,0:T(8,128)(2,1)S(1)} %pad_maximum_fusion.5), channel_id=1, source_target_pairs={{0,4},{4,8},{8,12},{12,16},{16,20},{20,24},{24,28},{1,5},{5,9},{9,... | collective-permute-start | bytes 393224 | tf_op jit(solution)/shard_map/ppermute | solution.py:655
  49.0 11.1 %collective-permute-start.2 = (bf16[2,2,128,128]{3,2,1,0:T(8,128)(2,1)S(1)}, bf16[2,2,128,128]{3,2,1,0:T(8,128)(2,1)S(1)}, u32[]{:S(2)}, u32[]{:S(2)}) collective-permute-start(bf16[2,2,128,128]{3,2,1,0:T(8,128)(2,1)S(1)} %pad_maximum_fusion.5), channel_id=1, source_target_pairs={{0,8},{4,12},{8,16},{12,20},{16,24},{20,28},{1,9},{5,13},{9,17},{1... | collective-permute-start | bytes 393224 | tf_op jit(solution)/shard_map/ppermute | solution.py:655
  52.4 7.6 %collective-permute-start.3 = (bf16[1,2,128,128]{3,2,1,0:T(8,128)(2,1)}, bf16[1,2,128,128]{3,2,1,0:T(8,128)(2,1)S(1)}, u32[]{:S(2)}, u32[]{:S(2)}) collective-permute-start(bf16[1,2,128,128]{3,2,1,0:T(8,128)(2,1)} %bitcast.50), channel_id=1, source_target_pairs={{0,12},{4,16},{8,20},{12,24},{16,28},{1,13},{5,17},{9,21},{13,25},... | collective-permute-start | bytes 196616 | tf_op jit(solution)/shard_map/ppermute | solution.py:655
  66.0 2.7 collective-permute-start.4
  70.1 14.0 %collective-permute-start.5 = (bf16[256,1024]{1,0:T(8,128)(2,1)S(1)}, bf16[256,1024]{1,0:T(8,128)(2,1)S(1)}, u32[]{:S(2)}, u32[]{:S(2)}) collective-permute-start(bf16[256,1024]{1,0:T(8,128)(2,1)S(1)} %add_convert_fusion.3), channel_id=1, source_target_pairs={{0,2},{1,3},{2,0},{3,1},{4,6},{5,7},{6,4},{7,5},{8,10},{9,11},{10,... | collective-permute-start | bytes 1572872 | tf_op jit(solution)/shard_map/ppermute | solution.py:659
  85.3 2.9 collective-permute-start.6
  100.0 10.0 %collective-permute-start.10 = (f32[256,1024]{1,0:T(8,128)}, f32[256,1024]{1,0:T(8,128)}, u32[]{:S(2)}, u32[]{:S(2)}) collective-permute-start(f32[256,1024]{1,0:T(8,128)} %constant_dynamic-slice_fusion.1), channel_id=1, source_target_pairs={{0,1},{1,0},{2,3},{3,2},{4,5},{5,4},{6,7},{7,6},{8,9},{9,8},{10,11... | collective-permute-start | bytes 3145736 | tf_op jit(solution)/shard_map/ppermute | solution.py:659
  102.4 17.1 %copy-start.34 = (bf16[2,128,128]{2,1,0:T(8,128)(2,1)S(1)}, bf16[2,128,128]{2,1,0:T(8,128)(2,1)}, u32[]{:S(2)}) copy-start(bf16[2,128,128]{2,1,0:T(8,128)(2,1)} %get-tuple-element.51) | copy-start | bytes 196612
  102.5 20.0 %collective-permute-start.7 = (f32[256,1024]{1,0:T(8,128)S(1)}, f32[256,1024]{1,0:T(8,128)S(1)}, u32[]{:S(2)}, u32[]{:S(2)}) collective-permute-start(f32[256,1024]{1,0:T(8,128)S(1)} %constant_dynamic-slice_fusion.2), channel_id=1, source_target_pairs={{0,1},{1,0},{2,3},{3,2},{4,5},{5,4},{6,7},{7,6},{8,9},{9,8},{10,11... | collective-permute-start | bytes 3145736 | tf_op jit(solution)/shard_map/ppermute | solution.py:659
  111.4 14.3 %collective-permute-start.11 = (bf16[256,1024]{1,0:T(8,128)(2,1)S(1)}, bf16[256,1024]{1,0:T(8,128)(2,1)S(1)}, u32[]{:S(2)}, u32[]{:S(2)}) collective-permute-start(bf16[256,1024]{1,0:T(8,128)(2,1)S(1)} %add_convert_fusion.1), channel_id=1, source_target_pairs={{0,2},{1,3},{2,0},{3,1},{4,6},{5,7},{6,4},{7,5},{8,10},{9,11},{10,... | collective-permute-start | bytes 1572872 | tf_op jit(solution)/shard_map/ppermute | solution.py:659
  119.5 35.7 %collective-permute-start.16 = (bf16[2,128,128]{2,1,0:T(8,128)(2,1)S(1)}, bf16[2,128,128]{2,1,0:T(8,128)(2,1)S(1)}, u32[]{:S(2)}, u32[]{:S(2)}) collective-permute-start(bf16[2,128,128]{2,1,0:T(8,128)(2,1)S(1)} %copy-done.34), channel_id=1, source_target_pairs={{4,0},{8,4},{12,8},{16,12},{20,16},{24,20},{28,24},{5,1},{9,5},{13... | collective-permute-start | bytes 196616 | tf_op jit(solution)/shard_map/ppermute | solution.py:655
  120.9 34.3 %collective-permute-start.17 = (bf16[2,128,128]{2,1,0:T(8,128)(2,1)S(1)}, bf16[2,128,128]{2,1,0:T(8,128)(2,1)S(1)}, u32[]{:S(2)}, u32[]{:S(2)}) collective-permute-start(bf16[2,128,128]{2,1,0:T(8,128)(2,1)S(1)} %copy-done.34), channel_id=1, source_target_pairs={{8,0},{12,4},{16,8},{20,12},{24,16},{28,20},{9,1},{13,5},{17,9},{2... | collective-permute-start | bytes 196616 | tf_op jit(solution)/shard_map/ppermute | solution.py:655
  122.6 14.1 %collective-permute-start.8 = (bf16[256,1024]{1,0:T(8,128)(2,1)S(1)}, bf16[256,1024]{1,0:T(8,128)(2,1)S(1)}, u32[]{:S(2)}, u32[]{:S(2)}) collective-permute-start(bf16[256,1024]{1,0:T(8,128)(2,1)S(1)} %add_convert_fusion.2), channel_id=1, source_target_pairs={{0,2},{1,3},{2,0},{3,1},{4,6},{5,7},{6,4},{7,5},{8,10},{9,11},{10,... | collective-permute-start | bytes 1572872 | tf_op jit(solution)/shard_map/ppermute | solution.py:659
  125.8 13.1 %collective-permute-start.12 = (f32[256,1024]{1,0:T(8,128)S(1)}, f32[256,1024]{1,0:T(8,128)S(1)}, u32[]{:S(2)}, u32[]{:S(2)}) collective-permute-start(f32[256,1024]{1,0:T(8,128)S(1)} %convert_add_fusion.2), channel_id=1, source_target_pairs={{0,1},{1,0},{2,3},{3,2},{4,5},{5,4},{6,7},{7,6},{8,9},{9,8},{10,11... | collective-permute-start | bytes 3145736 | tf_op jit(solution)/shard_map/ppermute | solution.py:659
  136.8 3.7 collective-permute-start.9
  147.5 7.7 %collective-permute-start.13 = (bf16[2,128,128]{2,1,0:T(8,128)(2,1)}, bf16[2,128,128]{2,1,0:T(8,128)(2,1)S(1)}, u32[]{:S(2)}, u32[]{:S(2)}) collective-permute-start(bf16[2,128,128]{2,1,0:T(8,128)(2,1)} %get-tuple-element.68), channel_id=1, source_target_pairs={{4,0},{8,4},{12,8},{16,12},{20,16},{24,20},{28,24},{5,1},{9,5},{13... | collective-permute-start | bytes 196616 | tf_op jit(solution)/shard_map/ppermute | solution.py:655
  148.9 8.7 %collective-permute-start.14 = (bf16[2,128,128]{2,1,0:T(8,128)(2,1)}, bf16[2,128,128]{2,1,0:T(8,128)(2,1)S(1)}, u32[]{:S(2)}, u32[]{:S(2)}) collective-permute-start(bf16[2,128,128]{2,1,0:T(8,128)(2,1)} %get-tuple-element.68), channel_id=1, source_target_pairs={{8,0},{12,4},{16,8},{20,12},{24,16},{28,20},{9,1},{13,5},{17,9},{2... | collective-permute-start | bytes 196616 | tf_op jit(solution)/shard_map/ppermute | solution.py:655
  150.2 10.2 %collective-permute-start.15 = (bf16[2,128,128]{2,1,0:T(8,128)(2,1)}, bf16[2,128,128]{2,1,0:T(8,128)(2,1)S(1)}, u32[]{:S(2)}, u32[]{:S(2)}) collective-permute-start(bf16[2,128,128]{2,1,0:T(8,128)(2,1)} %get-tuple-element.68), channel_id=1, source_target_pairs={{12,0},{16,4},{20,8},{24,12},{28,16},{13,1},{17,5},{21,9},{25,13},... | collective-permute-start | bytes 196616 | tf_op jit(solution)/shard_map/ppermute | solution.py:655
  189.8 8.1 %collective-permute-start.18 = (f32[8,1280]{1,0:T(8,128)}, f32[8,1280]{1,0:T(8,128)S(1)}, u32[]{:S(2)}, u32[]{:S(2)}) collective-permute-start(f32[8,1280]{1,0:T(8,128)} %get-tuple-element.71), channel_id=1, source_target_pairs={{4,0},{8,4},{12,8},{16,12},{20,16},{24,20},{28,24},{5,1},{9,5},{13... | collective-permute-start | bytes 122888 | tf_op jit(solution)/shard_map/ppermute | solution.py:655
  194.8 344.6 %all-reduce.8.cloned.1.call-start = ((), (), s32[]{:S(2)}) async-start(), calls=%async_computation.1 | async-start | bytes 15990784 | tf_op jit(solution)/shard_map/psum | solution.py:788
  206.3 17.7 %copy-start.62 = (f32[1,128]{1,0:T(1,128)S(1)}, f32[1,128]{1,0:T(1,128)}, u32[]{:S(2)}) copy-start(f32[1,128]{1,0:T(1,128)} %get-tuple-element.76) | copy-start | bytes 1540
  206.3 58.8 %copy-start.44 = (f32[8,1280]{1,0:T(8,128)S(1)}, f32[8,1280]{1,0:T(8,128)}, u32[]{:S(2)}) copy-start(f32[8,1280]{1,0:T(8,128)} %get-tuple-element.74) | copy-start | bytes 122884
  206.3 2.7 collective-permute-start.19
  209.2 14.0 %collective-permute-start.20 = (bf16[256,1024]{1,0:T(8,128)(2,1)S(1)}, bf16[256,1024]{1,0:T(8,128)(2,1)S(1)}, u32[]{:S(2)}, u32[]{:S(2)}) collective-permute-start(bf16[256,1024]{1,0:T(8,128)(2,1)S(1)} %add_convert_fusion), channel_id=1, source_target_pairs={{0,2},{1,3},{2,0},{3,1},{4,6},{5,7},{6,4},{7,5},{8,10},{9,11},{10,... | collective-permute-start | bytes 1572872 | tf_op jit(solution)/shard_map/ppermute | solution.py:659
  224.0 49.0 %collective-permute-start.21 = (f32[256,1024]{1,0:T(8,128)S(1)}, f32[256,1024]{1,0:T(8,128)}, u32[]{:S(2)}, u32[]{:S(2)}) collective-permute-start(f32[256,1024]{1,0:T(8,128)S(1)} %convert_add_fusion.1), channel_id=1, source_target_pairs={{0,1},{1,0},{2,3},{3,2},{4,5},{5,4},{6,7},{7,6},{8,9},{9,8},{10,11... | collective-permute-start | bytes 3145736 | tf_op jit(solution)/shard_map/ppermute | solution.py:659
  (60 other events, 218.6 us)
Sparse Core Ops, SparseCore 0:
  194.9 74.2 all-reduce.5
  276.3 263.0 all-reduce.7

commit v2 on v1

--- a/solution.py
+++ b/solution.py
@@ -1,4 +1,5 @@
 import functools
+import math
 import jax
 import jax.numpy as jnp
 from jax import lax
@@ -13,7 +14,9 @@
 BF = jnp.bfloat16
 F32 = jnp.float32
 VMEM = pltpu.VMEM
-VMEM_LIMIT = 60 * 1024 * 1024
+VMEM_LIMIT = 40 * 1024 * 1024
+SMALL_LIMIT = 24 * 1024 * 1024
+EARLY = 16
 
 
 def mm(left, right):
@@ -290,88 +293,9 @@
             VMEM((8, LANES, LANES), F32),
         ],
         compiler_params=pltpu.CompilerParams(vmem_limit_bytes=VMEM_LIMIT),
-        cost_estimate=pl.CostEstimate(flops=4_000_000_000, bytes_accessed=16_000_000, transcendentals=2_000_000),
+        cost_estimate=pl.CostEstimate(flops=2_000_000_000, bytes_accessed=4_000_000, transcendentals=0),
         name="mixer_prep",
     )(starts, log_rate, bias, proj, halo, conv_q, conv_k, conv_v, small)
-
-
-def attend_kernel(heads, reach, out_aug, outgate, o_gain, out_weight, *rest):
-    before = rest[:reach]
-    mixed, branch, partial, state_in = rest[reach:]
-    gain = o_gain[...]
-    for h in range(heads):
-        at = slice(h * LANES, (h + 1) * LANES)
-        state = before[reach - 1][0, h].astype(F32)
-        for r in range(reach - 2, -1, -1):
-            state = mm(before[r][1, h], state) + before[r][0, h].astype(F32)
-        state_in[h] = state
-        mix = out_aug[h, :, :LANES] + mm(out_aug[h, :, LANES:], state)
-        mixed[:, at] = mix
-        gate = outgate[:, at]
-        normed = mix * lax.rsqrt(jnp.mean(mix * mix, axis=1, keepdims=True) + EPSILON)
-        branch[:, at] = (normed * gain * (gate * sigmoid(gate))).astype(BF)
-    partial[...] = mm(branch[...], out_weight[...]).astype(partial.dtype)
-
-
-def attend(out_aug, outgate, o_gain, out_weight, before, dtype=F32):
-    heads, tokens, _ = out_aug.shape
-    shape = jax.ShapeDtypeStruct
-    reach = len(before)
-    outs = [
-        shape((tokens, heads * LANES), F32),
-        shape((tokens, heads * LANES), BF),
-        shape((tokens, out_weight.shape[1]), dtype),
-        shape((heads, LANES, LANES), F32),
-    ]
-    return pl.pallas_call(
-        functools.partial(attend_kernel, heads, reach),
-        out_shape=outs,
-        in_specs=specs(4 + reach),
-        out_specs=specs(len(outs)),
-        compiler_params=pltpu.CompilerParams(vmem_limit_bytes=VMEM_LIMIT),
-        name="attend",
-    )(out_aug, outgate, o_gain.reshape(1, -1), out_weight, *before)
-
-
-def attend_back_kernel(heads, grad, out_weight, mixed, outgate, o_gain, out_aug, d_mixed, d_outgate, d_gain, carry):
-    gain = o_gain[...]
-    d_branch = mm_nt(grad[...], out_weight[...])
-    gain_sum = jnp.zeros((1, LANES), F32)
-    for h in range(heads):
-        at = slice(h * LANES, (h + 1) * LANES)
-        mix = mixed[:, at]
-        gate = outgate[:, at]
-        grad_h = d_branch[:, at]
-        scale = lax.rsqrt(jnp.mean(mix * mix, axis=1, keepdims=True) + EPSILON)
-        normed = mix * scale
-        sg = sigmoid(gate)
-        through = grad_h * (gate * sg)
-        gain_sum += jnp.sum(through * normed, axis=0, keepdims=True)
-        d_normed = through * gain
-        d_mix = scale * (d_normed - normed * jnp.mean(d_normed * normed, axis=1, keepdims=True))
-        d_mixed[:, at] = d_mix.astype(BF)
-        d_outgate[:, at] = (grad_h * normed * gain * (sg * (1.0 + gate * (1.0 - sg)))).astype(BF)
-        carry[h] = mm_tn(out_aug[h, :, LANES:], d_mix).astype(carry.dtype)
-    d_gain[...] = gain_sum
-
-
-def attend_back(grad, out_weight, mixed, outgate, o_gain, out_aug):
-    heads, tokens, _ = out_aug.shape
-    shape = jax.ShapeDtypeStruct
-    outs = [
-        shape((tokens, heads * LANES), BF),
-        shape((tokens, heads * LANES), BF),
-        shape((1, LANES), F32),
-        shape((heads, LANES, LANES), BF),
-    ]
-    return pl.pallas_call(
-        functools.partial(attend_back_kernel, heads),
-        out_shape=outs,
-        in_specs=specs(6),
-        out_specs=specs(len(outs)),
-        compiler_params=pltpu.CompilerParams(vmem_limit_bytes=VMEM_LIMIT),
-        name="attend_back",
-    )(grad, out_weight, mixed, outgate, o_gain.reshape(1, -1), out_aug)
 
 
 def back_kernel(
@@ -382,7 +306,7 @@
     after = rest[:reach]
     later = rest[reach : 2 * reach - 1]
     (
-        d_proj, tail, lead_rows, d_small, d_taps, d_scalars,
+        d_kq, d_v, tail, d_halo, d_small, d_taps, d_scalars,
         ext, state_grads, d_query, d_key, d_value, col_grads, row_grads, d_total,
     ) = rest[2 * reach - 1 :]
     tokens = proj.shape[0]
@@ -588,7 +512,6 @@
         return 0
 
     lax.fori_loop(0, chunks, active_back, 0)
-    lead_rows[...] = d_total[0:8, :]
 
     def conv_back(c, _):
         base = pl.multiple_of(c * GROUP, GROUP)
@@ -605,11 +528,24 @@
             grad = kernel[taps - 1 : taps, cut] * window[:GROUP]
             for lag in range(1, taps):
                 grad += kernel[taps - 1 - lag : taps - lag, cut] * kept[lag - 1] * window[lag : lag + GROUP]
-            d_proj[rows, at] = grad.astype(BF)
-            tail[:, at] = grad[GROUP - 8 :]
+            target = d_v if kernel is conv_v else d_kq
+            shift = width_k if kernel is conv_q else 0
+            target[rows, cut.start + shift : cut.stop + shift] = grad.astype(BF)
+            tail[:, at] = grad[GROUP - 16 :]
         return 0
 
     lax.fori_loop(0, chunks, conv_back, 0)
+    position = lax.broadcasted_iota(jnp.int32, (8, LANES), 0) + (first - 8)
+    document = documents_at(starts, position)
+    for group in range(width // LANES):
+        at = slice(group * LANES, (group + 1) * LANES)
+        kernel, cut = kernel_of(group)
+        window = jnp.concatenate([jnp.zeros((8, LANES), F32), d_total[0:8, at]], axis=0)
+        grad = jnp.zeros((8, LANES), F32)
+        for lag in range(1, taps):
+            kept = (documents_at(starts, position + lag) == document).astype(F32)
+            grad += kernel[taps - 1 - lag : taps - lag, cut] * kept * window[lag : lag + 8]
+        d_halo[:, at] = grad
 
 
 def mixer_back(starts, log_rate, bias, proj, halo, conv_q, conv_k, conv_v, small, saved, state_in, d_mixed, after, later):
@@ -620,8 +556,9 @@
     square = (heads, chunks, LANES, LANES)
     shape = jax.ShapeDtypeStruct
     outs = [
-        shape((tokens, width), BF),
-        shape((8, width), F32),
+        shape((tokens, conv_k.shape[1] + conv_q.shape[1]), BF),
+        shape((tokens, conv_v.shape[1]), BF),
+        shape((16, width), F32),
         shape((8, width), F32),
         shape((tokens, LANES), BF),
         shape((8, width), F32),
@@ -644,9 +581,458 @@
             VMEM((tokens + 8, width), F32),
         ],
         compiler_params=pltpu.CompilerParams(vmem_limit_bytes=VMEM_LIMIT),
-        cost_estimate=pl.CostEstimate(flops=8_000_000_000, bytes_accessed=20_000_000, transcendentals=2_000_000),
+        cost_estimate=pl.CostEstimate(flops=2_000_000_000, bytes_accessed=4_000_000, transcendentals=0),
         name="mixer_back",
     )(*operands)
+
+
+def call(kernel, name, outs, operands, smem=0, scratch=(), flops=0, limit=SMALL_LIMIT):
+    moved = sum(a.size * a.dtype.itemsize for a in operands) + sum(
+        math.prod(o.shape) * jnp.dtype(o.dtype).itemsize for o in outs
+    )
+    return pl.pallas_call(
+        kernel,
+        out_shape=outs,
+        in_specs=specs(smem, pltpu.SMEM) + specs(len(operands) - smem),
+        out_specs=specs(len(outs)),
+        scratch_shapes=list(scratch),
+        compiler_params=pltpu.CompilerParams(vmem_limit_bytes=limit),
+        cost_estimate=pl.CostEstimate(flops=flops // EARLY, bytes_accessed=moved // EARLY, transcendentals=0),
+        name=name,
+    )(*operands)
+
+
+def shaped(dims, kind):
+    return jax.ShapeDtypeStruct(dims, kind)
+
+
+def half_rows(ref, own):
+    half = ref.shape[0] // 2
+    low = lax.axis_index("head") % 2
+    return pl.ds(pl.multiple_of((low if own else 1 - low) * half, half), half)
+
+
+def seq_bits():
+    at = lax.axis_index("seq")
+    z = at // 2 % 4
+    low, high = z % 2, z // 2
+    return {"x": at % 2, "pair": low ^ high, "cross": high}
+
+
+PARTNER = {"x": 1, "pair": 2, "cross": 6}
+X_FIRST = ("x", "pair", "cross")
+Z_FIRST = ("pair", "cross", "x")
+
+
+def half_width(ref, own, stage="x"):
+    half = ref.shape[1] // 2
+    low = seq_bits()[stage]
+    return pl.ds(pl.multiple_of((low if own else 1 - low) * half, half), half)
+
+
+def project_kernel(x, gain, q_w, k_w, v_w, gate_w, beta_w, decay_w, normed, projected, outgate, small, edge, side_w):
+    x_float = x[...].astype(F32)
+    low = (x_float * lax.rsqrt(jnp.mean(x_float * x_float, axis=1, keepdims=True) + EPSILON) * gain[...]).astype(BF)
+    normed[...] = low
+    last = x.shape[0] - edge.shape[0]
+    at = 0
+    for weight in (q_w, k_w, v_w):
+        piece = mm(low, weight[...]).astype(BF)
+        projected[:, at : at + weight.shape[1]] = piece
+        edge[:, at : at + weight.shape[1]] = piece[last:, :]
+        at += weight.shape[1]
+    edge[:, at:] = low[last:, :]
+    outgate[...] = mm(low, gate_w[...])
+    gather_side(side_w, beta_w, decay_w)
+    small[...] = mm_nt(low, side_w[...])
+
+
+def gather_side(side_w, beta_w, decay_w):
+    betas = beta_w.shape[0]
+    side_w[...] = jnp.zeros(side_w.shape, F32)
+    side_w[0:betas, :] = beta_w[...].astype(F32)
+    side_w[betas : betas + decay_w.shape[0], :] = decay_w[...].astype(F32)
+
+
+def project(x, gain, q_w, k_w, v_w, gate_w, beta_w, decay_w):
+    tokens, wide = x.shape
+    width = q_w.shape[1] + k_w.shape[1] + v_w.shape[1]
+    outs = [
+        shaped((tokens, wide), BF), shaped((tokens, width), BF),
+        shaped((tokens, gate_w.shape[1]), F32), shaped((tokens, LANES), F32), shaped((16, width + wide), BF),
+    ]
+    operands = [x, gain.reshape(1, -1), q_w, k_w, v_w, gate_w, beta_w, decay_w]
+    return call(
+        project_kernel, "project", outs, operands, flops=2 * tokens * wide * (width + 384),
+        scratch=[VMEM((LANES, wide), F32)],
+    )
+
+
+def attend_kernel(heads, reach, out_aug, outgate, o_gain, out_weight, *rest):
+    before = rest[:reach]
+    mixed, branch, give, keep, state_in = rest[reach:]
+    gain = o_gain[...]
+    for h in range(heads):
+        at = slice(h * LANES, (h + 1) * LANES)
+        state = before[reach - 1][0, h].astype(F32)
+        for r in range(reach - 2, -1, -1):
+            state = mm(before[r][1, h], state) + before[r][0, h].astype(F32)
+        state_in[h] = state
+        mix = out_aug[h, :, :LANES] + mm(out_aug[h, :, LANES:], state)
+        mixed[:, at] = mix
+        gate = outgate[:, at]
+        normed = mix * lax.rsqrt(jnp.mean(mix * mix, axis=1, keepdims=True) + EPSILON)
+        branch[:, at] = (normed * gain * (gate * sigmoid(gate))).astype(BF)
+    give[...] = mm(branch[half_rows(branch, False), :], out_weight[...]).astype(BF)
+    keep[...] = mm(branch[half_rows(branch, True), :], out_weight[...])
+
+
+def attend(out_aug, outgate, o_gain, out_weight, before):
+    heads, tokens, _ = out_aug.shape
+    wide = out_weight.shape[1]
+    outs = [
+        shaped((tokens, heads * LANES), F32), shaped((tokens, heads * LANES), BF),
+        shaped((tokens // 2, wide), BF), shaped((tokens // 2, wide), F32), shaped((heads, LANES, LANES), F32),
+    ]
+    operands = [out_aug, outgate, o_gain.reshape(1, -1), out_weight, *before]
+    return call(
+        functools.partial(attend_kernel, heads, len(before)), "attend", outs, operands,
+        flops=2 * tokens * wide * heads * LANES,
+    )
+
+
+def enter_kernel(x, mine, other, gain, hidden, normed):
+    value = x[half_rows(x, True), :].astype(F32) + mine[...].astype(F32) + other[...].astype(F32)
+    hidden[...] = value
+    normed[...] = (
+        value * lax.rsqrt(jnp.mean(value * value, axis=1, keepdims=True) + EPSILON) * gain[...]
+    ).astype(BF)
+
+
+def enter(x, mine, other, gain):
+    outs = [shaped(mine.shape, F32), shaped(mine.shape, BF)]
+    return call(enter_kernel, "enter", outs, [x, mine, other, gain.reshape(1, -1)])
+
+
+def feed_kernel(
+    own, other, gate_w, up_w, down_w, out_grad,
+    normed, d_gate, d_up, inner, part_give, part_keep, feed_give, feed_keep,
+):
+    for mine, source, part, fed in ((False, other, part_give, feed_give), (True, own, part_keep, feed_keep)):
+        rows = half_rows(normed, mine)
+        low = source[...]
+        normed[rows, :] = low
+        gate = mm_nt(low, gate_w[...])
+        up = mm_nt(low, up_w[...])
+        d_inner = mm_nt(out_grad[rows, :], down_w[...])
+        sg = sigmoid(gate)
+        active = gate * sg
+        low_inner = (active * up).astype(BF)
+        inner[rows, :] = low_inner
+        low_gate = (d_inner * up * (sg * (1.0 + gate * (1.0 - sg)))).astype(BF)
+        low_up = (d_inner * active).astype(BF)
+        d_gate[rows, :] = low_gate
+        d_up[rows, :] = low_up
+        part[...] = (mm(low_gate, gate_w[...]) + mm(low_up, up_w[...])).astype(part.dtype)
+        fed[...] = mm(low_inner, down_w[...]).astype(fed.dtype)
+
+
+def feed(own, other, gate_w, up_w, down_w, out_grad):
+    tokens, wide = out_grad.shape
+    units = gate_w.shape[0]
+    half = (tokens // 2, wide)
+    outs = [shaped((tokens, wide), BF)] + [shaped((tokens, units), BF)] * 3 + [
+        shaped(half, BF), shaped(half, F32), shaped(half, BF), shaped(half, F32),
+    ]
+    operands = [own, other, gate_w, up_w, down_w, out_grad]
+    return call(feed_kernel, "feed", outs, operands, flops=12 * tokens * wide * units)
+
+
+def leave_kernel(mine, other, hidden, gain, out_grad, d_hidden, low, d_gain):
+    grad = mine[...].astype(F32) + other[...].astype(F32)
+    value = hidden[...]
+    scale = lax.rsqrt(jnp.mean(value * value, axis=1, keepdims=True) + EPSILON)
+    unit = value * scale
+    d_gain[...] = jnp.sum(grad * unit, axis=0, keepdims=True)
+    d_unit = grad * gain[...]
+    total = out_grad[half_rows(out_grad, True), :].astype(F32) + scale * (
+        d_unit - unit * jnp.mean(d_unit * unit, axis=1, keepdims=True)
+    )
+    d_hidden[...] = total
+    low[...] = total.astype(BF)
+
+
+def leave(mine, other, hidden, gain, out_grad):
+    outs = [shaped(mine.shape, F32), shaped(mine.shape, BF), shaped((1, mine.shape[1]), F32)]
+    return call(leave_kernel, "leave", outs, [mine, other, hidden, gain.reshape(1, -1), out_grad])
+
+
+def finish_kernel(mine, other, x, gain, d_hidden, low, d_gain):
+    grad = mine[...].astype(F32) + other[...].astype(F32)
+    value = x[half_rows(x, True), :].astype(F32)
+    scale = lax.rsqrt(jnp.mean(value * value, axis=1, keepdims=True) + EPSILON)
+    unit = value * scale
+    d_gain[...] = jnp.sum(grad * unit, axis=0, keepdims=True)
+    d_unit = grad * gain[...]
+    low[...] = (
+        d_hidden[...] + scale * (d_unit - unit * jnp.mean(d_unit * unit, axis=1, keepdims=True))
+    ).astype(BF)
+
+
+def finish(mine, other, x, gain, d_hidden):
+    outs = [shaped(mine.shape, BF), shaped((1, mine.shape[1]), F32)]
+    return call(finish_kernel, "finish", outs, [mine, other, x, gain.reshape(1, -1), d_hidden])
+
+
+def attend_back_kernel(
+    heads, own, other, out_weight, mixed, outgate, o_gain, out_aug,
+    grad, d_mixed, d_outgate, d_gain, carry,
+):
+    gain = o_gain[...]
+    gain_sum = jnp.zeros((1, LANES), F32)
+    carries = [jnp.zeros((LANES, LANES), F32)] * heads
+    for mine, source in ((True, own), (False, other)):
+        rows = half_rows(grad, mine)
+        low = source[...]
+        grad[rows, :] = low
+        d_branch = mm_nt(low, out_weight[...])
+        for h in range(heads):
+            at = slice(h * LANES, (h + 1) * LANES)
+            mix = mixed[rows, at]
+            gate = outgate[rows, at]
+            grad_h = d_branch[:, at]
+            scale = lax.rsqrt(jnp.mean(mix * mix, axis=1, keepdims=True) + EPSILON)
+            normed = mix * scale
+            sg = sigmoid(gate)
+            through = grad_h * (gate * sg)
+            gain_sum += jnp.sum(through * normed, axis=0, keepdims=True)
+            d_normed = through * gain
+            d_mix = (scale * (d_normed - normed * jnp.mean(d_normed * normed, axis=1, keepdims=True))).astype(BF)
+            d_mixed[rows, at] = d_mix
+            d_outgate[rows, at] = (grad_h * normed * gain * (sg * (1.0 + gate * (1.0 - sg)))).astype(BF)
+            carries[h] += mm_tn(out_aug[h, rows, LANES:], d_mix)
+    for h in range(heads):
+        carry[h] = carries[h].astype(carry.dtype)
+    d_gain[...] = gain_sum
+
+
+def attend_back(own, other, out_weight, mixed, outgate, o_gain, out_aug):
+    heads, tokens, _ = out_aug.shape
+    wide = out_weight.shape[1]
+    outs = [
+        shaped((tokens, wide), BF), shaped((tokens, heads * LANES), BF), shaped((tokens, heads * LANES), BF),
+        shaped((1, LANES), F32), shaped((heads, LANES, LANES), BF),
+    ]
+    operands = [own, other, out_weight, mixed, outgate, o_gain.reshape(1, -1), out_aug]
+    return call(
+        functools.partial(attend_back_kernel, heads), "attend_back", outs, operands,
+        flops=2 * tokens * wide * heads * LANES,
+    )
+
+
+def store_rows_cut(part, at, piece):
+    quarters = part.shape[0]
+    rows = piece.shape[0] // quarters
+    for q in range(quarters):
+        for i in range(piece.shape[1] // LANES):
+            part[q, at + i * rows : at + (i + 1) * rows, :] = piece[
+                q * rows : (q + 1) * rows, i * LANES : (i + 1) * LANES
+            ].astype(BF)
+
+
+def store_cols_cut(part, at, piece):
+    for q in range(part.shape[0]):
+        part[q, at : at + piece.shape[0], :] = piece[:, q * LANES : (q + 1) * LANES].astype(BF)
+
+
+def feed_weights_kernel(normed, d_gate, d_up, inner, out_grad, grads):
+    units = inner.shape[1]
+    for k, (left, right) in enumerate(((d_gate, normed), (d_up, normed), (inner, out_grad))):
+        grads[k * units : (k + 1) * units, :] = mm_tn(left[...], right[...]).astype(BF)
+
+
+def feed_weights(normed, d_gate, d_up, inner, out_grad):
+    tokens, wide = normed.shape
+    rows = 3 * inner.shape[1]
+    operands = [normed, d_gate, d_up, inner, out_grad]
+    (grads,) = call(
+        feed_weights_kernel, "feed_weights", [shaped((rows, wide), BF)], operands, flops=2 * tokens * wide * rows
+    )
+    return grads
+
+
+def gate_weights_kernel(normed, d_outgate, branch, grad, give, keep):
+    for own, part in ((False, give), (True, keep)):
+        store_rows_cut(part, 0, mm_tn(normed[:, half_width(normed, own)], d_outgate[...]))
+        store_cols_cut(part, d_outgate.shape[1], mm_tn(branch[...], grad[:, half_width(grad, own)]))
+
+
+def gate_weights(normed, d_outgate, branch, grad):
+    rows = d_outgate.shape[1] + branch.shape[1]
+    outs = [shaped((4, rows, LANES), BF)] * 2
+    operands = [normed, d_outgate, branch, grad]
+    return call(
+        gate_weights_kernel, "gate_weights", outs, operands, flops=2 * normed.shape[0] * normed.shape[1] * rows
+    )
+
+
+def mix_weights_kernel(first, normed, halo, d_cols, d_halo, *rest):
+    *side, give, keep = rest
+    low_halo = d_halo[...].astype(BF)
+    for own, part in ((False, give), (True, keep)):
+        at = half_width(normed, own, first)
+        left = normed[:, at]
+        total = mm_tn(left, d_cols[...]) + mm_tn(halo[halo.shape[0] - d_halo.shape[0] :, at], low_halo)
+        store_rows_cut(part, 0, total)
+        if side:
+            store_cols_cut(part, d_cols.shape[1], mm_tn(side[0][...], left)[:16])
+
+
+def mix_weights(first, normed, halo, d_cols, d_halo, *side):
+    tokens, wide = normed.shape
+    rows = d_cols.shape[1] + 16 * len(side)
+    operands = [normed, halo, d_cols, d_halo, *side]
+    return call(
+        functools.partial(mix_weights_kernel, first), "mix_weights", [shaped((4, rows, LANES), BF)] * 2,
+        operands, flops=2 * tokens * wide * rows,
+    )
+
+
+def unproject_kernel(
+    d_kq, d_v, tail, following, d_outgate, d_small, q_w, k_w, v_w, gate_w, beta_w, decay_w, give, keep,
+    joined, side_w,
+):
+    tokens, width = joined.shape
+    wide_q, wide_k = q_w.shape[1], k_w.shape[1]
+    joined[:, 0:wide_q] = d_kq[:, wide_k:]
+    joined[:, wide_q : wide_q + wide_k] = d_kq[:, :wide_k]
+    joined[:, wide_q + wide_k :] = d_v[...]
+    joined[tokens - 16 :, :] = jnp.concatenate([tail[0:8, :], tail[8:16, :] + following[...]], axis=0).astype(BF)
+    gather_side(side_w, beta_w, decay_w)
+    for own, part in ((False, give), (True, keep)):
+        rows = half_rows(joined, own)
+        total = mm_nt(d_outgate[rows, :], gate_w[...]) + mm(d_small[rows, :], side_w[...])
+        at = 0
+        for weight in (q_w, k_w, v_w):
+            total += mm_nt(joined[rows, at : at + weight.shape[1]], weight[...])
+            at += weight.shape[1]
+        part[...] = total.astype(part.dtype)
+
+
+def unproject(d_kq, d_v, tail, following, d_outgate, d_small, q_w, k_w, v_w, gate_w, beta_w, decay_w):
+    tokens = d_v.shape[0]
+    wide, width = q_w.shape[0], tail.shape[1]
+    half = (tokens // 2, wide)
+    operands = [d_kq, d_v, tail, following, d_outgate, d_small, q_w, k_w, v_w, gate_w, beta_w, decay_w]
+    return call(
+        unproject_kernel, "unproject", [shaped(half, BF), shaped(half, F32)], operands,
+        scratch=[VMEM((tokens, width), BF), VMEM((LANES, wide), F32)],
+        flops=2 * tokens * (width + 384) * wide,
+    )
+
+
+def fold_kernel(stage, keep, got, *outs):
+    if len(outs) == 1:
+        outs[0][...] = (keep[...].astype(F32) + got[...].astype(F32)).astype(BF)
+        return
+    mine = seq_bits()[stage]
+    half = keep.shape[0] // 2
+    for own, out in ((False, outs[0]), (True, outs[1])):
+        at = (mine if own else 1 - mine) * half
+        for k in range(half):
+            out[k] = (keep[at + k].astype(F32) + got[at + k].astype(F32)).astype(BF)
+
+
+def fold(stage, keep, got):
+    count, rows, lanes = keep.shape
+    outs = [shaped((count // 2, rows, lanes), BF)] * 2 if stage else [shaped(keep.shape, BF)]
+    return call(functools.partial(fold_kernel, stage), "fold", outs, [keep, got])
+
+
+class Line:
+    def __init__(self):
+        self.last = None
+
+    def after(self, *arrays):
+        if self.last is None:
+            return arrays
+        return lax.optimization_barrier((*arrays, self.last))[:-1]
+
+    def step(self, function, *arrays):
+        result = function(*self.after(*arrays))
+        self.last = jax.tree.leaves(result)[0]
+        return result
+
+
+class Sum:
+    def __init__(self, line, order, give, keep):
+        self.line, self.order, self.keep, self.at = line, order, keep, 0
+        self.got = swapped(give, "seq", PARTNER[order[0]])
+
+    def next(self):
+        stages = len(self.order)
+        self.at += 1
+        if self.at < stages:
+            give, self.keep = self.line.step(
+                functools.partial(fold, self.order[self.at]), self.keep, self.got
+            )
+            self.got = swapped(give, "seq", PARTNER[self.order[self.at]])
+            return
+        if self.at == stages:
+            (mine,) = self.line.step(functools.partial(fold, None), self.keep, self.got)
+            bit = 8
+            while bit < lax.axis_size("seq"):
+                mine = (mine.astype(F32) + swapped(mine, "seq", bit).astype(F32)).astype(BF)
+                bit *= 2
+        else:
+            mine = self.line.step(lambda *parts: jnp.concatenate(parts, axis=0), self.keep, self.got)
+        self.keep = mine
+        self.got = swapped(mine, "seq", PARTNER[self.order[2 * stages - 1 - self.at]])
+
+    def finish(self, kernel, name, outs):
+        return self.line.step(
+            lambda *parts: call(functools.partial(kernel, self.order), name, outs, list(parts)), self.keep, self.got
+        )
+
+
+def blocks_of(order, mine, other):
+    bits = seq_bits()
+    first, second, third = (bits[stage] for stage in order)
+    for flip, ref in ((0, mine), (1, other)):
+        for slot in range(4):
+            yield 4 * (first ^ flip) + 2 * (second ^ (slot // 2)) + (third ^ (slot % 2)), ref, slot
+
+
+def at_block(index):
+    return pl.ds(pl.multiple_of(index * LANES, LANES), LANES)
+
+
+def load_rows_cut(ref, slot, at, count):
+    return [ref[slot, at + i * LANES : at + (i + 1) * LANES, :].astype(F32) for i in range(count)]
+
+
+def gate_out_kernel(order, mine, other, outgate, out):
+    for index, ref, slot in blocks_of(order, mine, other):
+        width = outgate.shape[1]
+        for i, piece in enumerate(load_rows_cut(ref, slot, 0, width // LANES)):
+            outgate[at_block(index), i * LANES : (i + 1) * LANES] = piece
+        out[:, at_block(index)] = ref[slot, width : width + out.shape[0], :].astype(F32)
+
+
+def mix_out_kernel(side, order, mine, other, *outs):
+    wide = outs if not side else outs[:-2]
+    for index, ref, slot in blocks_of(order, mine, other):
+        at = 0
+        for out in wide:
+            for i, piece in enumerate(load_rows_cut(ref, slot, at, out.shape[1] // LANES)):
+                out[at_block(index), i * LANES : (i + 1) * LANES] = piece
+            at += out.shape[1]
+        if side:
+            pieces = ref[slot, at : at + 16, :].astype(F32)
+            at = 0
+            for part in outs[-2:]:
+                part[:, at_block(index)] = pieces[at : at + part.shape[0], :]
+                at += part.shape[0]
 
 
 def shifted(value, axis, steps):
@@ -659,41 +1045,22 @@
     return lax.ppermute(value, axis, [(s, s ^ bit) for s in range(lax.axis_size(axis))])
 
 
-def head_sum(part):
-    count = lax.axis_size("head")
-    low = lax.axis_index("head") % 2
-    half = part.shape[0] // 2
-    keep = lax.dynamic_slice_in_dim(part, low * half, half, 0)
-    give = lax.dynamic_slice_in_dim(part, (1 - low) * half, half, 0)
-    total = keep.astype(F32) + swapped(give, "head", 1).astype(F32)
-    bit = 2
-    while bit < count:
-        sent = total.astype(BF)
-        total = sent.astype(F32) + swapped(sent, "head", bit).astype(F32)
+def head_sum(give, keep):
+    total = keep + swapped(give, "head", 1).astype(F32)
+    mine = total.astype(BF)
+    other = swapped(mine, "head", 2)
+    bit = 4
+    while bit < lax.axis_size("head"):
+        mine = (mine.astype(F32) + other.astype(F32)).astype(BF)
+        other = swapped(mine, "head", bit)
         bit *= 2
-    return total
+    return mine, other
 
 
 def both_halves(mine):
     low = lax.axis_index("head") % 2
     other = swapped(mine, "head", 1)
     return jnp.concatenate([jnp.where(low == 0, mine, other), jnp.where(low == 0, other, mine)], axis=0)
-
-
-def dot_plain(left, right):
-    return jnp.dot(left, right, preferred_element_type=F32)
-
-
-def dot_rows(left, right):
-    return lax.dot_general(left, right, (((1,), (1,)), ((), ())), preferred_element_type=F32)
-
-
-def dot_cols(left, right):
-    return lax.dot_general(left, right, (((0,), (0,)), ((), ())), preferred_element_type=F32)
-
-
-def rms_norm(values, gain):
-    return values * lax.rsqrt(jnp.mean(values * values, axis=-1, keepdims=True) + EPSILON) * gain
 
 
 def reach_of(tokens, count):
@@ -714,100 +1081,115 @@
     width = width_q + 2 * width_k
     betas = beta_weight.shape[1]
     reach = reach_of(tokens, lax.axis_size("seq"))
-    x_float = block_in.astype(F32)
-    normed_float, attn_norm_back = jax.vjp(rms_norm, x_float, attn_gain)
-    normed = normed_float.astype(BF)
-    mix_weight = jnp.concatenate([q_weight, k_weight, v_weight], axis=1)
-    small_weight = jnp.concatenate(
-        [beta_weight, decay_weight, jnp.zeros((beta_weight.shape[0], LANES - betas - heads), BF)], axis=1
-    )
-    projected = dot_plain(normed, mix_weight).astype(BF)
-    small = dot_plain(normed, small_weight)
-    outgate = dot_plain(normed, outgate_weight)
-    halo = shifted(projected[tokens - 16 :], "seq", 1)
+    wide = block_in.shape[1]
+    units = gate_weight.shape[1]
+    beta_rows, decay_rows = beta_weight.T, decay_weight.T
+    normed, projected, outgate, small, edge = project(
+        block_in, attn_gain, q_weight, k_weight, v_weight, outgate_weight, beta_rows, decay_rows
+    )
+    halo = shifted(edge, "seq", 1)
+    halo, normed_halo = halo[:, :width], halo[:, width:]
     mixer_args = (seq_start, a_log, dt_bias, projected, halo, conv_q, conv_k, conv_v, small)
     prepared = mixer_prep(*mixer_args)
     out_aug, saved, final_state, final_map = prepared[0], prepared[1:13], prepared[13], prepared[14]
     pair = jnp.stack([final_state, final_map])
     before = [shifted(pair, "seq", r) for r in range(1, reach)] + [shifted(final_state[None], "seq", reach)]
     later = [shifted(final_map, "seq", -r) for r in range(1, reach)]
-    mixed, branch, partial, state_in = attend(out_aug, outgate, o_gain, out_weight, before)
-    attention_out = both_halves(head_sum(partial))
-    hidden = x_float + attention_out
-    normed_mlp_float, mlp_norm_back = jax.vjp(rms_norm, hidden, mlp_gain)
-    normed_mlp = normed_mlp_float.astype(BF)
-    gate = dot_plain(normed_mlp, gate_weight)
-    up = dot_plain(normed_mlp, up_weight)
-
-    def swiglu(gate, up):
-        return jax.nn.silu(gate) * up
-
-    inner_float, swiglu_back = jax.vjp(swiglu, gate, up)
-    inner = inner_float.astype(BF)
-    grad_inner = dot_rows(out_grad, down_weight)
-    grad_gate, grad_up = swiglu_back(grad_inner)
-    grad_gate = grad_gate.astype(BF)
-    grad_up = grad_up.astype(BF)
-    part_mlp = dot_rows(grad_gate, gate_weight) + dot_rows(grad_up, up_weight)
-    grad_normed_mlp = both_halves(head_sum(part_mlp))
-    grad_hidden_norm, grad_mlp_gain = mlp_norm_back(grad_normed_mlp)
-    grad_hidden = out_grad.astype(F32) + grad_hidden_norm
-    attention_gradient = grad_hidden.astype(BF)
-    grad_mixed, grad_outgate, grad_o_part, carry = attend_back(
-        attention_gradient, out_weight, mixed, outgate, o_gain, out_aug
+    mixed, branch, give, keep, state_in = attend(out_aug, outgate, o_gain, out_weight, before)
+    hidden, normed_own = enter(block_in, *head_sum(give, keep), mlp_gain)
+    normed_mlp, d_gate, d_up, inner, part_give, part_keep, feed_give, feed_keep = feed(
+        normed_own, swapped(normed_own, "head", 1), gate_weight.T, up_weight.T, down_weight, out_grad
+    )
+    line = Line()
+    part_mine, part_other = head_sum(part_give, part_keep)
+    line.last = part_mine
+    feed_grads = line.step(feed_weights, normed_mlp, d_gate, d_up, inner, out_grad)
+    feed_sums = lax.psum(feed_grads, "seq")
+    d_hidden, attention_own, grad_mlp_gain = line.step(leave, part_mine, part_other, hidden, mlp_gain, out_grad)
+    attention_gradient, grad_mixed, grad_outgate, grad_o_part, carry = line.step(
+        attend_back, attention_own, swapped(attention_own, "head", 1), out_weight, mixed, outgate, o_gain, out_aug
     )
     after = [shifted(carry, "seq", -r) for r in range(1, reach + 1)]
-    feed_out = both_halves(head_sum(dot_plain(inner, down_weight)))
-    output = (hidden + feed_out).astype(BF)
-    early = lax.psum(
-        (
-            dot_cols(branch, attention_gradient).astype(BF),
-            dot_cols(normed_mlp, grad_gate).astype(BF),
-            dot_cols(normed_mlp, grad_up).astype(BF),
-            dot_cols(inner, out_grad).astype(BF),
-        ),
-        "seq",
-    )
-    grad_proj, tail, lead_rows, grad_small, grad_taps, grad_scalars = mixer_back(
-        *mixer_args, saved, state_in, grad_mixed, after, later
-    )
-    following = jnp.concatenate([jnp.zeros((8, width), F32), shifted(lead_rows, "seq", -1)], axis=0)
-    kernel = jnp.concatenate([conv_q, conv_k, conv_v], axis=1)
-    taps = kernel.shape[0]
-    position = lax.axis_index("seq") * tokens + tokens - 8 + jnp.arange(8, dtype=jnp.int32)
-    for lag in range(1, taps):
-        kept = documents_at(seq_start, position + lag) == documents_at(seq_start, position)
-        tail = tail + kernel[taps - 1 - lag] * following[lag : lag + 8] * kept.astype(F32)[:, None]
-    grad_proj = jnp.concatenate([grad_proj[: tokens - 8], tail.astype(BF)], axis=0)
-    part_attn = (
-        dot_rows(grad_proj, mix_weight) + dot_rows(grad_outgate, outgate_weight) + dot_rows(grad_small, small_weight)
-    )
-    grad_normed = both_halves(head_sum(part_attn))
-    grad_x_norm, grad_attn_gain = attn_norm_back(grad_normed)
-    grad_input = (grad_hidden + grad_x_norm).astype(BF)
-    grad_mix_w, grad_outgate_w, grad_small_w = lax.psum(
-        (
-            dot_cols(normed, grad_proj).astype(BF),
-            dot_cols(normed, grad_outgate).astype(BF),
-            dot_cols(normed, grad_small),
-        ),
-        "seq",
-    )
-    grad_attn_gain, grad_mlp_gain, grad_taps, grad_scalars = lax.psum(
-        (grad_attn_gain, grad_mlp_gain, grad_taps[:taps], grad_scalars), "seq"
-    )
-    grad_o_gain = lax.psum(grad_o_part, ("seq", "head"))[0]
-    grad_out_w, grad_gate_w, grad_up_w, grad_down_w = (a.astype(F32) for a in early)
-    grad_mix_w = grad_mix_w.astype(F32)
-    q_cols, k_cols, v_cols = slice(0, width_q), slice(width_q, width_q + width_k), slice(width_q + width_k, width)
+    sum_out = Sum(line, X_FIRST, *line.step(gate_weights, normed, grad_outgate, branch, attention_gradient))
+    feed_mine, feed_other = head_sum(feed_give, feed_keep)
+    output = both_halves((hidden + feed_mine.astype(F32) + feed_other.astype(F32)).astype(BF))
+    d_kq, d_v, tail, d_halo, grad_small, grad_taps, grad_scalars = line.step(
+        lambda d_mixed: mixer_back(*mixer_args, saved, state_in, d_mixed, after, later), grad_mixed
+    )
+    following = shifted(d_halo, "seq", -1)
+    cut_q, cut_k, cut_v = slice(0, width_q), slice(width_q, width_q + width_k), slice(width_q + width_k, width)
+    halo_kq = jnp.concatenate([d_halo[:, cut_k], d_halo[:, cut_q]], axis=1)
+    sum_kq = Sum(
+        line, X_FIRST, *line.step(functools.partial(mix_weights, X_FIRST[0]), normed, normed_halo, d_kq, halo_kq)
+    )
+    sum_v = Sum(
+        line, Z_FIRST,
+        *line.step(functools.partial(mix_weights, Z_FIRST[0]), normed, normed_halo, d_v, d_halo[:, cut_v], grad_small),
+    )
+    mine, other = head_sum(
+        *line.step(
+            unproject, d_kq, d_v, tail, following, grad_outgate, grad_small,
+            q_weight, k_weight, v_weight, outgate_weight, beta_rows, decay_rows,
+        )
+    )
+    taps = conv_q.shape[0]
+
+    def padded(*rows):
+        joined = jnp.concatenate(rows, axis=1)
+        return jnp.pad(joined, ((0, 0), (0, width - joined.shape[1])))
+
+    for part in (sum_out, sum_kq, sum_v):
+        part.next()
+    for part in (sum_out, sum_kq, sum_v):
+        part.next()
+    line.last = feed_sums
+    input_own, grad_attn_gain = line.step(finish, mine, other, block_in, attn_gain, d_hidden)
+    grad_input = both_halves(input_own)
+    small_sums = jnp.concatenate(
+        [
+            grad_taps[:taps], padded(grad_scalars[0:1], grad_scalars[1:2]),
+            padded(grad_attn_gain), padded(grad_mlp_gain), padded(grad_o_part),
+        ],
+        axis=0,
+    )
+    small_got = swapped(small_sums, "seq", 1)
+    bit = 2
+    rounds = 3
+    while small_got is not None or rounds > 0:
+        for part in (sum_out, sum_kq, sum_v) if rounds > 0 else ():
+            part.next()
+        rounds -= 1
+        if small_got is not None:
+            small_sums = line.step(jnp.add, small_sums, small_got)
+            small_got = swapped(small_sums, "seq", bit) if bit < lax.axis_size("seq") else None
+            bit *= 2
+    gains = small_sums[taps + 1 : taps + 4]
+    gains = gains + swapped(gains, "head", 1)
+    grad_o_gain = gains[2:3, :LANES]
+    bit = 2
+    while bit < lax.axis_size("head"):
+        grad_o_gain = grad_o_gain + swapped(grad_o_gain, "head", bit)
+        bit *= 2
+    grad_outgate_w, grad_out_w = sum_out.finish(
+        gate_out_kernel, "gate_out", [shaped((wide, width_q), F32), shaped((width_q, wide), F32)]
+    )
+    grad_v_w, grad_beta_w, grad_decay_w = sum_v.finish(
+        functools.partial(mix_out_kernel, True), "mix_out",
+        [shaped((wide, width_k), F32), shaped((betas, wide), F32), shaped((heads, wide), F32)],
+    )
+    grad_k_w, grad_q_w = sum_kq.finish(
+        functools.partial(mix_out_kernel, False), "mix_out",
+        [shaped((wide, width_k), F32), shaped((wide, width_q), F32)],
+    )
+    grad_gate_w, grad_up_w, grad_down_w = (
+        feed_sums[k * units : (k + 1) * units].astype(F32) for k in range(3)
+    )
+    rate, shift = small_sums[taps, betas : betas + heads], small_sums[taps, LANES + betas : LANES + betas + heads]
     return (
-        output, grad_input, grad_attn_gain,
-        grad_mix_w[:, q_cols], grad_mix_w[:, k_cols], grad_mix_w[:, v_cols],
-        grad_taps[:, q_cols], grad_taps[:, k_cols], grad_taps[:, v_cols],
-        grad_small_w[:, :betas], grad_small_w[:, betas : betas + heads],
-        grad_scalars[0, betas : betas + heads], grad_scalars[1, betas : betas + heads],
-        grad_outgate_w.astype(F32), grad_o_gain, grad_out_w, grad_mlp_gain,
-        grad_gate_w, grad_up_w, grad_down_w,
+        output, grad_input, gains[0, :wide], grad_q_w, grad_k_w, grad_v_w,
+        small_sums[:taps, cut_q], small_sums[:taps, cut_k], small_sums[:taps, cut_v],
+        grad_beta_w.T, grad_decay_w.T, rate, shift, grad_outgate_w, grad_o_gain[0], grad_out_w, gains[1, :wide],
+        grad_gate_w.T, grad_up_w.T, grad_down_w,
     )
 
 

time: 562 us -> 374 us (0.67)
  waiting for transfers between devices: 277 us -> 173 us
  blocking collectives: 78.9 us -> 0 us
  matrix products: 30.4 us -> 0 us
  starting transfers between devices: 31.8 us -> 61.8 us
  other arithmetic: 39.3 us -> 14.2 us
  Pallas kernels: 59.2 us -> 76.9 us
    psum x2 -> x1, waiting for transfers between devices: 225 us -> 43 us  [local(): feed_sums = lax.psum(feed_grads, 'seq')]
    psum x2 -> x0, blocking collectives: 78.9 us -> none  [the longest x1 41 us: local(): grad_o_gain = lax.psum(grad_o_part, ('seq', 'head'))[0]]
    ppermute x12 -> x35, waiting for transfers between devices: 43 us -> 97.1 us  [swapped(): lax.ppermute(value, axis, [(s, s ^ bit) for s in range(lax.axis_size(axis...]
    dot_general x19 -> x0, matrix products: 30.4 us -> none  [the longest x7 15.2 us: dot_cols(): lax.dot_general(left, right, (((0,), (0,)), ((), ())), preferred_element_...]
    ppermute x12 -> x35, starting transfers between devices: 5.31 us -> 35.2 us  [swapped(): lax.ppermute(value, axis, [(s, s ^ bit) for s in range(lax.axis_size(axis...]
    pallas_call x2 -> x24, Pallas kernels: 7.77 us -> 33.7 us  [call(): pl.pallas_call(kernel, out_shape=outs, in_specs=specs(smem, pltpu.SMEM) +...]
    ppermute x10, waiting for transfers between devices: 8.62 us -> 32.6 us  [shifted(): lax.ppermute(value, axis, [(source, source + steps) for source in range(l...]
    convert_element_type x15 -> x6, other arithmetic: 30 us -> 9.56 us  [the longest x1 6.07 us: local(): feed_sums[k * units:(k + 1) * units].astype(F32)]
  transfers between devices with their start and end apart: 24 -> 46, of which waited for: 13 -> 23; matrix products, arithmetic and copies ran while one was open for 10% -> 5% of each run, Pallas kernels for 1% -> 13%
where the time goes in v2:
time: 374 us; the launch traced here: 373 us
  waiting for transfers between devices  173 us (46%)
  Pallas kernels  76.9 us (21%)
  starting transfers between devices  61.8 us (17%)
  local copies, waits for them, and re-layouts  31.8 us (9%)
  between operations  15.4 us (4%)
  other arithmetic  14.2 us (4%)
    ppermute x35, waiting for transfers between devices, swapped(): lax.ppermute(value, axis, [(s, s ^ bit) for s in range(lax.axis_size(axis...  97.1 us
    psum x1, waiting for transfers between devices, local(): feed_sums = lax.psum(feed_grads, 'seq')  43 us
    ppermute x35, starting transfers between devices, swapped(): lax.ppermute(value, axis, [(s, s ^ bit) for s in range(lax.axis_size(axis...  35.2 us
    pallas_call x24, Pallas kernels, call(): pl.pallas_call(kernel, out_shape=outs, in_specs=specs(smem, pltpu.SMEM) +...  33.7 us
    ppermute x10, waiting for transfers between devices, shifted(): lax.ppermute(value, axis, [(source, source + steps) for source in range(l...  32.6 us
    ppermute x10, starting transfers between devices, shifted(): lax.ppermute(value, axis, [(source, source + steps) for source in range(l...  26.6 us
    unnamed x194, local copies, waits for them, and re-layouts  25.8 us
    pallas_call x1, Pallas kernels, mixer_back(): pl.pallas_call(functools.partial(back_kernel, heads, reach), out_shape=ou...  24.5 us
  transfers between devices with their start and end apart: 46, of which 23 were waited for; matrix products, arithmetic and copies ran while one was open for 5% of the time, Pallas kernels for 13%

profile of v2, /device:TPU:0, one launch (start us, length us, event | category | flops | bytes accessed | tf_op | source)
XLA Modules:
  0.0 372.8 jit_solution(6765353120562954677)
XLA Ops:
  15.1 2.3 project.1
  17.4 4.8 %collective-permute-start = (bf16[16,2304]{1,0:T(8,128)(2,1)S(1)}, bf16[16,2304]{1,0:T(8,128)(2,1)S(1)}, u32[]{:S(2)}, u32[]{:S(2)}) collective-permute-start(bf16[16,2304]{1,0:T(8,128)(2,1)S(1)} %get-tuple-element.190), channel_id=1, source_target_pairs={{0,4},{4,8},{8,12},{12,16},{16,20},{20,24},{24,28},{1,5},{5,9},{9,... | collective-permute-start | bytes 221192 | tf_op jit(solution)/shard_map/ppermute | solution.py:1041
  24.3 18.6 %mixer_prep.1 = (f32[2,512,256]{2,1,0:T(8,128)S(1)}, bf16[2,8,128,256]{3,2,1,0:T(8,128)(2,1)S(1)}, bf16[2,8,128,128]{3,2,1,0:T(8,128)(2,1)S(1)}, bf16[2,8,128,12...) custom-call(s32[10]{0:T(128)S(1)} %copy-done.84, ...), custom_call_target="tpu_custom_call" | custom-call | flops 2000000000 | bytes 4000000 | tf_op jit(solution)/shard_map/mixer_prep/pallas_call | solution.py:283
  49.1 4.3 %collective-permute-start.1 = (bf16[2,2,128,128]{3,2,1,0:T(8,128)(2,1)S(1)}, bf16[2,2,128,128]{3,2,1,0:T(8,128)(2,1)S(1)}, u32[]{:S(2)}, u32[]{:S(2)}) collective-permute-start(bf16[2,2,128,128]{3,2,1,0:T(8,128)(2,1)S(1)} %pad_maximum_fusion.2), channel_id=1, source_target_pairs={{0,4},{4,8},{8,12},{12,16},{16,20},{20,24},{24,28},{1,5},{5,9},{9,... | collective-permute-start | bytes 393224 | tf_op jit(solution)/shard_map/ppermute | solution.py:1041
  53.4 3.5 collective-permute-start.2
  56.9 5.5 %collective-permute-start.3 = (bf16[1,2,128,128]{3,2,1,0:T(8,128)(2,1)S(1)}, bf16[1,2,128,128]{3,2,1,0:T(8,128)(2,1)S(1)}, u32[]{:S(2)}, u32[]{:S(2)}) collective-permute-start(bf16[1,2,128,128]{3,2,1,0:T(8,128)(2,1)S(1)} %bitcast.30), channel_id=1, source_target_pairs={{0,12},{4,16},{8,20},{12,24},{16,28},{1,13},{5,17},{9,21},{13,25},... | collective-permute-start | bytes 196616 | tf_op jit(solution)/shard_map/ppermute | solution.py:1041
  69.1 12.4 %collective-permute-done.5.other = bf16[256,1024]{1,0:T(8,128)(2,1)S(1)} collective-permute-done((bf16[256,1024]{1,0:T(8,128)(2,1)S(1)}, bf16[256,1024]{1,0:T(8,128)(2,1)S(1)}, u32[]{:S(2)}, u32[]{:S(2)}) %collective-permute-start.5) | collective-permute-done | bytes 524320 | tf_op jit(solution)/shard_map/ppermute | solution.py:1045
  84.9 5.2 %feed.1 = (bf16[512,1024]{1,0:T(8,128)(2,1)S(1)}, bf16[512,704]{1,0:T(8,128)(2,1)S(1)}, bf16[512,704]{1,0:T(8,128)(2,1)S(1)}, bf16[512,704]{1,0:T(8,128)(2,1)S(1...) custom-call(bf16[256,1024]{1,0:T(8,128)(2,1)S(1)} %get-tuple-element, ...), custom_call_target="tpu_custom_call" | custom-call | flops 276824064 | bytes 798720 | tf_op jit(solution)/shard_map/feed/pallas_call | solution.py:593
  94.6 2.4 feed_weights.1
  97.0 2.1 copy-done
  99.1 8.2 %collective-permute-done.11.other = bf16[256,1024]{1,0:T(8,128)(2,1)} collective-permute-done((bf16[256,1024]{1,0:T(8,128)(2,1)}, bf16[256,1024]{1,0:T(8,128)(2,1)}, u32[]{:S(2)}, u32[]{:S(2)}) %collective-permute-start.11) | collective-permute-done | bytes 524320 | tf_op jit(solution)/shard_map/ppermute | solution.py:1045
  121.5 4.7 %collective-permute-done.8 = bf16[256,1024]{1,0:T(8,128)(2,1)S(1)} collective-permute-done((bf16[256,1024]{1,0:T(8,128)(2,1)S(1)}, bf16[256,1024]{1,0:T(8,128)(2,1)S(1)}, u32[]{:S(2)}, u32[]{:S(2)}) %collective-permute-start.8) | collective-permute-done | bytes 524320 | tf_op jit(solution)/shard_map/ppermute | solution.py:1045
  131.0 5.5 %collective-permute-done.14.rest_1_ = bf16[2,128,128]{2,1,0:T(8,128)(2,1)S(1)} collective-permute-done((bf16[2,128,128]{2,1,0:T(8,128)(2,1)S(1)}, bf16[2,128,128]{2,1,0:T(8,128)(2,1)S(1)}, u32[]{:S(2)}, u32[]{:S(2)}) %collective-permute-start.14) | collective-permute-done | bytes 65568 | tf_op jit(solution)/shard_map/ppermute | solution.py:1041
  138.3 24.5 %mixer_back.1 = (bf16[512,768]{1,0:T(8,128)(2,1)S(1)}, bf16[512,512]{1,0:T(8,128)(2,1)S(1)}, f32[16,1280]{1,0:T(8,128)S(1)}, f32[8,1280]{1,0:T(8,128)S(1)}, bf16...) custom-call(s32[10]{0:T(128)S(1)} %copy-done.85, f32[2]{0:T(128)S(1)} %copy-done.87, ...), custom_call_target="tpu_custom_call" | custom-call | flops 2000000000 | bytes 4000000 | tf_op jit(solution)/shard_map/mixer_back/pallas_call | solution.py:568
  162.9 2.3 mix_weights.2
  165.2 9.7 %collective-permute-start.24 = (bf16[4,768,128]{2,1,0:T(8,128)(2,1)}, bf16[4,768,128]{2,1,0:T(8,128)(2,1)}, u32[]{:S(2)}, u32[]{:S(2)}) collective-permute-start(bf16[4,768,128]{2,1,0:T(8,128)(2,1)} %get-tuple-element.262), channel_id=1, source_target_pairs={{0,4},{4,0},{8,12},{12,8},{16,20},{20,16},{24,28},{28,24},{1,5},{5... | collective-permute-start | bytes 2359304 | tf_op jit(solution)/shard_map/ppermute | solution.py:1045
  176.4 2.7 collective-permute-start.25
  180.3 21.8 %collective-permute-done.18.following = f32[8,1280]{1,0:T(8,128)S(1)} collective-permute-done((f32[8,1280]{1,0:T(8,128)S(1)}, f32[8,1280]{1,0:T(8,128)S(1)}, u32[]{:S(2)}, u32[]{:S(2)}) %collective-permute-start.18) | collective-permute-done | bytes 40992 | tf_op jit(solution)/shard_map/ppermute | solution.py:1041
  202.2 2.1 unproject.1
  206.3 9.3 %collective-permute-done.25.got = bf16[4,512,128]{2,1,0:T(8,128)(2,1)} collective-permute-done((bf16[4,512,128]{2,1,0:T(8,128)(2,1)}, bf16[4,512,128]{2,1,0:T(8,128)(2,1)}, u32[]{:S(2)}, u32[]{:S(2)}) %collective-permute-start.25) | collective-permute-done | bytes 524320 | tf_op jit(solution)/shard_map/ppermute | solution.py:1045
  219.2 2.0 collective-permute-start.27
  222.5 9.3 %collective-permute-done.23.got = bf16[4,528,128]{2,1,0:T(8,128)(2,1)S(1)} collective-permute-done((bf16[4,528,128]{2,1,0:T(8,128)(2,1)}, bf16[4,528,128]{2,1,0:T(8,128)(2,1)S(1)}, u32[]{:S(2)}, u32[]{:S(2)}) %collective-permute-start.23) | collective-permute-done | bytes 540704 | tf_op jit(solution)/shard_map/ppermute | solution.py:1045
  234.3 3.1 collective-permute-done.28.got
  238.8 22.4 %collective-permute-done.27.got = bf16[2,768,128]{2,1,0:T(8,128)(2,1)S(1)} collective-permute-done((bf16[2,768,128]{2,1,0:T(8,128)(2,1)S(1)}, bf16[2,768,128]{2,1,0:T(8,128)(2,1)S(1)}, u32[]{:S(2)}, u32[]{:S(2)}) %collective-permute-start.27) | collective-permute-done | bytes 393248 | tf_op jit(solution)/shard_map/ppermute | solution.py:1045
  264.7 43.0 %all-reduce.6.cloned.1.call-done = bf16[2112,1024]{1,0:T(8,128)(2,1)} async-done(((bf16[2112,1024]{1,0:T(8,128)(2,1)}), bf16[2112,1024]{1,0:T(8,128)(2,1)}) %all-reduce.6.cloned.1.call-update) | async-done | bytes 4325392 | tf_op jit(solution)/shard_map/psum | solution.py:1107
  312.8 2.4 collective-permute-start.35
  320.1 6.1 %slice_convert_fusion = (f32[704,1024]{1,0:T(8,128)}, f32[1024,704]{0,1:T(8,128)}, f32[1024,704]{0,1:T(8,128)}) fusion(bf16[2112,1024]{1,0:T(8,128)(2,1)} %all-reduce.6.cloned.1.call-done), kind=kLoop, calls=%fused_computation.2 | loop fusion | flops 2162688 | bytes 12976128 | tf_op jit(solution)/shard_map/convert_element_type | solution.py:1185
  326.3 2.1 collective-permute-start.39
  332.2 4.6 %collective-permute-done.39 = bf16[2,512,128]{2,1,0:T(8,128)(2,1)S(1)} collective-permute-done((bf16[2,512,128]{2,1,0:T(8,128)(2,1)S(1)}, bf16[2,512,128]{2,1,0:T(8,128)(2,1)S(1)}, u32[]{:S(2)}, u32[]{:S(2)}) %collective-permute-start.39) | collective-permute-done | bytes 262176 | tf_op jit(solution)/shard_map/ppermute | solution.py:1045
  338.7 9.8 %collective-permute-done.38 = bf16[2,768,128]{2,1,0:T(8,128)(2,1)S(1)} collective-permute-done((bf16[2,768,128]{2,1,0:T(8,128)(2,1)S(1)}, bf16[2,768,128]{2,1,0:T(8,128)(2,1)S(1)}, u32[]{:S(2)}, u32[]{:S(2)}) %collective-permute-start.38) | collective-permute-done | bytes 393248 | tf_op jit(solution)/shard_map/ppermute | solution.py:1045
  357.5 4.5 %collective-permute-done.42.other = bf16[4,528,128]{2,1,0:T(8,128)(2,1)S(1)} collective-permute-done((bf16[4,528,128]{2,1,0:T(8,128)(2,1)S(1)}, bf16[4,528,128]{2,1,0:T(8,128)(2,1)S(1)}, u32[]{:S(2)}, u32[]{:S(2)}) %collective-permute-start.42) | collective-permute-done | bytes 540704 | tf_op jit(solution)/shard_map/ppermute | solution.py:1045
  364.0 2.0 mix_out.3
  (321 shorter events, 94.1 us)
Async XLA Ops:
  7.2 300.5 %all-reduce.6.cloned.1.call-start = ((), (), s32[]{:S(2)}) async-start(), calls=%async_computation | async-start | bytes 8650752 | tf_op jit(solution)/shard_map/psum | solution.py:1107
  49.1 15.0 %collective-permute-start.1 = (bf16[2,2,128,128]{3,2,1,0:T(8,128)(2,1)S(1)}, bf16[2,2,128,128]{3,2,1,0:T(8,128)(2,1)S(1)}, u32[]{:S(2)}, u32[]{:S(2)}) collective-permute-start(bf16[2,2,128,128]{3,2,1,0:T(8,128)(2,1)S(1)} %pad_maximum_fusion.2), channel_id=1, source_target_pairs={{0,4},{4,8},{8,12},{12,16},{16,20},{20,24},{24,28},{1,5},{5,9},{9,... | collective-permute-start | bytes 393224 | tf_op jit(solution)/shard_map/ppermute | solution.py:1041
  67.6 14.0 %collective-permute-start.5 = (bf16[256,1024]{1,0:T(8,128)(2,1)S(1)}, bf16[256,1024]{1,0:T(8,128)(2,1)S(1)}, u32[]{:S(2)}, u32[]{:S(2)}) collective-permute-start(bf16[256,1024]{1,0:T(8,128)(2,1)S(1)} %add_convert_fusion.4.mine), channel_id=1, source_target_pairs={{0,2},{1,3},{2,0},{3,1},{4,6},{5,7},{6,4},{7,5},{8,10},{9,11},{10,... | collective-permute-start | bytes 1572872 | tf_op jit(solution)/shard_map/ppermute | solution.py:1045
  93.0 14.3 %collective-permute-start.11 = (bf16[256,1024]{1,0:T(8,128)(2,1)}, bf16[256,1024]{1,0:T(8,128)(2,1)}, u32[]{:S(2)}, u32[]{:S(2)}) collective-permute-start(bf16[256,1024]{1,0:T(8,128)(2,1)} %add_convert_fusion.1.mine), channel_id=1, source_target_pairs={{0,2},{1,3},{2,0},{3,1},{4,6},{5,7},{6,4},{7,5},{8,10},{9,11},{10,... | collective-permute-start | bytes 1572872 | tf_op jit(solution)/shard_map/ppermute | solution.py:1045
  112.3 13.9 %collective-permute-start.8 = (bf16[256,1024]{1,0:T(8,128)(2,1)S(1)}, bf16[256,1024]{1,0:T(8,128)(2,1)S(1)}, u32[]{:S(2)}, u32[]{:S(2)}) collective-permute-start(bf16[256,1024]{1,0:T(8,128)(2,1)S(1)} %add_convert_fusion.3), channel_id=1, source_target_pairs={{0,2},{1,3},{2,0},{3,1},{4,6},{5,7},{6,4},{7,5},{8,10},{9,11},{10,... | collective-permute-start | bytes 1572872 | tf_op jit(solution)/shard_map/ppermute | solution.py:1045
  113.9 17.1 %collective-permute-start.16 = (bf16[2,128,128]{2,1,0:T(8,128)(2,1)S(1)}, bf16[2,128,128]{2,1,0:T(8,128)(2,1)S(1)}, u32[]{:S(2)}, u32[]{:S(2)}) collective-permute-start(bf16[2,128,128]{2,1,0:T(8,128)(2,1)S(1)} %get-tuple-element.195), channel_id=1, source_target_pairs={{4,0},{8,4},{12,8},{16,12},{20,16},{24,20},{28,24},{5,1},{9,5},{13... | collective-permute-start | bytes 196616 | tf_op jit(solution)/shard_map/ppermute | solution.py:1041
  115.2 15.8 %collective-permute-start.17 = (bf16[2,128,128]{2,1,0:T(8,128)(2,1)S(1)}, bf16[2,128,128]{2,1,0:T(8,128)(2,1)S(1)}, u32[]{:S(2)}, u32[]{:S(2)}) collective-permute-start(bf16[2,128,128]{2,1,0:T(8,128)(2,1)S(1)} %get-tuple-element.195), channel_id=1, source_target_pairs={{8,0},{12,4},{16,8},{20,12},{24,16},{28,20},{9,1},{13,5},{17,9},{2... | collective-permute-start | bytes 196616 | tf_op jit(solution)/shard_map/ppermute | solution.py:1041
  118.6 12.4 %collective-permute-start.13 = (bf16[2,128,128]{2,1,0:T(8,128)(2,1)S(1)}, bf16[2,128,128]{2,1,0:T(8,128)(2,1)S(1)}, u32[]{:S(2)}, u32[]{:S(2)}) collective-permute-start(bf16[2,128,128]{2,1,0:T(8,128)(2,1)S(1)} %get-tuple-element.252), channel_id=1, source_target_pairs={{4,0},{8,4},{12,8},{16,12},{20,16},{24,20},{28,24},{5,1},{9,5},{13... | collective-permute-start | bytes 196616 | tf_op jit(solution)/shard_map/ppermute | solution.py:1041
  120.2 16.3 %collective-permute-start.14 = (bf16[2,128,128]{2,1,0:T(8,128)(2,1)S(1)}, bf16[2,128,128]{2,1,0:T(8,128)(2,1)S(1)}, u32[]{:S(2)}, u32[]{:S(2)}) collective-permute-start(bf16[2,128,128]{2,1,0:T(8,128)(2,1)S(1)} %get-tuple-element.252), channel_id=1, source_target_pairs={{8,0},{12,4},{16,8},{20,12},{24,16},{28,20},{9,1},{13,5},{17,9},{2... | collective-permute-start | bytes 196616 | tf_op jit(solution)/shard_map/ppermute | solution.py:1041
  131.0 74.0 %collective-permute-start.9 = (bf16[256,1024]{1,0:T(8,128)(2,1)}, bf16[256,1024]{1,0:T(8,128)(2,1)}, u32[]{:S(2)}, u32[]{:S(2)}) collective-permute-start(bf16[256,1024]{1,0:T(8,128)(2,1)} %add_convert_fusion.2), channel_id=1, source_target_pairs={{0,1},{1,0},{2,3},{3,2},{4,5},{5,4},{6,7},{7,6},{8,9},{9,8},{10,11... | collective-permute-start | bytes 1572872 | tf_op jit(solution)/shard_map/ppermute | solution.py:1045
  165.2 52.6 %collective-permute-start.24 = (bf16[4,768,128]{2,1,0:T(8,128)(2,1)}, bf16[4,768,128]{2,1,0:T(8,128)(2,1)}, u32[]{:S(2)}, u32[]{:S(2)}) collective-permute-start(bf16[4,768,128]{2,1,0:T(8,128)(2,1)} %get-tuple-element.262), channel_id=1, source_target_pairs={{0,4},{4,0},{8,12},{12,8},{16,20},{20,16},{24,28},{28,24},{1,5},{5... | collective-permute-start | bytes 2359304 | tf_op jit(solution)/shard_map/ppermute | solution.py:1045
  174.9 27.2 %collective-permute-start.18 = (f32[8,1280]{1,0:T(8,128)S(1)}, f32[8,1280]{1,0:T(8,128)S(1)}, u32[]{:S(2)}, u32[]{:S(2)}) collective-permute-start(f32[8,1280]{1,0:T(8,128)S(1)} %get-tuple-element.256), channel_id=1, source_target_pairs={{4,0},{8,4},{12,8},{16,12},{20,16},{24,20},{28,24},{5,1},{9,5},{13... | collective-permute-start | bytes 122888 | tf_op jit(solution)/shard_map/ppermute | solution.py:1041
  176.4 39.1 %collective-permute-start.25 = (bf16[4,512,128]{2,1,0:T(8,128)(2,1)}, bf16[4,512,128]{2,1,0:T(8,128)(2,1)}, u32[]{:S(2)}, u32[]{:S(2)}) collective-permute-start(bf16[4,512,128]{2,1,0:T(8,128)(2,1)} %get-tuple-element.250), channel_id=1, source_target_pairs={{0,4},{4,0},{8,12},{12,8},{16,20},{20,16},{24,28},{28,24},{1,5},{5... | collective-permute-start | bytes 1572872 | tf_op jit(solution)/shard_map/ppermute | solution.py:1045
  204.3 17.0 %collective-permute-start.19 = (bf16[256,1024]{1,0:T(8,128)(2,1)}, bf16[256,1024]{1,0:T(8,128)(2,1)}, u32[]{:S(2)}, u32[]{:S(2)}) collective-permute-start(bf16[256,1024]{1,0:T(8,128)(2,1)} %get-tuple-element.282), channel_id=1, source_target_pairs={{0,1},{1,0},{2,3},{3,2},{4,5},{5,4},{6,7},{7,6},{8,9},{9,8},{10,11... | collective-permute-start | bytes 1572872 | tf_op jit(solution)/shard_map/ppermute | solution.py:1045
  205.0 26.9 %collective-permute-start.23 = (bf16[4,528,128]{2,1,0:T(8,128)(2,1)}, bf16[4,528,128]{2,1,0:T(8,128)(2,1)S(1)}, u32[]{:S(2)}, u32[]{:S(2)}) collective-permute-start(bf16[4,528,128]{2,1,0:T(8,128)(2,1)} %copy-done.90), channel_id=1, source_target_pairs={{0,8},{4,12},{8,0},{12,4},{16,24},{20,28},{24,16},{28,20},{1,9},{5... | collective-permute-start | bytes 1622024 | tf_op jit(solution)/shard_map/ppermute | solution.py:1045
  217.7 19.7 %collective-permute-start.28 = (bf16[2,512,128]{2,1,0:T(8,128)(2,1)S(1)}, bf16[2,512,128]{2,1,0:T(8,128)(2,1)S(1)}, u32[]{:S(2)}, u32[]{:S(2)}) collective-permute-start(bf16[2,512,128]{2,1,0:T(8,128)(2,1)S(1)} %get-tuple-element.299), channel_id=1, source_target_pairs={{0,8},{4,12},{8,0},{12,4},{16,24},{20,28},{24,16},{28,20},{1,9},{5... | collective-permute-start | bytes 786440 | tf_op jit(solution)/shard_map/ppermute | solution.py:1045
  219.2 42.0 %collective-permute-start.27 = (bf16[2,768,128]{2,1,0:T(8,128)(2,1)S(1)}, bf16[2,768,128]{2,1,0:T(8,128)(2,1)S(1)}, u32[]{:S(2)}, u32[]{:S(2)}) collective-permute-start(bf16[2,768,128]{2,1,0:T(8,128)(2,1)S(1)} %get-tuple-element.302), channel_id=1, source_target_pairs={{0,8},{4,12},{8,0},{12,4},{16,24},{20,28},{24,16},{28,20},{1,9},{5... | collective-permute-start | bytes 1179656 | tf_op jit(solution)/shard_map/ppermute | solution.py:1045
  222.4 41.5 %collective-permute-start.20 = (bf16[256,1024]{1,0:T(8,128)(2,1)S(1)}, bf16[256,1024]{1,0:T(8,128)(2,1)S(1)}, u32[]{:S(2)}, u32[]{:S(2)}) collective-permute-start(bf16[256,1024]{1,0:T(8,128)(2,1)S(1)} %add_convert_fusion.mine), channel_id=1, source_target_pairs={{0,2},{1,3},{2,0},{3,1},{4,6},{5,7},{6,4},{7,5},{8,10},{9,11},{10,... | collective-permute-start | bytes 1572872 | tf_op jit(solution)/shard_map/ppermute | solution.py:1045
  232.0 29.9 %collective-permute-start.26 = (bf16[2,528,128]{2,1,0:T(8,128)(2,1)S(1)}, bf16[2,528,128]{2,1,0:T(8,128)(2,1)S(1)}, u32[]{:S(2)}, u32[]{:S(2)}) collective-permute-start(bf16[2,528,128]{2,1,0:T(8,128)(2,1)S(1)} %get-tuple-element.306), channel_id=1, source_target_pairs={{0,24},{4,28},{8,16},{12,20},{16,8},{20,12},{24,0},{28,4},{1,25},{... | collective-permute-start | bytes 811016 | tf_op jit(solution)/shard_map/ppermute | solution.py:1045
  238.1 72.8 %collective-permute-start.31 = (bf16[1,512,128]{2,1,0:T(8,128)(2,1)}, bf16[1,512,128]{2,1,0:T(8,128)(2,1)}, u32[]{:S(2)}, u32[]{:S(2)}) collective-permute-start(bf16[1,512,128]{2,1,0:T(8,128)(2,1)} %get-tuple-element.311), channel_id=1, source_target_pairs={{0,24},{4,28},{8,16},{12,20},{16,8},{20,12},{24,0},{28,4},{1,25},{... | collective-permute-start | bytes 393224 | tf_op jit(solution)/shard_map/ppermute | solution.py:1045
  261.9 53.2 %collective-permute-start.30 = (bf16[1,768,128]{2,1,0:T(8,128)(2,1)}, bf16[1,768,128]{2,1,0:T(8,128)(2,1)S(1)}, u32[]{:S(2)}, u32[]{:S(2)}) collective-permute-start(bf16[1,768,128]{2,1,0:T(8,128)(2,1)} %get-tuple-element.314), channel_id=1, source_target_pairs={{0,24},{4,28},{8,16},{12,20},{16,8},{20,12},{24,0},{28,4},{1,25},{... | collective-permute-start | bytes 589832 | tf_op jit(solution)/shard_map/ppermute | solution.py:1045
  263.3 53.5 %collective-permute-start.29 = (bf16[1,528,128]{2,1,0:T(8,128)(2,1)}, bf16[1,528,128]{2,1,0:T(8,128)(2,1)}, u32[]{:S(2)}, u32[]{:S(2)}) collective-permute-start(bf16[1,528,128]{2,1,0:T(8,128)(2,1)} %get-tuple-element.318), channel_id=1, source_target_pairs={{0,4},{4,0},{8,12},{12,8},{16,20},{20,16},{24,28},{28,24},{1,5},{5... | collective-permute-start | bytes 405512 | tf_op jit(solution)/shard_map/ppermute | solution.py:1045
  309.3 28.2 %collective-permute-start.21 = (bf16[256,1024]{1,0:T(8,128)(2,1)S(1)}, bf16[256,1024]{1,0:T(8,128)(2,1)S(1)}, u32[]{:S(2)}, u32[]{:S(2)}) collective-permute-start(bf16[256,1024]{1,0:T(8,128)(2,1)S(1)} %get-tuple-element.288), channel_id=1, source_target_pairs={{0,1},{1,0},{2,3},{3,2},{4,5},{5,4},{6,7},{7,6},{8,9},{9,8},{10,11... | collective-permute-start | bytes 1572872 | tf_op jit(solution)/shard_map/ppermute | solution.py:1045
  310.2 15.9 %collective-permute-start.22 = (f32[8,1280]{1,0:T(8,128)S(1)}, f32[8,1280]{1,0:T(8,128)S(1)}, u32[]{:S(2)}, u32[]{:S(2)}) collective-permute-start(f32[8,1280]{1,0:T(8,128)S(1)} %concatenate.37), channel_id=1, source_target_pairs={{0,4},{4,0},{8,12},{12,8},{16,20},{20,16},{24,28},{28,24},{1,5},{5... | collective-permute-start | bytes 122888 | tf_op jit(solution)/shard_map/ppermute | solution.py:1045
  312.8 13.5 %collective-permute-start.35 = (bf16[1,512,128]{2,1,0:T(8,128)(2,1)S(1)}, bf16[1,512,128]{2,1,0:T(8,128)(2,1)S(1)}, u32[]{:S(2)}, u32[]{:S(2)}) collective-permute-start(bf16[1,512,128]{2,1,0:T(8,128)(2,1)S(1)} %fold.15), channel_id=1, source_target_pairs={{0,24},{4,28},{8,16},{12,20},{16,8},{20,12},{24,0},{28,4},{1,25},{... | collective-permute-start | bytes 393224 | tf_op jit(solution)/shard_map/ppermute | solution.py:1045
  315.2 13.2 %collective-permute-start.34 = (bf16[1,768,128]{2,1,0:T(8,128)(2,1)S(1)}, bf16[1,768,128]{2,1,0:T(8,128)(2,1)S(1)}, u32[]{:S(2)}, u32[]{:S(2)}) collective-permute-start(bf16[1,768,128]{2,1,0:T(8,128)(2,1)S(1)} %fold.16), channel_id=1, source_target_pairs={{0,24},{4,28},{8,16},{12,20},{16,8},{20,12},{24,0},{28,4},{1,25},{... | collective-permute-start | bytes 589832 | tf_op jit(solution)/shard_map/ppermute | solution.py:1045
  328.4 20.0 %collective-permute-start.38 = (bf16[2,768,128]{2,1,0:T(8,128)(2,1)S(1)}, bf16[2,768,128]{2,1,0:T(8,128)(2,1)S(1)}, u32[]{:S(2)}, u32[]{:S(2)}) collective-permute-start(bf16[2,768,128]{2,1,0:T(8,128)(2,1)S(1)} %constant_dynamic-update-slice_fusion.2), channel_id=1, source_target_pairs={{0,8},{4,12},{8,0},{12,4},{16,24},{20,28},{24,16},{28,20},{1,9},{5... | collective-permute-start | bytes 1179656 | tf_op jit(solution)/shard_map/ppermute | solution.py:1045
  328.9 20.9 %collective-permute-start.37 = (bf16[2,528,128]{2,1,0:T(8,128)(2,1)S(1)}, bf16[2,528,128]{2,1,0:T(8,128)(2,1)S(1)}, u32[]{:S(2)}, u32[]{:S(2)}) collective-permute-start(bf16[2,528,128]{2,1,0:T(8,128)(2,1)S(1)} %constant_dynamic-update-slice_fusion.4), channel_id=1, source_target_pairs={{0,24},{4,28},{8,16},{12,20},{16,8},{20,12},{24,0},{28,4},{1,25},{... | collective-permute-start | bytes 811016 | tf_op jit(solution)/shard_map/ppermute | solution.py:1045
  330.8 19.2 %collective-permute-start.36 = (f32[8,1280]{1,0:T(8,128)S(1)}, f32[8,1280]{1,0:T(8,128)S(1)}, u32[]{:S(2)}, u32[]{:S(2)}) collective-permute-start(f32[8,1280]{1,0:T(8,128)S(1)} %add.56), channel_id=1, source_target_pairs={{0,16},{4,20},{8,24},{12,28},{16,0},{20,4},{24,8},{28,12},{1,17},{... | collective-permute-start | bytes 122888 | tf_op jit(solution)/shard_map/ppermute | solution.py:1045
  336.9 19.1 %collective-permute-start.43 = (bf16[4,512,128]{2,1,0:T(8,128)(2,1)S(1)}, bf16[4,512,128]{2,1,0:T(8,128)(2,1)S(1)}, u32[]{:S(2)}, u32[]{:S(2)}) collective-permute-start(bf16[4,512,128]{2,1,0:T(8,128)(2,1)S(1)} %constant_dynamic-update-slice_fusion.6.mine), channel_id=1, source_target_pairs={{0,4},{4,0},{8,12},{12,8},{16,20},{20,16},{24,28},{28,24},{1,5},{5... | collective-permute-start | bytes 1572872 | tf_op jit(solution)/shard_map/ppermute | solution.py:1045
  348.6 15.4 %collective-permute-start.41 = (bf16[4,768,128]{2,1,0:T(8,128)(2,1)S(1)}, bf16[4,768,128]{2,1,0:T(8,128)(2,1)S(1)}, u32[]{:S(2)}, u32[]{:S(2)}) collective-permute-start(bf16[4,768,128]{2,1,0:T(8,128)(2,1)S(1)} %constant_dynamic-update-slice_fusion.8.mine), channel_id=1, source_target_pairs={{0,4},{4,0},{8,12},{12,8},{16,20},{20,16},{24,28},{28,24},{1,5},{5... | collective-permute-start | bytes 2359304 | tf_op jit(solution)/shard_map/ppermute | solution.py:1045
  349.9 12.1 %collective-permute-start.42 = (bf16[4,528,128]{2,1,0:T(8,128)(2,1)S(1)}, bf16[4,528,128]{2,1,0:T(8,128)(2,1)S(1)}, u32[]{:S(2)}, u32[]{:S(2)}) collective-permute-start(bf16[4,528,128]{2,1,0:T(8,128)(2,1)S(1)} %constant_dynamic-update-slice_fusion.10.mine), channel_id=1, source_target_pairs={{0,8},{4,12},{8,0},{12,4},{16,24},{20,28},{24,16},{28,20},{1,9},{5... | collective-permute-start | bytes 1622024 | tf_op jit(solution)/shard_map/ppermute | solution.py:1045
  (108 other events, 1569.3 us)
Sparse Core Ops, SparseCore 0:
  107.5 200.1 all-reduce.5

commit v3 on v2

--- a/solution.py
+++ b/solution.py
@@ -14,9 +14,19 @@
 BF = jnp.bfloat16
 F32 = jnp.float32
 VMEM = pltpu.VMEM
-VMEM_LIMIT = 40 * 1024 * 1024
+HBM = pltpu.HBM
+VMEM_LIMIT = 60 * 1024 * 1024
 SMALL_LIMIT = 24 * 1024 * 1024
 EARLY = 16
+SEQ = ("far", "near")
+
+
+def seq_index():
+    return lax.axis_index("far") * 2 + lax.axis_index("near")
+
+
+def seq_size():
+    return lax.axis_size("far") * lax.axis_size("near")
 
 
 def mm(left, right):
@@ -106,21 +116,42 @@
     return row, col
 
 
+def copies(pairs, sems, first=0):
+    return [
+        pltpu.make_async_copy(source, target, sems.at[first + k]) for k, (source, target) in enumerate(pairs)
+    ]
+
+
+def begin(waiting):
+    for copy in waiting:
+        copy.start()
+    return waiting
+
+
+def end(waiting):
+    for copy in waiting:
+        copy.wait()
+
+
 def prep_kernel(
-    heads, starts, log_rate, bias, proj, halo, conv_q, conv_k, conv_v, small,
-    out_aug, state_aug, wy_k, wy_v, inverse, step_p, query_map, keys, queries, conv_total, cols, doc, row,
+    heads, starts, log_rate, bias, far_proj, halo, conv_q, conv_k, conv_v, far_small,
+    out_aug, far_state_aug, far_wy_k, far_wy_v, far_inverse, far_step_p, far_query_map, far_keys, far_queries,
+    far_conv_total, far_cols, far_doc, far_row,
     final_state, final_map,
-    ext, vals, score_map, step_b, masks,
+    proj, small, state_aug, wy_k, wy_v, inverse, step_p, query_map, keys, queries, conv_total, cols, doc, row,
+    ext, vals, score_map, step_b, masks, sems,
 ):
+    arriving = begin(copies([(far_small, small), (far_proj, proj)], sems))
     tokens = proj.shape[0]
     chunks = tokens // GROUP
-    first = lax.axis_index("seq") * tokens
+    first = seq_index() * tokens
     lead = 8
     lower_r = lax.broadcasted_iota(jnp.int32, (LANES, LANES), 0)
     lower_c = lax.broadcasted_iota(jnp.int32, (LANES, LANES), 1)
     lower = ((lower_r >= lower_c) & (lower_r // GROUP == lower_c // GROUP)).astype(F32)
     lane = lax.broadcasted_iota(jnp.int32, (LANES, LANES), 1)
     per = LANES // GROUP
+    end(arriving[:1])
     for block in range(tokens // LANES):
         at = pl.ds(block * LANES, LANES)
         betas, logdec, _, _ = gate_columns(small[at, :], log_rate, bias, heads)
@@ -142,6 +173,7 @@
         masks[level] = inside.astype(F32)
         level += 1
         width *= 2
+    end(arriving[1:])
     ext[0:lead, :] = halo[16 - lead : 16, :].astype(F32)
     ext[lead:, :] = proj[...].astype(F32)
     width_q = heads * LANES
@@ -184,6 +216,15 @@
         return 0
 
     lax.fori_loop(0, chunks, conv_chunk, 0)
+    leaving = begin(
+        copies(
+            [
+                (conv_total, far_conv_total), (keys, far_keys), (queries, far_queries),
+                (cols, far_cols), (doc, far_doc), (row, far_row),
+            ],
+            sems, 2,
+        )
+    )
 
     strict = order_r > order_c
     eye = (lower_r == lower_c).astype(F32)
@@ -226,6 +267,15 @@
         return 0
 
     lax.fori_loop(0, chunks // together, part_chunks, 0)
+    leaving += begin(
+        copies(
+            [
+                (wy_k, far_wy_k), (wy_v, far_wy_v), (inverse, far_inverse), (step_p, far_step_p),
+                (query_map, far_query_map),
+            ],
+            sems, 8,
+        )
+    )
 
     zero = jnp.zeros((LANES, LANES), F32)
 
@@ -246,11 +296,13 @@
             out_aug[h, rows, :] = jnp.concatenate([mapped[:, :LANES] + score_map[h, c], mapped[:, LANES:]], axis=1)
         return tuple(new)
 
-    begin = jnp.concatenate([zero, eye], axis=1)
-    end = lax.fori_loop(0, chunks, advance, (begin,) * heads)
+    initial = jnp.concatenate([zero, eye], axis=1)
+    last = lax.fori_loop(0, chunks, advance, (initial,) * heads)
+    leaving += begin(copies([(state_aug, far_state_aug)], sems, 13))
     for h in range(heads):
-        final_state[h] = end[h][:, :LANES].astype(final_state.dtype)
-        final_map[h] = end[h][:, LANES:].astype(final_map.dtype)
+        final_state[h] = last[h][:, :LANES].astype(final_state.dtype)
+        final_map[h] = last[h][:, LANES:].astype(final_map.dtype)
+    end(leaving)
 
 
 def specs(count, space=None):
@@ -283,35 +335,50 @@
     return pl.pallas_call(
         functools.partial(prep_kernel, heads),
         out_shape=outs,
-        in_specs=specs(3, pltpu.SMEM) + specs(6),
-        out_specs=specs(len(outs)),
-        scratch_shapes=[
+        in_specs=specs(3, pltpu.SMEM) + specs(1, HBM) + specs(4) + specs(1, HBM),
+        out_specs=specs(1) + specs(12, HBM) + specs(2),
+        scratch_shapes=[VMEM(proj.shape, BF), VMEM(small.shape, F32)]
+        + [VMEM(out.shape, out.dtype) for out in outs[1:13]]
+        + [
             VMEM((tokens + 8, width), F32),
             VMEM(square, BF),
             VMEM((heads, chunks, GROUP, LANES), F32),
             VMEM(square, F32),
             VMEM((8, LANES, LANES), F32),
+            pltpu.SemaphoreType.DMA((14,)),
         ],
         compiler_params=pltpu.CompilerParams(vmem_limit_bytes=VMEM_LIMIT),
-        cost_estimate=pl.CostEstimate(flops=2_000_000_000, bytes_accessed=4_000_000, transcendentals=0),
+        cost_estimate=pl.CostEstimate(flops=24_000_000_000, bytes_accessed=4_000_000, transcendentals=0),
         name="mixer_prep",
     )(starts, log_rate, bias, proj, halo, conv_q, conv_k, conv_v, small)
 
 
 def back_kernel(
-    heads, reach, starts, log_rate, bias, proj, halo, conv_q, conv_k, conv_v, small,
-    state_aug, wy_k, wy_v, inverse, step_p, query_map, keys, queries, conv_total, cols, doc, row,
-    state_in, d_mixed, *rest,
+    heads, reach, starts, log_rate, bias, far_proj, halo, conv_q, conv_k, conv_v, far_small,
+    far_state_aug, far_wy_k, far_wy_v, far_inverse, far_step_p, far_query_map, far_keys, far_queries,
+    far_conv_total, far_cols, far_doc, far_row, state_in, d_mixed, *rest,
 ):
     after = rest[:reach]
     later = rest[reach : 2 * reach - 1]
     (
         d_kq, d_v, tail, d_halo, d_small, d_taps, d_scalars,
-        ext, state_grads, d_query, d_key, d_value, col_grads, row_grads, d_total,
+        proj, small, state_aug, wy_k, wy_v, inverse, step_p, query_map, keys, queries, conv_total, cols, doc, row,
+        ext, state_grads, d_query, d_key, d_value, col_grads, row_grads, d_total, sems,
     ) = rest[2 * reach - 1 :]
+    arriving = begin(
+        copies(
+            [
+                (far_step_p, step_p), (far_query_map, query_map), (far_cols, cols), (far_doc, doc), (far_row, row),
+                (far_state_aug, state_aug), (far_wy_k, wy_k), (far_wy_v, wy_v), (far_inverse, inverse),
+                (far_keys, keys), (far_queries, queries),
+                (far_small, small), (far_conv_total, conv_total), (far_proj, proj),
+            ],
+            sems,
+        )
+    )
     tokens = proj.shape[0]
     chunks = tokens // GROUP
-    first = lax.axis_index("seq") * tokens
+    first = seq_index() * tokens
     lead = 8
     lane = lax.broadcasted_iota(jnp.int32, (GROUP, LANES), 1)
 
@@ -323,12 +390,13 @@
         last = cols[at, NH * heads + h : NH * heads + h + 1][7:8, :]
         return jnp.where(doc[at, 0:1][7:8, :] == document_before(c), jnp.exp(last), 0.0)
 
-    begin = []
+    at_end = []
     for h in range(heads):
         state = after[reach - 1][h].astype(F32)
         for r in range(reach - 2, -1, -1):
             state = mm_tn(later[r][h], state) + after[r][h].astype(F32)
-        begin.append(state)
+        at_end.append(state)
+    end(arriving[:5])
 
     def retreat(step, carry):
         c = chunks - 1 - step
@@ -344,7 +412,8 @@
             )
         return tuple(new)
 
-    lax.fori_loop(0, chunks, retreat, tuple(begin))
+    lax.fori_loop(0, chunks, retreat, tuple(at_end))
+    end(arriving[5:11])
 
     order_r, order_c = order_pair()
     strict = order_r > order_c
@@ -404,10 +473,10 @@
                 ending = key_end * fresh_grad
                 parts = decayed - key_start * solved_state - ending
                 parts = parts[:GROUP] + parts[GROUP:] + score_decay + (start * query_f) * out_state
-                at_end = jnp.sum(ending, keepdims=True) + whole_decay(c, h) * jnp.sum(
+                last_grad = jnp.sum(ending, keepdims=True) + whole_decay(c, h) * jnp.sum(
                     state * d_state.astype(F32), keepdims=True
                 )
-                decay_col = jnp.sum(parts, axis=1, keepdims=True) + jnp.where(last_token, at_end, 0.0)
+                decay_col = jnp.sum(parts, axis=1, keepdims=True) + jnp.where(last_token, last_grad, 0.0)
                 beta_sum = jnp.sum(d_wide * fresh, axis=1, keepdims=True)
                 col_acc = jnp.where(lane == NH * heads + h, decay_col, col_acc)
                 for s in range(NH):
@@ -422,6 +491,8 @@
         return 0
 
     lax.fori_loop(0, chunks // together, chunk_back, 0)
+
+    end(arriving[11:])
 
     lower_r = lax.broadcasted_iota(jnp.int32, (LANES, LANES), 0)
     lower_c = lax.broadcasted_iota(jnp.int32, (LANES, LANES), 1)
@@ -568,9 +639,10 @@
     return pl.pallas_call(
         functools.partial(back_kernel, heads, reach),
         out_shape=outs,
-        in_specs=specs(3, pltpu.SMEM) + specs(len(operands) - 3),
+        in_specs=specs(3, pltpu.SMEM) + specs(1, HBM) + specs(4) + specs(13, HBM) + specs(len(operands) - 21),
         out_specs=specs(len(outs)),
-        scratch_shapes=[
+        scratch_shapes=[VMEM(a.shape, a.dtype) for a in (proj, small, *saved)]
+        + [
             VMEM((tokens + 8, width), F32),
             VMEM(square, BF),
             VMEM((heads, chunks, GROUP, LANES), F32),
@@ -579,6 +651,7 @@
             VMEM((tokens, LANES), F32),
             VMEM((chunks, 8, LANES), F32),
             VMEM((tokens + 8, width), F32),
+            pltpu.SemaphoreType.DMA((14,)),
         ],
         compiler_params=pltpu.CompilerParams(vmem_limit_bytes=VMEM_LIMIT),
         cost_estimate=pl.CostEstimate(flops=2_000_000_000, bytes_accessed=4_000_000, transcendentals=0),
@@ -613,7 +686,7 @@
 
 
 def seq_bits():
-    at = lax.axis_index("seq")
+    at = seq_index()
     z = at // 2 % 4
     low, high = z % 2, z // 2
     return {"x": at % 2, "pair": low ^ high, "cross": high}
@@ -630,21 +703,35 @@
     return pl.ds(pl.multiple_of((low if own else 1 - low) * half, half), half)
 
 
-def project_kernel(x, gain, q_w, k_w, v_w, gate_w, beta_w, decay_w, normed, projected, outgate, small, edge, side_w):
+def project_kernel(
+    far_x, gain, far_q, far_k, far_v, far_gate, beta_w, decay_w, far_normed, far_projected, far_outgate, far_small, edge,
+    x, q_w, k_w, v_w, gate_w, normed, projected, outgate, small, side_w, sems,
+):
+    arriving = begin(
+        copies([(far_x, x), (far_q, q_w), (far_k, k_w), (far_v, v_w), (far_gate, gate_w)], sems)
+    )
+    gather_side(side_w, beta_w, decay_w)
+    end(arriving[:1])
     x_float = x[...].astype(F32)
     low = (x_float * lax.rsqrt(jnp.mean(x_float * x_float, axis=1, keepdims=True) + EPSILON) * gain[...]).astype(BF)
     normed[...] = low
+    leaving = begin(copies([(normed, far_normed)], sems, 5))
     last = x.shape[0] - edge.shape[0]
+    small[...] = mm_nt(low, side_w[...])
+    leaving += begin(copies([(small, far_small)], sems, 6))
     at = 0
-    for weight in (q_w, k_w, v_w):
+    for k, weight in enumerate((q_w, k_w, v_w)):
+        end(arriving[1 + k : 2 + k])
         piece = mm(low, weight[...]).astype(BF)
         projected[:, at : at + weight.shape[1]] = piece
         edge[:, at : at + weight.shape[1]] = piece[last:, :]
         at += weight.shape[1]
     edge[:, at:] = low[last:, :]
+    leaving += begin(copies([(projected, far_projected)], sems, 7))
+    end(arriving[4:])
     outgate[...] = mm(low, gate_w[...])
-    gather_side(side_w, beta_w, decay_w)
-    small[...] = mm_nt(low, side_w[...])
+    leaving += begin(copies([(outgate, far_outgate)], sems, 8))
+    end(leaving)
 
 
 def gather_side(side_w, beta_w, decay_w):
@@ -662,10 +749,19 @@
         shaped((tokens, gate_w.shape[1]), F32), shaped((tokens, LANES), F32), shaped((16, width + wide), BF),
     ]
     operands = [x, gain.reshape(1, -1), q_w, k_w, v_w, gate_w, beta_w, decay_w]
-    return call(
-        project_kernel, "project", outs, operands, flops=2 * tokens * wide * (width + 384),
-        scratch=[VMEM((LANES, wide), F32)],
-    )
+    moved = 8 * x.size
+    return pl.pallas_call(
+        project_kernel,
+        out_shape=outs,
+        in_specs=specs(1, HBM) + specs(1) + specs(4, HBM) + specs(2),
+        out_specs=specs(4, HBM) + specs(1),
+        scratch_shapes=[VMEM(a.shape, a.dtype) for a in (x, q_w, k_w, v_w, gate_w)]
+        + [VMEM(out.shape, out.dtype) for out in outs[:4]]
+        + [VMEM((LANES, wide), F32), pltpu.SemaphoreType.DMA((9,))],
+        compiler_params=pltpu.CompilerParams(vmem_limit_bytes=VMEM_LIMIT),
+        cost_estimate=pl.CostEstimate(flops=8 * tokens * wide * width, bytes_accessed=moved, transcendentals=0),
+        name="project",
+    )(*operands)
 
 
 def attend_kernel(heads, reach, out_aug, outgate, o_gain, out_weight, *rest):
@@ -714,34 +810,54 @@
     return call(enter_kernel, "enter", outs, [x, mine, other, gain.reshape(1, -1)])
 
 
+def near_units(units, own):
+    near = lax.axis_index("near")
+    return pl.ds(pl.multiple_of((near if own else 1 - near) * (units // 2), 16), units // 2)
+
+
+def half_lanes(ref, own):
+    half = ref.shape[1] // 2
+    low = lax.axis_index("head") % 2
+    return pl.ds(pl.multiple_of((low if own else 1 - low) * half, half), half)
+
+
 def feed_kernel(
     own, other, gate_w, up_w, down_w, out_grad,
-    normed, d_gate, d_up, inner, part_give, part_keep, feed_give, feed_keep,
+    normed, d_give, d_keep, part_give, part_keep, feed_give, feed_keep,
 ):
+    units = gate_w.shape[0]
+    half = units // 2
     for mine, source, part, fed in ((False, other, part_give, feed_give), (True, own, part_keep, feed_keep)):
         rows = half_rows(normed, mine)
+        lanes = half_lanes(d_give, mine)
         low = source[...]
         normed[rows, :] = low
-        gate = mm_nt(low, gate_w[...])
-        up = mm_nt(low, up_w[...])
-        d_inner = mm_nt(out_grad[rows, :], down_w[...])
-        sg = sigmoid(gate)
-        active = gate * sg
-        low_inner = (active * up).astype(BF)
-        inner[rows, :] = low_inner
-        low_gate = (d_inner * up * (sg * (1.0 + gate * (1.0 - sg)))).astype(BF)
-        low_up = (d_inner * active).astype(BF)
-        d_gate[rows, :] = low_gate
-        d_up[rows, :] = low_up
-        part[...] = (mm(low_gate, gate_w[...]) + mm(low_up, up_w[...])).astype(part.dtype)
-        fed[...] = mm(low_inner, down_w[...]).astype(fed.dtype)
+        part_sum = jnp.zeros(part.shape, F32)
+        feed_sum = jnp.zeros(fed.shape, F32)
+        for near, out in ((False, d_give), (True, d_keep)):
+            cut = near_units(units, near)
+            gate = mm_nt(gate_w[cut, :], low)
+            up = mm_nt(up_w[cut, :], low)
+            d_inner = mm_nt(down_w[cut, :], out_grad[rows, :])
+            sg = sigmoid(gate)
+            active = gate * sg
+            low_inner = (active * up).astype(BF)
+            low_gate = (d_inner * up * (sg * (1.0 + gate * (1.0 - sg)))).astype(BF)
+            low_up = (d_inner * active).astype(BF)
+            out[0:half, lanes] = low_gate
+            out[half : 2 * half, lanes] = low_up
+            out[2 * half : 3 * half, lanes] = low_inner
+            part_sum += mm_tn(low_gate, gate_w[cut, :]) + mm_tn(low_up, up_w[cut, :])
+            feed_sum += mm_tn(low_inner, down_w[cut, :])
+        part[...] = part_sum.astype(part.dtype)
+        fed[...] = feed_sum.astype(fed.dtype)
 
 
 def feed(own, other, gate_w, up_w, down_w, out_grad):
     tokens, wide = out_grad.shape
     units = gate_w.shape[0]
     half = (tokens // 2, wide)
-    outs = [shaped((tokens, wide), BF)] + [shaped((tokens, units), BF)] * 3 + [
+    outs = [shaped((tokens, wide), BF)] + [shaped((3 * units // 2, tokens), BF)] * 2 + [
         shaped(half, BF), shaped(half, F32), shaped(half, BF), shaped(half, F32),
     ]
     operands = [own, other, gate_w, up_w, down_w, out_grad]
@@ -845,20 +961,35 @@
         part[q, at : at + piece.shape[0], :] = piece[:, q * LANES : (q + 1) * LANES].astype(BF)
 
 
-def feed_weights_kernel(normed, d_gate, d_up, inner, out_grad, grads):
-    units = inner.shape[1]
-    for k, (left, right) in enumerate(((d_gate, normed), (d_up, normed), (inner, out_grad))):
-        grads[k * units : (k + 1) * units, :] = mm_tn(left[...], right[...]).astype(BF)
-
-
-def feed_weights(normed, d_gate, d_up, inner, out_grad):
+def feed_weights_kernel(
+    d_own, normed, out_grad, d_near, normed_mine, normed_other, grad_mine, grad_other, grads
+):
+    half = d_own.shape[0] // 3
+    for k in range(3):
+        right, mine, other = (out_grad, grad_mine, grad_other) if k == 2 else (normed, normed_mine, normed_other)
+        rows = slice(k * half, (k + 1) * half)
+        total = mm(d_own[rows, :], right[...])
+        total += mm(d_near[rows, half_lanes(d_near, True)], mine[...])
+        total += mm(d_near[rows, half_lanes(d_near, False)], other[...])
+        grads[rows, :] = total.astype(BF)
+
+
+def feed_weights(d_own, normed, out_grad, d_near, normed_mine, normed_other, grad_mine, grad_other):
     tokens, wide = normed.shape
-    rows = 3 * inner.shape[1]
-    operands = [normed, d_gate, d_up, inner, out_grad]
+    rows = d_own.shape[0]
+    operands = [d_own, normed, out_grad, d_near, normed_mine, normed_other, grad_mine, grad_other]
     (grads,) = call(
-        feed_weights_kernel, "feed_weights", [shaped((rows, wide), BF)], operands, flops=2 * tokens * wide * rows
+        feed_weights_kernel, "feed_weights", [shaped((rows, wide), BF)], operands, flops=4 * tokens * wide * rows
     )
     return grads
+
+
+def feed_out_kernel(mine, other, *outs):
+    units = outs[0].shape[0]
+    half = units // 2
+    for own, ref in ((True, mine), (False, other)):
+        for k, out in enumerate(outs):
+            out[near_units(units, own), :] = ref[k * half : (k + 1) * half, :].astype(F32)
 
 
 def gate_weights_kernel(normed, d_outgate, branch, grad, give, keep):
@@ -967,7 +1098,7 @@
 class Sum:
     def __init__(self, line, order, give, keep):
         self.line, self.order, self.keep, self.at = line, order, keep, 0
-        self.got = swapped(give, "seq", PARTNER[order[0]])
+        self.got = swapped(give, SEQ, PARTNER[order[0]])
 
     def next(self):
         stages = len(self.order)
@@ -976,18 +1107,18 @@
             give, self.keep = self.line.step(
                 functools.partial(fold, self.order[self.at]), self.keep, self.got
             )
-            self.got = swapped(give, "seq", PARTNER[self.order[self.at]])
+            self.got = swapped(give, SEQ, PARTNER[self.order[self.at]])
             return
         if self.at == stages:
             (mine,) = self.line.step(functools.partial(fold, None), self.keep, self.got)
             bit = 8
-            while bit < lax.axis_size("seq"):
-                mine = (mine.astype(F32) + swapped(mine, "seq", bit).astype(F32)).astype(BF)
+            while bit < seq_size():
+                mine = (mine.astype(F32) + swapped(mine, SEQ, bit).astype(F32)).astype(BF)
                 bit *= 2
         else:
             mine = self.line.step(lambda *parts: jnp.concatenate(parts, axis=0), self.keep, self.got)
         self.keep = mine
-        self.got = swapped(mine, "seq", PARTNER[self.order[2 * stages - 1 - self.at]])
+        self.got = swapped(mine, SEQ, PARTNER[self.order[2 * stages - 1 - self.at]])
 
     def finish(self, kernel, name, outs):
         return self.line.step(
@@ -1036,13 +1167,13 @@
 
 
 def shifted(value, axis, steps):
-    count = lax.axis_size(axis)
+    count = seq_size()
     leading, last = max(0, -steps), min(count, count - steps)
     return lax.ppermute(value, axis, [(source, source + steps) for source in range(leading, last)])
 
 
 def swapped(value, axis, bit):
-    return lax.ppermute(value, axis, [(s, s ^ bit) for s in range(lax.axis_size(axis))])
+    return lax.ppermute(value, axis, [(s, s ^ bit) for s in range(seq_size() if axis == SEQ else lax.axis_size(axis))])
 
 
 def head_sum(give, keep):
@@ -1080,43 +1211,54 @@
     width_k = k_weight.shape[1]
     width = width_q + 2 * width_k
     betas = beta_weight.shape[1]
-    reach = reach_of(tokens, lax.axis_size("seq"))
+    reach = reach_of(tokens, seq_size())
     wide = block_in.shape[1]
     units = gate_weight.shape[1]
     beta_rows, decay_rows = beta_weight.T, decay_weight.T
+    core = lax.axis_index("head") % 2
+    grad_mine = swapped(lax.dynamic_slice_in_dim(out_grad, core * (tokens // 2), tokens // 2, 0), SEQ, 1)
     normed, projected, outgate, small, edge = project(
         block_in, attn_gain, q_weight, k_weight, v_weight, outgate_weight, beta_rows, decay_rows
     )
-    halo = shifted(edge, "seq", 1)
+    halo = shifted(edge, SEQ, 1)
     halo, normed_halo = halo[:, :width], halo[:, width:]
     mixer_args = (seq_start, a_log, dt_bias, projected, halo, conv_q, conv_k, conv_v, small)
     prepared = mixer_prep(*mixer_args)
     out_aug, saved, final_state, final_map = prepared[0], prepared[1:13], prepared[13], prepared[14]
+    final_state, grad_mine = lax.optimization_barrier((final_state, grad_mine))
+    grad_other = swapped(grad_mine, "head", 1)
     pair = jnp.stack([final_state, final_map])
-    before = [shifted(pair, "seq", r) for r in range(1, reach)] + [shifted(final_state[None], "seq", reach)]
-    later = [shifted(final_map, "seq", -r) for r in range(1, reach)]
+    before = [shifted(pair, SEQ, r) for r in range(1, reach)] + [shifted(final_state[None], SEQ, reach)]
+    later = [shifted(final_map, SEQ, -r) for r in range(1, reach)]
     mixed, branch, give, keep, state_in = attend(out_aug, outgate, o_gain, out_weight, before)
     hidden, normed_own = enter(block_in, *head_sum(give, keep), mlp_gain)
-    normed_mlp, d_gate, d_up, inner, part_give, part_keep, feed_give, feed_keep = feed(
+    near_mine = swapped(normed_own, SEQ, 1)
+    normed_mlp, d_give, d_keep, part_give, part_keep, feed_give, feed_keep = feed(
         normed_own, swapped(normed_own, "head", 1), gate_weight.T, up_weight.T, down_weight, out_grad
     )
     line = Line()
     part_mine, part_other = head_sum(part_give, part_keep)
     line.last = part_mine
-    feed_grads = line.step(feed_weights, normed_mlp, d_gate, d_up, inner, out_grad)
-    feed_sums = lax.psum(feed_grads, "seq")
+    d_give, near_mine = lax.optimization_barrier((d_give, near_mine))
+    d_near = swapped(d_give, SEQ, 1)
+    near_other = swapped(near_mine, "head", 1)
     d_hidden, attention_own, grad_mlp_gain = line.step(leave, part_mine, part_other, hidden, mlp_gain, out_grad)
     attention_gradient, grad_mixed, grad_outgate, grad_o_part, carry = line.step(
         attend_back, attention_own, swapped(attention_own, "head", 1), out_weight, mixed, outgate, o_gain, out_aug
     )
-    after = [shifted(carry, "seq", -r) for r in range(1, reach + 1)]
+    after = [shifted(carry, SEQ, -r) for r in range(1, reach + 1)]
+    feed_grads = line.step(
+        feed_weights, d_keep, normed_mlp, out_grad, d_near, near_mine, near_other, grad_mine, grad_other
+    )
+    feed_sums = lax.psum(feed_grads, "far")
+    feed_near = swapped(feed_sums, SEQ, 1)
     sum_out = Sum(line, X_FIRST, *line.step(gate_weights, normed, grad_outgate, branch, attention_gradient))
     feed_mine, feed_other = head_sum(feed_give, feed_keep)
     output = both_halves((hidden + feed_mine.astype(F32) + feed_other.astype(F32)).astype(BF))
     d_kq, d_v, tail, d_halo, grad_small, grad_taps, grad_scalars = line.step(
         lambda d_mixed: mixer_back(*mixer_args, saved, state_in, d_mixed, after, later), grad_mixed
     )
-    following = shifted(d_halo, "seq", -1)
+    following = shifted(d_halo, SEQ, -1)
     cut_q, cut_k, cut_v = slice(0, width_q), slice(width_q, width_q + width_k), slice(width_q + width_k, width)
     halo_kq = jnp.concatenate([d_halo[:, cut_k], d_halo[:, cut_q]], axis=1)
     sum_kq = Sum(
@@ -1126,20 +1268,20 @@
         line, Z_FIRST,
         *line.step(functools.partial(mix_weights, Z_FIRST[0]), normed, normed_halo, d_v, d_halo[:, cut_v], grad_small),
     )
+    taps = conv_q.shape[0]
+
+    def padded(*rows):
+        joined = jnp.concatenate(rows, axis=1)
+        return jnp.pad(joined, ((0, 0), (0, width - joined.shape[1])))
+
+    for part in (sum_out, sum_kq, sum_v):
+        part.next()
     mine, other = head_sum(
         *line.step(
             unproject, d_kq, d_v, tail, following, grad_outgate, grad_small,
             q_weight, k_weight, v_weight, outgate_weight, beta_rows, decay_rows,
         )
     )
-    taps = conv_q.shape[0]
-
-    def padded(*rows):
-        joined = jnp.concatenate(rows, axis=1)
-        return jnp.pad(joined, ((0, 0), (0, width - joined.shape[1])))
-
-    for part in (sum_out, sum_kq, sum_v):
-        part.next()
     for part in (sum_out, sum_kq, sum_v):
         part.next()
     line.last = feed_sums
@@ -1152,16 +1294,18 @@
         ],
         axis=0,
     )
-    small_got = swapped(small_sums, "seq", 1)
+    small_got = swapped(small_sums, SEQ, 1)
     bit = 2
     rounds = 3
     while small_got is not None or rounds > 0:
+        if rounds == 1:
+            line.last = feed_near
         for part in (sum_out, sum_kq, sum_v) if rounds > 0 else ():
             part.next()
         rounds -= 1
         if small_got is not None:
             small_sums = line.step(jnp.add, small_sums, small_got)
-            small_got = swapped(small_sums, "seq", bit) if bit < lax.axis_size("seq") else None
+            small_got = swapped(small_sums, SEQ, bit) if bit < seq_size() else None
             bit *= 2
     gains = small_sums[taps + 1 : taps + 4]
     gains = gains + swapped(gains, "head", 1)
@@ -1181,8 +1325,8 @@
         functools.partial(mix_out_kernel, False), "mix_out",
         [shaped((wide, width_k), F32), shaped((wide, width_q), F32)],
     )
-    grad_gate_w, grad_up_w, grad_down_w = (
-        feed_sums[k * units : (k + 1) * units].astype(F32) for k in range(3)
+    grad_gate_w, grad_up_w, grad_down_w = call(
+        feed_out_kernel, "feed_out", [shaped((units, wide), F32)] * 3, [feed_sums, feed_near]
     )
     rate, shift = small_sums[taps, betas : betas + heads], small_sums[taps, LANES + betas : LANES + betas + heads]
     return (
@@ -1195,15 +1339,17 @@
 
 def solution(mesh):
     placed = (
-        P("seq", None), P(), P(), P(None, "head"), P(None, "head"), P(None, "head"), P(None, "head"),
+        P(SEQ, None), P(), P(), P(None, "head"), P(None, "head"), P(None, "head"), P(None, "head"),
         P(None, "head"), P(None, "head"), P(None, "head"), P(None, "head"), P("head"), P("head"),
         P(None, "head"), P(), P("head", None), P(), P(None, "head"), P(None, "head"), P("head", None),
-        P("seq", None),
+        P(SEQ, None),
     )
     given = (
-        P("seq", None), P("seq", None), P(), P(None, "head"), P(None, "head"), P(None, "head"),
+        P(SEQ, None), P(SEQ, None), P(), P(None, "head"), P(None, "head"), P(None, "head"),
         P(None, "head"), P(None, "head"), P(None, "head"), P(None, "head"), P(None, "head"), P("head"),
         P("head"), P(None, "head"), P(), P("head", None), P(), P(None, "head"), P(None, "head"),
         P("head", None),
     )
+    seq, head = mesh.devices.shape
+    mesh = jax.sharding.Mesh(mesh.devices.reshape(seq // 2, 2, head), ("far", "near", "head"))
     return jax.shard_map(local, mesh=mesh, in_specs=placed, out_specs=given, check_vma=False)

time: 374 us -> 341 us (0.912)
  waiting for transfers between devices: 173 us -> 119 us
  Pallas kernels: 76.9 us -> 95.4 us
  starting transfers between devices: 61.8 us -> 78 us
  local copies, waits for them, and re-layouts: 31.8 us -> 18.6 us
    psum x1, waiting for transfers between devices: 43 us -> 0.01 us  [local(): feed_sums = lax.psum(feed_grads, 'far')]
    ppermute x10, waiting for transfers between devices: 32.6 us -> 10.7 us  [shifted(): lax.ppermute(value, axis, [(source, source + steps) for source in range(l...]
    ppermute x35 -> x41, starting transfers between devices: 35.2 us -> 52.1 us  [swapped(): lax.ppermute(value, axis, [(s, s ^ bit) for s in range(seq_size() if axis...]
    unnamed x194 -> x120, local copies, waits for them, and re-layouts: 25.8 us -> 10.3 us
    ppermute x35 -> x41, waiting for transfers between devices: 97.1 us -> 109 us  [swapped(): lax.ppermute(value, axis, [(s, s ^ bit) for s in range(seq_size() if axis...]
    pallas_call x0 -> x1, Pallas kernels: none -> 6.97 us  [project(): pl.pallas_call(project_kernel, out_shape=outs, in_specs=specs(1, HBM) + s...]
    convert_element_type x1 -> x0, other arithmetic: 6.07 us -> none  [local(): feed_sums[k * units:(k + 1) * units].astype(F32)]
    pallas_call x24, Pallas kernels: 33.7 us -> 39.2 us  [call(): pl.pallas_call(kernel, out_shape=outs, in_specs=specs(smem, pltpu.SMEM) +...]
  transfers between devices with their start and end apart: 46 -> 52, of which waited for: 23 -> 22; matrix products, arithmetic and copies ran while one was open for 5% -> 6% of each run, Pallas kernels for 13% -> 24%
where the time goes in v3:
time: 341 us; the launch traced here: 339 us
  waiting for transfers between devices  119 us (35%)
  Pallas kernels  95.4 us (28%)
  starting transfers between devices  78 us (23%)
  local copies, waits for them, and re-layouts  18.6 us (5%)
  between operations  15 us (4%)
  other arithmetic  13 us (4%)
    ppermute x41, waiting for transfers between devices, swapped(): lax.ppermute(value, axis, [(s, s ^ bit) for s in range(seq_size() if axis...  109 us
    ppermute x41, starting transfers between devices, swapped(): lax.ppermute(value, axis, [(s, s ^ bit) for s in range(seq_size() if axis...  52.1 us
    pallas_call x24, Pallas kernels, call(): pl.pallas_call(kernel, out_shape=outs, in_specs=specs(smem, pltpu.SMEM) +...  39.2 us
    pallas_call x1, Pallas kernels, mixer_back(): pl.pallas_call(functools.partial(back_kernel, heads, reach), out_shape=ou...  27.2 us
    ppermute x10, starting transfers between devices, shifted(): lax.ppermute(value, axis, [(source, source + steps) for source in range(l...  25.9 us
    pallas_call x1, Pallas kernels, mixer_prep(): pl.pallas_call(functools.partial(prep_kernel, heads), out_shape=outs, in_...  22 us
    ppermute x10, waiting for transfers between devices, shifted(): lax.ppermute(value, axis, [(source, source + steps) for source in range(l...  10.7 us
    unnamed x120, local copies, waits for them, and re-layouts  10.3 us
  transfers between devices with their start and end apart: 52, of which 22 were waited for; matrix products, arithmetic and copies ran while one was open for 6% of the time, Pallas kernels for 24%

profile of v3, /device:TPU:0, one launch (start us, length us, event | category | flops | bytes accessed | tf_op | source)
XLA Modules:
  0.0 339.4 jit_solution(7900400519686793475)
XLA Ops:
  7.2 7.0 %project.1 = (bf16[512,1024]{1,0:T(8,128)(2,1)}, bf16[512,1280]{1,0:T(8,128)(2,1)}, f32[512,256]{1,0:T(8,128)}, f32[512,128]{1,0:T(8,128)}, bf16[16,2304]{1,0:T(8,128)(2,1)}) custom-call(bf16[512,1024]{1,0:T(8,128)(2,1)} %x.10, f32[1,1024]{1,0:T(1,128)} %bitcast.30, bf16[1024,256]{1,0:T(8,128)(2,1)} %q_w, bf16[1024,512]{1,0:T(8,128)(2,1)} %k_w, ...), custom_call_target="tpu_custom_call" | custom-call | flops 5368709120 | bytes 4194304 | tf_op jit(solution)/shard_map/project/pallas_call | solution.py:753
  14.2 4.8 %collective-permute-start = (bf16[16,2304]{1,0:T(8,128)(2,1)}, bf16[16,2304]{1,0:T(8,128)(2,1)S(1)}, u32[]{:S(2)}, u32[]{:S(2)}) collective-permute-start(bf16[16,2304]{1,0:T(8,128)(2,1)} %get-tuple-element.199), channel_id=1, source_target_pairs={{0,4},{4,8},{8,12},{12,16},{16,20},{20,24},{24,28},{1,5},{5,9},{9,... | collective-permute-start | bytes 221192 | tf_op jit(solution)/shard_map/ppermute | solution.py:1172
  22.6 22.0 %mixer_prep.1 = (f32[2,512,256]{2,1,0:T(8,128)}, bf16[2,8,128,256]{3,2,1,0:T(8,128)(2,1)}, bf16[2,8,128,128]{3,2,1,0:T(8,128)(2,1)}, bf16[2,8,128,128]{3,2,1,0:T...) custom-call(s32[10]{0:T(128)} %starts.3, ...), custom_call_target="tpu_custom_call" | custom-call | flops 24000000000 | bytes 4000000 | tf_op jit(solution)/shard_map/mixer_prep/pallas_call | solution.py:335
  45.6 4.3 %collective-permute-start.2 = (bf16[2,2,128,128]{3,2,1,0:T(8,128)(2,1)S(1)}, bf16[2,2,128,128]{3,2,1,0:T(8,128)(2,1)S(1)}, u32[]{:S(2)}, u32[]{:S(2)}) collective-permute-start(bf16[2,2,128,128]{3,2,1,0:T(8,128)(2,1)S(1)} %pad_maximum_fusion.2), channel_id=1, source_target_pairs={{0,4},{4,8},{8,12},{12,16},{16,20},{20,24},{24,28},{1,5},{5,9},{9,... | collective-permute-start | bytes 393224 | tf_op jit(solution)/shard_map/ppermute | solution.py:1172
  50.0 3.5 %collective-permute-start.3 = (bf16[2,2,128,128]{3,2,1,0:T(8,128)(2,1)S(1)}, bf16[2,2,128,128]{3,2,1,0:T(8,128)(2,1)S(1)}, u32[]{:S(2)}, u32[]{:S(2)}) collective-permute-start(bf16[2,2,128,128]{3,2,1,0:T(8,128)(2,1)S(1)} %pad_maximum_fusion.2), channel_id=1, source_target_pairs={{0,8},{4,12},{8,16},{12,20},{16,24},{20,28},{1,9},{5,13},{9,17},{1... | collective-permute-start | bytes 393224 | tf_op jit(solution)/shard_map/ppermute | solution.py:1172
  53.5 4.9 %collective-permute-start.4 = (bf16[1,2,128,128]{3,2,1,0:T(8,128)(2,1)}, bf16[1,2,128,128]{3,2,1,0:T(8,128)(2,1)S(1)}, u32[]{:S(2)}, u32[]{:S(2)}) collective-permute-start(bf16[1,2,128,128]{3,2,1,0:T(8,128)(2,1)} %bitcast.38), channel_id=1, source_target_pairs={{0,12},{4,16},{8,20},{12,24},{16,28},{1,13},{5,17},{9,21},{13,25},... | collective-permute-start | bytes 196616 | tf_op jit(solution)/shard_map/ppermute | solution.py:1172
  67.8 12.4 %collective-permute-done.6.other = bf16[256,1024]{1,0:T(8,128)(2,1)S(1)} collective-permute-done((bf16[256,1024]{1,0:T(8,128)(2,1)S(1)}, bf16[256,1024]{1,0:T(8,128)(2,1)S(1)}, u32[]{:S(2)}, u32[]{:S(2)}) %collective-permute-start.6) | collective-permute-done | bytes 524320 | tf_op jit(solution)/shard_map/ppermute | solution.py:1176
  82.5 7.2 %feed.1 = (bf16[512,1024]{1,0:T(8,128)(2,1)S(1)}, bf16[1056,512]{1,0:T(8,128)(2,1)S(1)}, bf16[1056,512]{1,0:T(8,128)(2,1)S(1)}, bf16[256,1024]{1,0:T(8,128)(2,1)...) custom-call(bf16[256,1024]{1,0:T(8,128)(2,1)S(1)} %get-tuple-element.209.own, ...), custom_call_target="tpu_custom_call" | custom-call | flops 276824064 | bytes 798720 | tf_op jit(solution)/shard_map/feed/pallas_call | solution.py:666
  89.9 5.1 %collective-permute-done.14.normed_mine = bf16[256,1024]{1,0:T(8,128)(2,1)S(1)} collective-permute-done((bf16[256,1024]{1,0:T(8,128)(2,1)S(1)}, bf16[256,1024]{1,0:T(8,128)(2,1)S(1)}, u32[]{:S(2)}, u32[]{:S(2)}) %collective-permute-start.14) | collective-permute-done | bytes 524320 | tf_op jit(solution)/shard_map/ppermute | solution.py:1176
  98.1 11.7 %collective-permute-done.12.other = bf16[256,1024]{1,0:T(8,128)(2,1)S(1)} collective-permute-done((bf16[256,1024]{1,0:T(8,128)(2,1)S(1)}, bf16[256,1024]{1,0:T(8,128)(2,1)S(1)}, u32[]{:S(2)}, u32[]{:S(2)}) %collective-permute-start.12) | collective-permute-done | bytes 524320 | tf_op jit(solution)/shard_map/ppermute | solution.py:1176
  116.1 4.3 %collective-permute-done.15.d_near = bf16[1056,512]{1,0:T(8,128)(2,1)S(1)} collective-permute-done((bf16[1056,512]{1,0:T(8,128)(2,1)S(1)}, bf16[1056,512]{1,0:T(8,128)(2,1)S(1)}, u32[]{:S(2)}, u32[]{:S(2)}) %collective-permute-start.15) | collective-permute-done | bytes 1081376 | tf_op jit(solution)/shard_map/ppermute | solution.py:1176
  120.4 3.7 %feed_weights.1 = bf16[1056,1024]{1,0:T(8,128)(2,1)} custom-call(bf16[1056,512]{1,0:T(8,128)(2,1)S(1)} %get-tuple-element.253.d_own, bf16[512,1024]{1,0:T(8,128)(2,1)S(1)} %get-tuple-element.254.normed, bf16[512,1024]{1,0:T(8,128)(2,1)S(1)} %copy-done, bf16[1056,512]{1,0:T(8,128)(2,1)S(1)} %collective-permute-done.15.d_near, ...), custom_call_target="tpu_custom_call" | custom-call | flops 138412032 | bytes 532480 | tf_op jit(solution)/shard_map/feed_weights/pallas_call | solution.py:666
  135.9 2.7 collective-permute-start.26
  138.7 4.9 %collective-permute-done.19.rest_1_ = bf16[2,128,128]{2,1,0:T(8,128)(2,1)S(1)} collective-permute-done((bf16[2,128,128]{2,1,0:T(8,128)(2,1)S(1)}, bf16[2,128,128]{2,1,0:T(8,128)(2,1)S(1)}, u32[]{:S(2)}, u32[]{:S(2)}) %collective-permute-start.19) | collective-permute-done | bytes 65568 | tf_op jit(solution)/shard_map/ppermute | solution.py:1172
  146.1 27.2 %mixer_back.1 = (bf16[512,768]{1,0:T(8,128)(2,1)}, bf16[512,512]{1,0:T(8,128)(2,1)}, f32[16,1280]{1,0:T(8,128)}, f32[8,1280]{1,0:T(8,128)}, bf16[512,128]{1,0:T(...) custom-call(s32[10]{0:T(128)} %starts.3, f32[2]{0:T(128)} %log_rate.3, f32[2]{0:T(128)} %bias.3, ...), custom_call_target="tpu_custom_call" | custom-call | flops 2000000000 | bytes 4000000 | tf_op jit(solution)/shard_map/mixer_back/pallas_call | solution.py:639
  177.4 9.8 %collective-permute-start.25 = (bf16[4,768,128]{2,1,0:T(8,128)(2,1)S(1)}, bf16[4,768,128]{2,1,0:T(8,128)(2,1)S(1)}, u32[]{:S(2)}, u32[]{:S(2)}) collective-permute-start(bf16[4,768,128]{2,1,0:T(8,128)(2,1)S(1)} %get-tuple-element.277), channel_id=1, source_target_pairs={{0,4},{4,0},{8,12},{12,8},{16,20},{20,16},{24,28},{28,24},{1,5},{5... | collective-permute-start | bytes 2359304 | tf_op jit(solution)/shard_map/ppermute | solution.py:1176
  194.8 4.8 %collective-permute-done.25.got = bf16[4,768,128]{2,1,0:T(8,128)(2,1)S(1)} collective-permute-done((bf16[4,768,128]{2,1,0:T(8,128)(2,1)S(1)}, bf16[4,768,128]{2,1,0:T(8,128)(2,1)S(1)}, u32[]{:S(2)}, u32[]{:S(2)}) %collective-permute-start.25) | collective-permute-done | bytes 786464 | tf_op jit(solution)/shard_map/ppermute | solution.py:1176
  200.4 26.2 %collective-permute-done.24.got = bf16[4,528,128]{2,1,0:T(8,128)(2,1)S(1)} collective-permute-done((bf16[4,528,128]{2,1,0:T(8,128)(2,1)S(1)}, bf16[4,528,128]{2,1,0:T(8,128)(2,1)S(1)}, u32[]{:S(2)}, u32[]{:S(2)}) %collective-permute-start.24) | collective-permute-done | bytes 540704 | tf_op jit(solution)/shard_map/ppermute | solution.py:1176
  232.6 2.6 collective-permute-start.45
  238.5 2.2 broadcast_select_fusion.3
  242.8 3.8 %collective-permute-start.36 = (bf16[1,512,128]{2,1,0:T(8,128)(2,1)}, bf16[1,512,128]{2,1,0:T(8,128)(2,1)}, u32[]{:S(2)}, u32[]{:S(2)}) collective-permute-start(bf16[1,512,128]{2,1,0:T(8,128)(2,1)} %get-tuple-element.326), channel_id=1, source_target_pairs={{0,24},{4,28},{8,16},{12,20},{16,8},{20,12},{24,0},{28,4},{1,25},{... | collective-permute-start | bytes 393224 | tf_op jit(solution)/shard_map/ppermute | solution.py:1176
  246.6 9.6 %collective-permute-done.32.got = bf16[2,768,128]{2,1,0:T(8,128)(2,1)} collective-permute-done((bf16[2,768,128]{2,1,0:T(8,128)(2,1)}, bf16[2,768,128]{2,1,0:T(8,128)(2,1)}, u32[]{:S(2)}, u32[]{:S(2)}) %collective-permute-start.32) | collective-permute-done | bytes 393248 | tf_op jit(solution)/shard_map/ppermute | solution.py:1176
  259.9 2.6 collective-permute-start.34
  266.6 3.9 %collective-permute-start.40 = (bf16[1,512,128]{2,1,0:T(8,128)(2,1)S(1)}, bf16[1,512,128]{2,1,0:T(8,128)(2,1)S(1)}, u32[]{:S(2)}, u32[]{:S(2)}) collective-permute-start(bf16[1,512,128]{2,1,0:T(8,128)(2,1)S(1)} %fold.15), channel_id=1, source_target_pairs={{0,24},{4,28},{8,16},{12,20},{16,8},{20,12},{24,0},{28,4},{1,25},{... | collective-permute-start | bytes 393224 | tf_op jit(solution)/shard_map/ppermute | solution.py:1176
  270.5 2.2 pad_maximum_fusion
  273.8 11.9 %collective-permute-done.34.got = bf16[1,528,128]{2,1,0:T(8,128)(2,1)} collective-permute-done((bf16[1,528,128]{2,1,0:T(8,128)(2,1)}, bf16[1,528,128]{2,1,0:T(8,128)(2,1)}, u32[]{:S(2)}, u32[]{:S(2)}) %collective-permute-start.34) | collective-permute-done | bytes 135200 | tf_op jit(solution)/shard_map/ppermute | solution.py:1176
  288.8 4.4 %collective-permute-done.39 = bf16[1,768,128]{2,1,0:T(8,128)(2,1)S(1)} collective-permute-done((bf16[1,768,128]{2,1,0:T(8,128)(2,1)S(1)}, bf16[1,768,128]{2,1,0:T(8,128)(2,1)S(1)}, u32[]{:S(2)}, u32[]{:S(2)}) %collective-permute-start.39) | collective-permute-done | bytes 196640 | tf_op jit(solution)/shard_map/ppermute | solution.py:1176
  293.3 2.5 collective-permute-start.44
  297.2 2.4 collective-permute-start.41
  305.0 5.9 %collective-permute-done.43 = bf16[2,768,128]{2,1,0:T(8,128)(2,1)S(1)} collective-permute-done((bf16[2,768,128]{2,1,0:T(8,128)(2,1)S(1)}, bf16[2,768,128]{2,1,0:T(8,128)(2,1)S(1)}, u32[]{:S(2)}, u32[]{:S(2)}) %collective-permute-start.43) | collective-permute-done | bytes 393248 | tf_op jit(solution)/shard_map/ppermute | solution.py:1176
  311.9 5.3 %collective-permute-done.42 = bf16[2,528,128]{2,1,0:T(8,128)(2,1)S(1)} collective-permute-done((bf16[2,528,128]{2,1,0:T(8,128)(2,1)S(1)}, bf16[2,528,128]{2,1,0:T(8,128)(2,1)S(1)}, u32[]{:S(2)}, u32[]{:S(2)}) %collective-permute-start.42) | collective-permute-done | bytes 270368 | tf_op jit(solution)/shard_map/ppermute | solution.py:1176
  319.2 3.9 %feed_out.1 = (f32[704,1024]{1,0:T(8,128)}, f32[704,1024]{1,0:T(8,128)}, f32[704,1024]{1,0:T(8,128)}) custom-call(bf16[1056,1024]{1,0:T(8,128)(2,1)S(1)} %copy-done.7, bf16[1056,1024]{1,0:T(8,128)(2,1)S(1)} %collective-permute-done.45.other), custom_call_target="tpu_custom_call" | custom-call | bytes 811008 | tf_op jit(solution)/shard_map/feed_out/pallas_call | solution.py:666
  (260 shorter events, 94.7 us)
Async XLA Ops:
  7.2 225.4 %all-reduce.6.cloned.1.call-start = ((), (), s32[]{:S(2)}) async-start(), calls=%async_computation | async-start | bytes 4325376 | tf_op jit(solution)/shard_map/psum | solution.py:1253
  19.1 25.4 %collective-permute-start.1 = (bf16[256,1024]{1,0:T(8,128)(2,1)S(1)}, bf16[256,1024]{1,0:T(8,128)(2,1)S(1)}, u32[]{:S(2)}, u32[]{:S(2)}) collective-permute-start(bf16[256,1024]{1,0:T(8,128)(2,1)S(1)} %constant_dynamic-slice_fusion), channel_id=1, source_target_pairs={{0,4},{4,0},{8,12},{12,8},{16,20},{20,16},{24,28},{28,24},{1,5},{5... | collective-permute-start | bytes 1572872 | tf_op jit(solution)/shard_map/ppermute | solution.py:1176
  45.6 14.7 %collective-permute-start.2 = (bf16[2,2,128,128]{3,2,1,0:T(8,128)(2,1)S(1)}, bf16[2,2,128,128]{3,2,1,0:T(8,128)(2,1)S(1)}, u32[]{:S(2)}, u32[]{:S(2)}) collective-permute-start(bf16[2,2,128,128]{3,2,1,0:T(8,128)(2,1)S(1)} %pad_maximum_fusion.2), channel_id=1, source_target_pairs={{0,4},{4,8},{8,12},{12,16},{16,20},{20,24},{24,28},{1,5},{5,9},{9,... | collective-permute-start | bytes 393224 | tf_op jit(solution)/shard_map/ppermute | solution.py:1172
  66.2 14.0 %collective-permute-start.6 = (bf16[256,1024]{1,0:T(8,128)(2,1)S(1)}, bf16[256,1024]{1,0:T(8,128)(2,1)S(1)}, u32[]{:S(2)}, u32[]{:S(2)}) collective-permute-start(bf16[256,1024]{1,0:T(8,128)(2,1)S(1)} %add_convert_fusion.4.mine), channel_id=1, source_target_pairs={{0,2},{1,3},{2,0},{3,1},{4,6},{5,7},{6,4},{7,5},{8,10},{9,11},{10,... | collective-permute-start | bytes 1572872 | tf_op jit(solution)/shard_map/ppermute | solution.py:1176
  80.6 14.3 %collective-permute-start.14 = (bf16[256,1024]{1,0:T(8,128)(2,1)S(1)}, bf16[256,1024]{1,0:T(8,128)(2,1)S(1)}, u32[]{:S(2)}, u32[]{:S(2)}) collective-permute-start(bf16[256,1024]{1,0:T(8,128)(2,1)S(1)} %get-tuple-element.209.own), channel_id=1, source_target_pairs={{0,4},{4,0},{8,12},{12,8},{16,20},{20,16},{24,28},{28,24},{1,5},{5... | collective-permute-start | bytes 1572872 | tf_op jit(solution)/shard_map/ppermute | solution.py:1176
  95.0 25.4 %collective-permute-start.15 = (bf16[1056,512]{1,0:T(8,128)(2,1)S(1)}, bf16[1056,512]{1,0:T(8,128)(2,1)S(1)}, u32[]{:S(2)}, u32[]{:S(2)}) collective-permute-start(bf16[1056,512]{1,0:T(8,128)(2,1)S(1)} %get-tuple-element.250), channel_id=1, source_target_pairs={{0,4},{4,0},{8,12},{12,8},{16,20},{20,16},{24,28},{28,24},{1,5},{5... | collective-permute-start | bytes 3244040 | tf_op jit(solution)/shard_map/ppermute | solution.py:1176
  96.5 13.3 %collective-permute-start.12 = (bf16[256,1024]{1,0:T(8,128)(2,1)S(1)}, bf16[256,1024]{1,0:T(8,128)(2,1)S(1)}, u32[]{:S(2)}, u32[]{:S(2)}) collective-permute-start(bf16[256,1024]{1,0:T(8,128)(2,1)S(1)} %add_convert_fusion.1.mine), channel_id=1, source_target_pairs={{0,2},{1,3},{2,0},{3,1},{4,6},{5,7},{6,4},{7,5},{8,10},{9,11},{10,... | collective-permute-start | bytes 1572872 | tf_op jit(solution)/shard_map/ppermute | solution.py:1176
  126.9 11.8 %collective-permute-start.18 = (bf16[2,128,128]{2,1,0:T(8,128)(2,1)S(1)}, bf16[2,128,128]{2,1,0:T(8,128)(2,1)S(1)}, u32[]{:S(2)}, u32[]{:S(2)}) collective-permute-start(bf16[2,128,128]{2,1,0:T(8,128)(2,1)S(1)} %get-tuple-element.267), channel_id=1, source_target_pairs={{4,0},{8,4},{12,8},{16,12},{20,16},{24,20},{28,24},{5,1},{9,5},{13... | collective-permute-start | bytes 196616 | tf_op jit(solution)/shard_map/ppermute | solution.py:1172
  128.2 15.4 %collective-permute-start.19 = (bf16[2,128,128]{2,1,0:T(8,128)(2,1)S(1)}, bf16[2,128,128]{2,1,0:T(8,128)(2,1)S(1)}, u32[]{:S(2)}, u32[]{:S(2)}) collective-permute-start(bf16[2,128,128]{2,1,0:T(8,128)(2,1)S(1)} %get-tuple-element.267), channel_id=1, source_target_pairs={{8,0},{12,4},{16,8},{20,12},{24,16},{28,20},{9,1},{13,5},{17,9},{2... | collective-permute-start | bytes 196616 | tf_op jit(solution)/shard_map/ppermute | solution.py:1172
  129.5 16.0 %collective-permute-start.20 = (bf16[2,128,128]{2,1,0:T(8,128)(2,1)S(1)}, bf16[2,128,128]{2,1,0:T(8,128)(2,1)S(1)}, u32[]{:S(2)}, u32[]{:S(2)}) collective-permute-start(bf16[2,128,128]{2,1,0:T(8,128)(2,1)S(1)} %get-tuple-element.267), channel_id=1, source_target_pairs={{12,0},{16,4},{20,8},{24,12},{28,16},{13,1},{17,5},{21,9},{25,13},... | collective-permute-start | bytes 196616 | tf_op jit(solution)/shard_map/ppermute | solution.py:1172
  135.3 53.2 %collective-permute-start.8 = (bf16[256,1024]{1,0:T(8,128)(2,1)}, bf16[256,1024]{1,0:T(8,128)(2,1)}, u32[]{:S(2)}, u32[]{:S(2)}) collective-permute-start(bf16[256,1024]{1,0:T(8,128)(2,1)} %get-tuple-element.211), channel_id=1, source_target_pairs={{0,1},{1,0},{2,3},{3,2},{4,5},{5,4},{6,7},{7,6},{8,9},{9,8},{10,11... | collective-permute-start | bytes 1572872 | tf_op jit(solution)/shard_map/ppermute | solution.py:1176
  135.9 57.0 %collective-permute-start.26 = (bf16[4,512,128]{2,1,0:T(8,128)(2,1)}, bf16[4,512,128]{2,1,0:T(8,128)(2,1)}, u32[]{:S(2)}, u32[]{:S(2)}) collective-permute-start(bf16[4,512,128]{2,1,0:T(8,128)(2,1)} %get-tuple-element.265), channel_id=1, source_target_pairs={{0,4},{4,0},{8,12},{12,8},{16,20},{20,16},{24,28},{28,24},{1,5},{5... | collective-permute-start | bytes 1572872 | tf_op jit(solution)/shard_map/ppermute | solution.py:1176
  177.4 22.1 %collective-permute-start.25 = (bf16[4,768,128]{2,1,0:T(8,128)(2,1)S(1)}, bf16[4,768,128]{2,1,0:T(8,128)(2,1)S(1)}, u32[]{:S(2)}, u32[]{:S(2)}) collective-permute-start(bf16[4,768,128]{2,1,0:T(8,128)(2,1)S(1)} %get-tuple-element.277), channel_id=1, source_target_pairs={{0,4},{4,0},{8,12},{12,8},{16,20},{20,16},{24,28},{28,24},{1,5},{5... | collective-permute-start | bytes 2359304 | tf_op jit(solution)/shard_map/ppermute | solution.py:1176
  188.4 38.2 %collective-permute-start.24 = (bf16[4,528,128]{2,1,0:T(8,128)(2,1)S(1)}, bf16[4,528,128]{2,1,0:T(8,128)(2,1)S(1)}, u32[]{:S(2)}, u32[]{:S(2)}) collective-permute-start(bf16[4,528,128]{2,1,0:T(8,128)(2,1)S(1)} %get-tuple-element.284), channel_id=1, source_target_pairs={{0,8},{4,12},{8,0},{12,4},{16,24},{20,28},{24,16},{28,20},{1,9},{5... | collective-permute-start | bytes 1622024 | tf_op jit(solution)/shard_map/ppermute | solution.py:1176
  189.8 39.3 %collective-permute-start.9 = (bf16[256,1024]{1,0:T(8,128)(2,1)S(1)}, bf16[256,1024]{1,0:T(8,128)(2,1)S(1)}, u32[]{:S(2)}, u32[]{:S(2)}) collective-permute-start(bf16[256,1024]{1,0:T(8,128)(2,1)S(1)} %add_convert_fusion.3), channel_id=1, source_target_pairs={{0,2},{1,3},{2,0},{3,1},{4,6},{5,7},{6,4},{7,5},{8,10},{9,11},{10,... | collective-permute-start | bytes 1572872 | tf_op jit(solution)/shard_map/ppermute | solution.py:1176
  191.4 35.3 %collective-permute-start.23 = (f32[8,1280]{1,0:T(8,128)S(1)}, f32[8,1280]{1,0:T(8,128)S(1)}, u32[]{:S(2)}, u32[]{:S(2)}) collective-permute-start(f32[8,1280]{1,0:T(8,128)S(1)} %copy-done.55), channel_id=1, source_target_pairs={{4,0},{8,4},{12,8},{16,12},{20,16},{24,20},{28,24},{5,1},{9,5},{13... | collective-permute-start | bytes 122888 | tf_op jit(solution)/shard_map/ppermute | solution.py:1172
  231.3 25.0 %collective-permute-start.32 = (bf16[2,768,128]{2,1,0:T(8,128)(2,1)}, bf16[2,768,128]{2,1,0:T(8,128)(2,1)}, u32[]{:S(2)}, u32[]{:S(2)}) collective-permute-start(bf16[2,768,128]{2,1,0:T(8,128)(2,1)} %get-tuple-element.292), channel_id=1, source_target_pairs={{0,8},{4,12},{8,0},{12,4},{16,24},{20,28},{24,16},{28,20},{1,9},{5... | collective-permute-start | bytes 1179656 | tf_op jit(solution)/shard_map/ppermute | solution.py:1176
  232.6 70.8 %collective-permute-start.45 = (bf16[1056,1024]{1,0:T(8,128)(2,1)}, bf16[1056,1024]{1,0:T(8,128)(2,1)S(1)}, u32[]{:S(2)}, u32[]{:S(2)}) collective-permute-start(bf16[1056,1024]{1,0:T(8,128)(2,1)} %all-reduce.6.cloned.1.call-done.mine), channel_id=1, source_target_pairs={{0,4},{4,0},{8,12},{12,8},{16,20},{20,16},{24,28},{28,24},{1,5},{5... | collective-permute-start | bytes 6488072 | tf_op jit(solution)/shard_map/ppermute | solution.py:1176
  236.9 25.6 %collective-permute-start.28 = (bf16[256,1024]{1,0:T(8,128)(2,1)S(1)}, bf16[256,1024]{1,0:T(8,128)(2,1)S(1)}, u32[]{:S(2)}, u32[]{:S(2)}) collective-permute-start(bf16[256,1024]{1,0:T(8,128)(2,1)S(1)} %add_convert_fusion.mine), channel_id=1, source_target_pairs={{0,2},{1,3},{2,0},{3,1},{4,6},{5,7},{6,4},{7,5},{8,10},{9,11},{10,... | collective-permute-start | bytes 1572872 | tf_op jit(solution)/shard_map/ppermute | solution.py:1176
  241.3 17.9 %collective-permute-start.31 = (bf16[2,528,128]{2,1,0:T(8,128)(2,1)S(1)}, bf16[2,528,128]{2,1,0:T(8,128)(2,1)S(1)}, u32[]{:S(2)}, u32[]{:S(2)}) collective-permute-start(bf16[2,528,128]{2,1,0:T(8,128)(2,1)S(1)} %copy-done.48), channel_id=1, source_target_pairs={{0,24},{4,28},{8,16},{12,20},{16,8},{20,12},{24,0},{28,4},{1,25},{... | collective-permute-start | bytes 811016 | tf_op jit(solution)/shard_map/ppermute | solution.py:1176
  242.8 22.0 %collective-permute-start.36 = (bf16[1,512,128]{2,1,0:T(8,128)(2,1)}, bf16[1,512,128]{2,1,0:T(8,128)(2,1)}, u32[]{:S(2)}, u32[]{:S(2)}) collective-permute-start(bf16[1,512,128]{2,1,0:T(8,128)(2,1)} %get-tuple-element.326), channel_id=1, source_target_pairs={{0,24},{4,28},{8,16},{12,20},{16,8},{20,12},{24,0},{28,4},{1,25},{... | collective-permute-start | bytes 393224 | tf_op jit(solution)/shard_map/ppermute | solution.py:1176
  258.0 14.8 %collective-permute-start.35 = (bf16[1,768,128]{2,1,0:T(8,128)(2,1)}, bf16[1,768,128]{2,1,0:T(8,128)(2,1)}, u32[]{:S(2)}, u32[]{:S(2)}) collective-permute-start(bf16[1,768,128]{2,1,0:T(8,128)(2,1)} %get-tuple-element.329), channel_id=1, source_target_pairs={{0,24},{4,28},{8,16},{12,20},{16,8},{20,12},{24,0},{28,4},{1,25},{... | collective-permute-start | bytes 589832 | tf_op jit(solution)/shard_map/ppermute | solution.py:1176
  259.9 25.7 %collective-permute-start.34 = (bf16[1,528,128]{2,1,0:T(8,128)(2,1)}, bf16[1,528,128]{2,1,0:T(8,128)(2,1)}, u32[]{:S(2)}, u32[]{:S(2)}) collective-permute-start(bf16[1,528,128]{2,1,0:T(8,128)(2,1)} %get-tuple-element.333), channel_id=1, source_target_pairs={{0,4},{4,0},{8,12},{12,8},{16,20},{20,16},{24,28},{28,24},{1,5},{5... | collective-permute-start | bytes 405512 | tf_op jit(solution)/shard_map/ppermute | solution.py:1176
  264.7 21.8 %collective-permute-start.30 = (f32[8,1280]{1,0:T(8,128)S(1)}, f32[8,1280]{1,0:T(8,128)S(1)}, u32[]{:S(2)}, u32[]{:S(2)}) collective-permute-start(f32[8,1280]{1,0:T(8,128)S(1)} %concatenate.37), channel_id=1, source_target_pairs={{0,4},{4,0},{8,12},{12,8},{16,20},{20,16},{24,28},{28,24},{1,5},{5... | collective-permute-start | bytes 122888 | tf_op jit(solution)/shard_map/ppermute | solution.py:1176
  266.6 21.7 %collective-permute-start.40 = (bf16[1,512,128]{2,1,0:T(8,128)(2,1)S(1)}, bf16[1,512,128]{2,1,0:T(8,128)(2,1)S(1)}, u32[]{:S(2)}, u32[]{:S(2)}) collective-permute-start(bf16[1,512,128]{2,1,0:T(8,128)(2,1)S(1)} %fold.15), channel_id=1, source_target_pairs={{0,24},{4,28},{8,16},{12,20},{16,8},{20,12},{24,0},{28,4},{1,25},{... | collective-permute-start | bytes 393224 | tf_op jit(solution)/shard_map/ppermute | solution.py:1176
  272.8 24.4 %collective-permute-start.29 = (bf16[256,1024]{1,0:T(8,128)(2,1)}, bf16[256,1024]{1,0:T(8,128)(2,1)S(1)}, u32[]{:S(2)}, u32[]{:S(2)}) collective-permute-start(bf16[256,1024]{1,0:T(8,128)(2,1)} %get-tuple-element.315), channel_id=1, source_target_pairs={{0,1},{1,0},{2,3},{3,2},{4,5},{5,4},{6,7},{7,6},{8,9},{9,8},{10,11... | collective-permute-start | bytes 1572872 | tf_op jit(solution)/shard_map/ppermute | solution.py:1176
  295.8 15.1 %collective-permute-start.43 = (bf16[2,768,128]{2,1,0:T(8,128)(2,1)S(1)}, bf16[2,768,128]{2,1,0:T(8,128)(2,1)S(1)}, u32[]{:S(2)}, u32[]{:S(2)}) collective-permute-start(bf16[2,768,128]{2,1,0:T(8,128)(2,1)S(1)} %constant_dynamic-update-slice_fusion.2), channel_id=1, source_target_pairs={{0,8},{4,12},{8,0},{12,4},{16,24},{20,28},{24,16},{28,20},{1,9},{5... | collective-permute-start | bytes 1179656 | tf_op jit(solution)/shard_map/ppermute | solution.py:1176
  296.0 21.3 %collective-permute-start.42 = (bf16[2,528,128]{2,1,0:T(8,128)(2,1)S(1)}, bf16[2,528,128]{2,1,0:T(8,128)(2,1)S(1)}, u32[]{:S(2)}, u32[]{:S(2)}) collective-permute-start(bf16[2,528,128]{2,1,0:T(8,128)(2,1)S(1)} %constant_dynamic-update-slice_fusion.4), channel_id=1, source_target_pairs={{0,24},{4,28},{8,16},{12,20},{16,8},{20,12},{24,0},{28,4},{1,25},{... | collective-permute-start | bytes 811016 | tf_op jit(solution)/shard_map/ppermute | solution.py:1176
  297.2 20.2 %collective-permute-start.41 = (f32[8,1280]{1,0:T(8,128)S(1)}, f32[8,1280]{1,0:T(8,128)S(1)}, u32[]{:S(2)}, u32[]{:S(2)}) collective-permute-start(f32[8,1280]{1,0:T(8,128)S(1)} %add.61), channel_id=1, source_target_pairs={{0,16},{4,20},{8,24},{12,28},{16,0},{20,4},{24,8},{28,12},{1,17},{... | collective-permute-start | bytes 122888 | tf_op jit(solution)/shard_map/ppermute | solution.py:1176
  303.5 23.8 %collective-permute-start.49 = (bf16[4,512,128]{2,1,0:T(8,128)(2,1)S(1)}, bf16[4,512,128]{2,1,0:T(8,128)(2,1)S(1)}, u32[]{:S(2)}, u32[]{:S(2)}) collective-permute-start(bf16[4,512,128]{2,1,0:T(8,128)(2,1)S(1)} %constant_dynamic-update-slice_fusion.6.mine), channel_id=1, source_target_pairs={{0,4},{4,0},{8,12},{12,8},{16,20},{20,16},{24,28},{28,24},{1,5},{5... | collective-permute-start | bytes 1572872 | tf_op jit(solution)/shard_map/ppermute | solution.py:1176
  311.0 19.6 %collective-permute-start.47 = (bf16[4,768,128]{2,1,0:T(8,128)(2,1)S(1)}, bf16[4,768,128]{2,1,0:T(8,128)(2,1)S(1)}, u32[]{:S(2)}, u32[]{:S(2)}) collective-permute-start(bf16[4,768,128]{2,1,0:T(8,128)(2,1)S(1)} %constant_dynamic-update-slice_fusion.8.mine), channel_id=1, source_target_pairs={{0,4},{4,0},{8,12},{12,8},{16,20},{20,16},{24,28},{28,24},{1,5},{5... | collective-permute-start | bytes 2359304 | tf_op jit(solution)/shard_map/ppermute | solution.py:1176
  317.3 11.7 %collective-permute-start.48 = (bf16[4,528,128]{2,1,0:T(8,128)(2,1)S(1)}, bf16[4,528,128]{2,1,0:T(8,128)(2,1)S(1)}, u32[]{:S(2)}, u32[]{:S(2)}) collective-permute-start(bf16[4,528,128]{2,1,0:T(8,128)(2,1)S(1)} %constant_dynamic-update-slice_fusion.10.mine), channel_id=1, source_target_pairs={{0,8},{4,12},{8,0},{12,4},{16,24},{20,28},{24,16},{28,20},{1,9},{5... | collective-permute-start | bytes 1622024 | tf_op jit(solution)/shard_map/ppermute | solution.py:1176
  (77 other events, 1068.7 us)
Sparse Core Ops, SparseCore 0:
  124.3 105.5 all-reduce.5

commit v4 on v3

--- a/solution.py
+++ b/solution.py
@@ -17,7 +17,7 @@
 HBM = pltpu.HBM
 VMEM_LIMIT = 60 * 1024 * 1024
 SMALL_LIMIT = 24 * 1024 * 1024
-EARLY = 16
+EARLY = 64
 SEQ = ("far", "near")
 
 
@@ -228,7 +228,7 @@
 
     strict = order_r > order_c
     eye = (lower_r == lower_c).astype(F32)
-    together = 2
+    together = 4
 
     def part_chunks(step, _):
         jobs = []
@@ -694,6 +694,7 @@
 
 PARTNER = {"x": 1, "pair": 2, "cross": 6}
 X_FIRST = ("x", "pair", "cross")
+V_BACK = ("x", "cross", "pair")
 Z_FIRST = ("pair", "cross", "x")
 
 
@@ -1096,8 +1097,9 @@
 
 
 class Sum:
-    def __init__(self, line, order, give, keep):
+    def __init__(self, line, order, give, keep, back=None):
         self.line, self.order, self.keep, self.at = line, order, keep, 0
+        self.back = order[::-1] if back is None else back
         self.got = swapped(give, SEQ, PARTNER[order[0]])
 
     def next(self):
@@ -1118,20 +1120,22 @@
         else:
             mine = self.line.step(lambda *parts: jnp.concatenate(parts, axis=0), self.keep, self.got)
         self.keep = mine
-        self.got = swapped(mine, SEQ, PARTNER[self.order[2 * stages - 1 - self.at]])
+        self.got = swapped(mine, SEQ, PARTNER[self.back[self.at - stages]])
 
     def finish(self, kernel, name, outs):
         return self.line.step(
-            lambda *parts: call(functools.partial(kernel, self.order), name, outs, list(parts)), self.keep, self.got
+            lambda *parts: call(functools.partial(kernel, (self.order, self.back)), name, outs, list(parts)), self.keep, self.got
         )
 
 
-def blocks_of(order, mine, other):
+def blocks_of(orders, mine, other):
+    order, back = orders
     bits = seq_bits()
-    first, second, third = (bits[stage] for stage in order)
-    for flip, ref in ((0, mine), (1, other)):
+    for last, ref in ((0, mine), (1, other)):
         for slot in range(4):
-            yield 4 * (first ^ flip) + 2 * (second ^ (slot // 2)) + (third ^ (slot % 2)), ref, slot
+            flips = dict(zip(back, (slot % 2, slot // 2, last)))
+            first, second, third = (bits[stage] ^ flips[stage] for stage in order)
+            yield 4 * first + 2 * second + third, ref, slot
 
 
 def at_block(index):
@@ -1265,8 +1269,9 @@
         line, X_FIRST, *line.step(functools.partial(mix_weights, X_FIRST[0]), normed, normed_halo, d_kq, halo_kq)
     )
     sum_v = Sum(
-        line, Z_FIRST,
-        *line.step(functools.partial(mix_weights, Z_FIRST[0]), normed, normed_halo, d_v, d_halo[:, cut_v], grad_small),
+        line, X_FIRST,
+        *line.step(functools.partial(mix_weights, X_FIRST[0]), normed, normed_halo, d_v, d_halo[:, cut_v], grad_small),
+        back=V_BACK,
     )
     taps = conv_q.shape[0]
 
@@ -1274,7 +1279,7 @@
         joined = jnp.concatenate(rows, axis=1)
         return jnp.pad(joined, ((0, 0), (0, width - joined.shape[1])))
 
-    for part in (sum_out, sum_kq, sum_v):
+    for part in (sum_kq, sum_out, sum_v):
         part.next()
     mine, other = head_sum(
         *line.step(
@@ -1282,7 +1287,8 @@
             q_weight, k_weight, v_weight, outgate_weight, beta_rows, decay_rows,
         )
     )
-    for part in (sum_out, sum_kq, sum_v):
+    line.last = feed_sums
+    for part in (sum_kq, sum_out, sum_v):
         part.next()
     line.last = feed_sums
     input_own, grad_attn_gain = line.step(finish, mine, other, block_in, attn_gain, d_hidden)
@@ -1294,19 +1300,19 @@
         ],
         axis=0,
     )
-    small_got = swapped(small_sums, SEQ, 1)
-    bit = 2
-    rounds = 3
-    while small_got is not None or rounds > 0:
-        if rounds == 1:
+    bits = [1 << k for k in range(1, seq_size().bit_length() - 1)] + [1]
+    small_got = swapped(small_sums, SEQ, bits[0])
+    rounds = 0
+    while rounds < max(3, len(bits)):
+        if rounds == 2:
             line.last = feed_near
-        for part in (sum_out, sum_kq, sum_v) if rounds > 0 else ():
+        for part in (sum_kq, sum_out, sum_v) if rounds < 3 else ():
             part.next()
-        rounds -= 1
-        if small_got is not None:
+        rounds += 1
+        if rounds <= len(bits):
             small_sums = line.step(jnp.add, small_sums, small_got)
-            small_got = swapped(small_sums, SEQ, bit) if bit < seq_size() else None
-            bit *= 2
+        if rounds < len(bits):
+            small_got = swapped(small_sums, SEQ, bits[rounds])
     gains = small_sums[taps + 1 : taps + 4]
     gains = gains + swapped(gains, "head", 1)
     grad_o_gain = gains[2:3, :LANES]

time: 341 us -> 319 us (0.935)
  waiting for transfers between devices: 119 us -> 101 us
  Pallas kernels: 95.4 us -> 88.7 us
  starting transfers between devices: 78 us -> 81.7 us
    ppermute x41, waiting for transfers between devices: 109 us -> 85.9 us  [swapped(): lax.ppermute(value, axis, [(s, s ^ bit) for s in range(seq_size() if axis...]
    psum x1, waiting for transfers between devices: 0.01 us -> 4.26 us  [local(): feed_sums = lax.psum(feed_grads, 'far')]
    pallas_call x1, Pallas kernels: 22 us -> 18.1 us  [mixer_prep(): pl.pallas_call(functools.partial(prep_kernel, heads), out_shape=outs, in_...]
    ppermute x41, starting transfers between devices: 52.1 us -> 55.8 us  [swapped(): lax.ppermute(value, axis, [(s, s ^ bit) for s in range(seq_size() if axis...]
  transfers between devices with their start and end apart: 52 -> 52, of which waited for: 22 -> 25; matrix products, arithmetic and copies ran while one was open for 6% -> 6% of each run, Pallas kernels for 24% -> 23%
where the time goes in v4:
time: 319 us; the launch traced here: 318 us
  waiting for transfers between devices  101 us (32%)
  Pallas kernels  88.7 us (28%)
  starting transfers between devices  81.7 us (26%)
  local copies, waits for them, and re-layouts  19.2 us (6%)
  between operations  14.9 us (5%)
  other arithmetic  12.2 us (4%)
    ppermute x41, waiting for transfers between devices, swapped(): lax.ppermute(value, axis, [(s, s ^ bit) for s in range(seq_size() if axis...  85.9 us
    ppermute x41, starting transfers between devices, swapped(): lax.ppermute(value, axis, [(s, s ^ bit) for s in range(seq_size() if axis...  55.8 us
    pallas_call x24, Pallas kernels, call(): pl.pallas_call(kernel, out_shape=outs, in_specs=specs(smem, pltpu.SMEM) +...  36.4 us
    pallas_call x1, Pallas kernels, mixer_back(): pl.pallas_call(functools.partial(back_kernel, heads, reach), out_shape=ou...  27.2 us
    ppermute x10, starting transfers between devices, shifted(): lax.ppermute(value, axis, [(source, source + steps) for source in range(l...  25.9 us
    pallas_call x1, Pallas kernels, mixer_prep(): pl.pallas_call(functools.partial(prep_kernel, heads), out_shape=outs, in_...  18.1 us
    unnamed x120, local copies, waits for them, and re-layouts  11.9 us
    ppermute x10, waiting for transfers between devices, shifted(): lax.ppermute(value, axis, [(source, source + steps) for source in range(l...  10.9 us
  transfers between devices with their start and end apart: 52, of which 25 were waited for; matrix products, arithmetic and copies ran while one was open for 6% of the time, Pallas kernels for 23%

profile of v4, /device:TPU:0, one launch (start us, length us, event | category | flops | bytes accessed | tf_op | source)
XLA Modules:
  0.0 317.8 jit_solution(15940267772881803686)
XLA Ops:
  7.2 7.0 %project.1 = (bf16[512,1024]{1,0:T(8,128)(2,1)}, bf16[512,1280]{1,0:T(8,128)(2,1)}, f32[512,256]{1,0:T(8,128)}, f32[512,128]{1,0:T(8,128)}, bf16[16,2304]{1,0:T(8,128)(2,1)}) custom-call(bf16[512,1024]{1,0:T(8,128)(2,1)} %x.10, f32[1,1024]{1,0:T(1,128)} %bitcast.30, bf16[1024,256]{1,0:T(8,128)(2,1)} %q_w, bf16[1024,512]{1,0:T(8,128)(2,1)} %k_w, ...), custom_call_target="tpu_custom_call" | custom-call | flops 5368709120 | bytes 4194304 | tf_op jit(solution)/shard_map/project/pallas_call | solution.py:754
  14.2 4.8 %collective-permute-start = (bf16[16,2304]{1,0:T(8,128)(2,1)}, bf16[16,2304]{1,0:T(8,128)(2,1)S(1)}, u32[]{:S(2)}, u32[]{:S(2)}) collective-permute-start(bf16[16,2304]{1,0:T(8,128)(2,1)} %get-tuple-element.199), channel_id=1, source_target_pairs={{0,4},{4,8},{8,12},{12,16},{16,20},{20,24},{24,28},{1,5},{5,9},{9,... | collective-permute-start | bytes 221192 | tf_op jit(solution)/shard_map/ppermute | solution.py:1176
  22.6 18.1 %mixer_prep.1 = (f32[2,512,256]{2,1,0:T(8,128)}, bf16[2,8,128,256]{3,2,1,0:T(8,128)(2,1)}, bf16[2,8,128,128]{3,2,1,0:T(8,128)(2,1)}, bf16[2,8,128,128]{3,2,1,0:T...) custom-call(s32[10]{0:T(128)} %starts.3, ...), custom_call_target="tpu_custom_call" | custom-call | flops 24000000000 | bytes 4000000 | tf_op jit(solution)/shard_map/mixer_prep/pallas_call | solution.py:335
  41.8 4.3 %collective-permute-start.2 = (bf16[2,2,128,128]{3,2,1,0:T(8,128)(2,1)S(1)}, bf16[2,2,128,128]{3,2,1,0:T(8,128)(2,1)S(1)}, u32[]{:S(2)}, u32[]{:S(2)}) collective-permute-start(bf16[2,2,128,128]{3,2,1,0:T(8,128)(2,1)S(1)} %pad_maximum_fusion.2), channel_id=1, source_target_pairs={{0,4},{4,8},{8,12},{12,16},{16,20},{20,24},{24,28},{1,5},{5,9},{9,... | collective-permute-start | bytes 393224 | tf_op jit(solution)/shard_map/ppermute | solution.py:1176
  46.1 3.5 %collective-permute-start.3 = (bf16[2,2,128,128]{3,2,1,0:T(8,128)(2,1)S(1)}, bf16[2,2,128,128]{3,2,1,0:T(8,128)(2,1)S(1)}, u32[]{:S(2)}, u32[]{:S(2)}) collective-permute-start(bf16[2,2,128,128]{3,2,1,0:T(8,128)(2,1)S(1)} %pad_maximum_fusion.2), channel_id=1, source_target_pairs={{0,8},{4,12},{8,16},{12,20},{16,24},{20,28},{1,9},{5,13},{9,17},{1... | collective-permute-start | bytes 393224 | tf_op jit(solution)/shard_map/ppermute | solution.py:1176
  49.6 4.9 %collective-permute-start.4 = (bf16[1,2,128,128]{3,2,1,0:T(8,128)(2,1)}, bf16[1,2,128,128]{3,2,1,0:T(8,128)(2,1)S(1)}, u32[]{:S(2)}, u32[]{:S(2)}) collective-permute-start(bf16[1,2,128,128]{3,2,1,0:T(8,128)(2,1)} %bitcast.38), channel_id=1, source_target_pairs={{0,12},{4,16},{8,20},{12,24},{16,28},{1,13},{5,17},{9,21},{13,25},... | collective-permute-start | bytes 196616 | tf_op jit(solution)/shard_map/ppermute | solution.py:1176
  63.9 12.4 %collective-permute-done.6.other = bf16[256,1024]{1,0:T(8,128)(2,1)S(1)} collective-permute-done((bf16[256,1024]{1,0:T(8,128)(2,1)S(1)}, bf16[256,1024]{1,0:T(8,128)(2,1)S(1)}, u32[]{:S(2)}, u32[]{:S(2)}) %collective-permute-start.6) | collective-permute-done | bytes 524320 | tf_op jit(solution)/shard_map/ppermute | solution.py:1180
  78.7 7.2 %feed.1 = (bf16[512,1024]{1,0:T(8,128)(2,1)S(1)}, bf16[1056,512]{1,0:T(8,128)(2,1)S(1)}, bf16[1056,512]{1,0:T(8,128)(2,1)S(1)}, bf16[256,1024]{1,0:T(8,128)(2,1)...) custom-call(bf16[256,1024]{1,0:T(8,128)(2,1)S(1)} %get-tuple-element.209.own, ...), custom_call_target="tpu_custom_call" | custom-call | flops 69206016 | bytes 199680 | tf_op jit(solution)/shard_map/feed/pallas_call | solution.py:666
  86.0 5.1 %collective-permute-done.14.normed_mine = bf16[256,1024]{1,0:T(8,128)(2,1)S(1)} collective-permute-done((bf16[256,1024]{1,0:T(8,128)(2,1)S(1)}, bf16[256,1024]{1,0:T(8,128)(2,1)S(1)}, u32[]{:S(2)}, u32[]{:S(2)}) %collective-permute-start.14) | collective-permute-done | bytes 524320 | tf_op jit(solution)/shard_map/ppermute | solution.py:1180
  94.2 11.7 %collective-permute-done.12.other = bf16[256,1024]{1,0:T(8,128)(2,1)S(1)} collective-permute-done((bf16[256,1024]{1,0:T(8,128)(2,1)S(1)}, bf16[256,1024]{1,0:T(8,128)(2,1)S(1)}, u32[]{:S(2)}, u32[]{:S(2)}) %collective-permute-start.12) | collective-permute-done | bytes 524320 | tf_op jit(solution)/shard_map/ppermute | solution.py:1180
  112.2 4.3 %collective-permute-done.15.d_near = bf16[1056,512]{1,0:T(8,128)(2,1)S(1)} collective-permute-done((bf16[1056,512]{1,0:T(8,128)(2,1)S(1)}, bf16[1056,512]{1,0:T(8,128)(2,1)S(1)}, u32[]{:S(2)}, u32[]{:S(2)}) %collective-permute-start.15) | collective-permute-done | bytes 1081376 | tf_op jit(solution)/shard_map/ppermute | solution.py:1180
  116.5 3.7 %feed_weights.1 = bf16[1056,1024]{1,0:T(8,128)(2,1)} custom-call(bf16[1056,512]{1,0:T(8,128)(2,1)S(1)} %get-tuple-element.253.d_own, bf16[512,1024]{1,0:T(8,128)(2,1)S(1)} %get-tuple-element.254.normed, bf16[512,1024]{1,0:T(8,128)(2,1)S(1)} %copy-done, bf16[1056,512]{1,0:T(8,128)(2,1)S(1)} %collective-permute-done.15.d_near, ...), custom_call_target="tpu_custom_call" | custom-call | flops 34603008 | bytes 133120 | tf_op jit(solution)/shard_map/feed_weights/pallas_call | solution.py:666
  132.1 2.7 collective-permute-start.25
  134.8 4.9 %collective-permute-done.19.rest_1_ = bf16[2,128,128]{2,1,0:T(8,128)(2,1)S(1)} collective-permute-done((bf16[2,128,128]{2,1,0:T(8,128)(2,1)S(1)}, bf16[2,128,128]{2,1,0:T(8,128)(2,1)S(1)}, u32[]{:S(2)}, u32[]{:S(2)}) %collective-permute-start.19) | collective-permute-done | bytes 65568 | tf_op jit(solution)/shard_map/ppermute | solution.py:1176
  142.2 27.2 %mixer_back.1 = (bf16[512,768]{1,0:T(8,128)(2,1)}, bf16[512,512]{1,0:T(8,128)(2,1)}, f32[16,1280]{1,0:T(8,128)}, f32[8,1280]{1,0:T(8,128)}, bf16[512,128]{1,0:T(...) custom-call(s32[10]{0:T(128)} %starts.3, f32[2]{0:T(128)} %log_rate.3, f32[2]{0:T(128)} %bias.3, ...), custom_call_target="tpu_custom_call" | custom-call | flops 2000000000 | bytes 4000000 | tf_op jit(solution)/shard_map/mixer_back/pallas_call | solution.py:639
  173.5 9.8 %collective-permute-start.26 = (bf16[4,768,128]{2,1,0:T(8,128)(2,1)S(1)}, bf16[4,768,128]{2,1,0:T(8,128)(2,1)S(1)}, u32[]{:S(2)}, u32[]{:S(2)}) collective-permute-start(bf16[4,768,128]{2,1,0:T(8,128)(2,1)S(1)} %get-tuple-element.277), channel_id=1, source_target_pairs={{0,4},{4,0},{8,12},{12,8},{16,20},{20,16},{24,28},{28,24},{1,5},{5... | collective-permute-start | bytes 2359304 | tf_op jit(solution)/shard_map/ppermute | solution.py:1180
  189.1 12.4 %collective-permute-done.26.got = bf16[4,768,128]{2,1,0:T(8,128)(2,1)S(1)} collective-permute-done((bf16[4,768,128]{2,1,0:T(8,128)(2,1)S(1)}, bf16[4,768,128]{2,1,0:T(8,128)(2,1)S(1)}, u32[]{:S(2)}, u32[]{:S(2)}) %collective-permute-start.26) | collective-permute-done | bytes 786464 | tf_op jit(solution)/shard_map/ppermute | solution.py:1180
  204.3 2.9 collective-permute-done.24.got
  211.5 4.3 %all-reduce.6.cloned.1.call-done.mine = bf16[1056,1024]{1,0:T(8,128)(2,1)} async-done(((bf16[1056,1024]{1,0:T(8,128)(2,1)}), bf16[1056,1024]{1,0:T(8,128)(2,1)}) %all-reduce.6.cloned.1.call-update) | async-done | bytes 2162704 | tf_op jit(solution)/shard_map/psum | solution.py:1257
  216.4 2.3 add_convert_fusion.mine
  220.3 2.3 broadcast_select_fusion.3
  225.8 2.5 collective-permute-start.36
  229.0 3.4 %collective-permute-done.28.other = bf16[256,1024]{1,0:T(8,128)(2,1)} collective-permute-done((bf16[256,1024]{1,0:T(8,128)(2,1)}, bf16[256,1024]{1,0:T(8,128)(2,1)}, u32[]{:S(2)}, u32[]{:S(2)}) %collective-permute-start.28) | collective-permute-done | bytes 524320 | tf_op jit(solution)/shard_map/ppermute | solution.py:1180
  235.1 7.3 %collective-permute-done.36.got = bf16[1,768,128]{2,1,0:T(8,128)(2,1)S(1)} collective-permute-done((bf16[1,768,128]{2,1,0:T(8,128)(2,1)S(1)}, bf16[1,768,128]{2,1,0:T(8,128)(2,1)S(1)}, u32[]{:S(2)}, u32[]{:S(2)}) %collective-permute-start.36) | collective-permute-done | bytes 196640 | tf_op jit(solution)/shard_map/ppermute | solution.py:1180
  244.9 3.7 %collective-permute-start.35 = (bf16[1,512,128]{2,1,0:T(8,128)(2,1)S(1)}, bf16[1,512,128]{2,1,0:T(8,128)(2,1)S(1)}, u32[]{:S(2)}, u32[]{:S(2)}) collective-permute-start(bf16[1,512,128]{2,1,0:T(8,128)(2,1)S(1)} %get-tuple-element.329), channel_id=1, source_target_pairs={{0,24},{4,28},{8,16},{12,20},{16,8},{20,12},{24,0},{28,4},{1,25},{... | collective-permute-start | bytes 393224 | tf_op jit(solution)/shard_map/ppermute | solution.py:1180
  258.5 7.0 %collective-permute-start.37 = (f32[8,1280]{1,0:T(8,128)S(1)}, f32[8,1280]{1,0:T(8,128)S(1)}, u32[]{:S(2)}, u32[]{:S(2)}) collective-permute-start(f32[8,1280]{1,0:T(8,128)S(1)} %add.60), channel_id=1, source_target_pairs={{0,16},{4,20},{8,24},{12,28},{16,0},{20,4},{24,8},{28,12},{1,17},{... | collective-permute-start | bytes 122888 | tf_op jit(solution)/shard_map/ppermute | solution.py:1180
  274.7 4.0 %collective-permute-done.44 = bf16[2,768,128]{2,1,0:T(8,128)(2,1)S(1)} collective-permute-done((bf16[2,768,128]{2,1,0:T(8,128)(2,1)S(1)}, bf16[2,768,128]{2,1,0:T(8,128)(2,1)S(1)}, u32[]{:S(2)}, u32[]{:S(2)}) %collective-permute-start.44) | collective-permute-done | bytes 393248 | tf_op jit(solution)/shard_map/ppermute | solution.py:1180
  280.3 3.3 %collective-permute-done.43 = bf16[2,512,128]{2,1,0:T(8,128)(2,1)S(1)} collective-permute-done((bf16[2,512,128]{2,1,0:T(8,128)(2,1)S(1)}, bf16[2,512,128]{2,1,0:T(8,128)(2,1)S(1)}, u32[]{:S(2)}, u32[]{:S(2)}) %collective-permute-start.43) | collective-permute-done | bytes 262176 | tf_op jit(solution)/shard_map/ppermute | solution.py:1180
  285.5 4.7 %collective-permute-done.42 = bf16[2,528,128]{2,1,0:T(8,128)(2,1)S(1)} collective-permute-done((bf16[2,528,128]{2,1,0:T(8,128)(2,1)S(1)}, bf16[2,528,128]{2,1,0:T(8,128)(2,1)S(1)}, u32[]{:S(2)}, u32[]{:S(2)}) %collective-permute-start.42) | collective-permute-done | bytes 270368 | tf_op jit(solution)/shard_map/ppermute | solution.py:1180
  292.1 3.9 %feed_out.1 = (f32[704,1024]{1,0:T(8,128)}, f32[704,1024]{1,0:T(8,128)}, f32[704,1024]{1,0:T(8,128)}) custom-call(bf16[1056,1024]{1,0:T(8,128)(2,1)S(1)} %copy-done.7, bf16[1056,1024]{1,0:T(8,128)(2,1)S(1)} %collective-permute-done.45.other), custom_call_target="tpu_custom_call" | custom-call | bytes 202752 | tf_op jit(solution)/shard_map/feed_out/pallas_call | solution.py:666
  296.0 2.6 collective-permute-start.50
  300.6 5.2 %collective-permute-done.49.other = bf16[4,512,128]{2,1,0:T(8,128)(2,1)S(1)} collective-permute-done((bf16[4,512,128]{2,1,0:T(8,128)(2,1)S(1)}, bf16[4,512,128]{2,1,0:T(8,128)(2,1)S(1)}, u32[]{:S(2)}, u32[]{:S(2)}) %collective-permute-start.49) | collective-permute-done | bytes 524320 | tf_op jit(solution)/shard_map/ppermute | solution.py:1180
  (260 shorter events, 99.5 us)
Async XLA Ops:
  7.2 208.6 %all-reduce.6.cloned.1.call-start = ((), (), s32[]{:S(2)}) async-start(), calls=%async_computation | async-start | bytes 4325376 | tf_op jit(solution)/shard_map/psum | solution.py:1257
  19.1 21.6 %collective-permute-start.1 = (bf16[256,1024]{1,0:T(8,128)(2,1)S(1)}, bf16[256,1024]{1,0:T(8,128)(2,1)S(1)}, u32[]{:S(2)}, u32[]{:S(2)}) collective-permute-start(bf16[256,1024]{1,0:T(8,128)(2,1)S(1)} %constant_dynamic-slice_fusion), channel_id=1, source_target_pairs={{0,4},{4,0},{8,12},{12,8},{16,20},{20,16},{24,28},{28,24},{1,5},{5... | collective-permute-start | bytes 1572872 | tf_op jit(solution)/shard_map/ppermute | solution.py:1180
  41.8 14.7 %collective-permute-start.2 = (bf16[2,2,128,128]{3,2,1,0:T(8,128)(2,1)S(1)}, bf16[2,2,128,128]{3,2,1,0:T(8,128)(2,1)S(1)}, u32[]{:S(2)}, u32[]{:S(2)}) collective-permute-start(bf16[2,2,128,128]{3,2,1,0:T(8,128)(2,1)S(1)} %pad_maximum_fusion.2), channel_id=1, source_target_pairs={{0,4},{4,8},{8,12},{12,16},{16,20},{20,24},{24,28},{1,5},{5,9},{9,... | collective-permute-start | bytes 393224 | tf_op jit(solution)/shard_map/ppermute | solution.py:1176
  62.3 14.0 %collective-permute-start.6 = (bf16[256,1024]{1,0:T(8,128)(2,1)S(1)}, bf16[256,1024]{1,0:T(8,128)(2,1)S(1)}, u32[]{:S(2)}, u32[]{:S(2)}) collective-permute-start(bf16[256,1024]{1,0:T(8,128)(2,1)S(1)} %add_convert_fusion.4.mine), channel_id=1, source_target_pairs={{0,2},{1,3},{2,0},{3,1},{4,6},{5,7},{6,4},{7,5},{8,10},{9,11},{10,... | collective-permute-start | bytes 1572872 | tf_op jit(solution)/shard_map/ppermute | solution.py:1180
  76.8 14.3 %collective-permute-start.14 = (bf16[256,1024]{1,0:T(8,128)(2,1)S(1)}, bf16[256,1024]{1,0:T(8,128)(2,1)S(1)}, u32[]{:S(2)}, u32[]{:S(2)}) collective-permute-start(bf16[256,1024]{1,0:T(8,128)(2,1)S(1)} %get-tuple-element.209.own), channel_id=1, source_target_pairs={{0,4},{4,0},{8,12},{12,8},{16,20},{20,16},{24,28},{28,24},{1,5},{5... | collective-permute-start | bytes 1572872 | tf_op jit(solution)/shard_map/ppermute | solution.py:1180
  91.1 25.4 %collective-permute-start.15 = (bf16[1056,512]{1,0:T(8,128)(2,1)S(1)}, bf16[1056,512]{1,0:T(8,128)(2,1)S(1)}, u32[]{:S(2)}, u32[]{:S(2)}) collective-permute-start(bf16[1056,512]{1,0:T(8,128)(2,1)S(1)} %get-tuple-element.250), channel_id=1, source_target_pairs={{0,4},{4,0},{8,12},{12,8},{16,20},{20,16},{24,28},{28,24},{1,5},{5... | collective-permute-start | bytes 3244040 | tf_op jit(solution)/shard_map/ppermute | solution.py:1180
  92.6 13.3 %collective-permute-start.12 = (bf16[256,1024]{1,0:T(8,128)(2,1)S(1)}, bf16[256,1024]{1,0:T(8,128)(2,1)S(1)}, u32[]{:S(2)}, u32[]{:S(2)}) collective-permute-start(bf16[256,1024]{1,0:T(8,128)(2,1)S(1)} %add_convert_fusion.1.mine), channel_id=1, source_target_pairs={{0,2},{1,3},{2,0},{3,1},{4,6},{5,7},{6,4},{7,5},{8,10},{9,11},{10,... | collective-permute-start | bytes 1572872 | tf_op jit(solution)/shard_map/ppermute | solution.py:1180
  123.0 11.8 %collective-permute-start.18 = (bf16[2,128,128]{2,1,0:T(8,128)(2,1)S(1)}, bf16[2,128,128]{2,1,0:T(8,128)(2,1)S(1)}, u32[]{:S(2)}, u32[]{:S(2)}) collective-permute-start(bf16[2,128,128]{2,1,0:T(8,128)(2,1)S(1)} %get-tuple-element.267), channel_id=1, source_target_pairs={{4,0},{8,4},{12,8},{16,12},{20,16},{24,20},{28,24},{5,1},{9,5},{13... | collective-permute-start | bytes 196616 | tf_op jit(solution)/shard_map/ppermute | solution.py:1176
  124.3 15.4 %collective-permute-start.19 = (bf16[2,128,128]{2,1,0:T(8,128)(2,1)S(1)}, bf16[2,128,128]{2,1,0:T(8,128)(2,1)S(1)}, u32[]{:S(2)}, u32[]{:S(2)}) collective-permute-start(bf16[2,128,128]{2,1,0:T(8,128)(2,1)S(1)} %get-tuple-element.267), channel_id=1, source_target_pairs={{8,0},{12,4},{16,8},{20,12},{24,16},{28,20},{9,1},{13,5},{17,9},{2... | collective-permute-start | bytes 196616 | tf_op jit(solution)/shard_map/ppermute | solution.py:1176
  125.6 16.0 %collective-permute-start.20 = (bf16[2,128,128]{2,1,0:T(8,128)(2,1)S(1)}, bf16[2,128,128]{2,1,0:T(8,128)(2,1)S(1)}, u32[]{:S(2)}, u32[]{:S(2)}) collective-permute-start(bf16[2,128,128]{2,1,0:T(8,128)(2,1)S(1)} %get-tuple-element.267), channel_id=1, source_target_pairs={{12,0},{16,4},{20,8},{24,12},{28,16},{13,1},{17,5},{21,9},{25,13},... | collective-permute-start | bytes 196616 | tf_op jit(solution)/shard_map/ppermute | solution.py:1176
  131.4 53.2 %collective-permute-start.8 = (bf16[256,1024]{1,0:T(8,128)(2,1)}, bf16[256,1024]{1,0:T(8,128)(2,1)}, u32[]{:S(2)}, u32[]{:S(2)}) collective-permute-start(bf16[256,1024]{1,0:T(8,128)(2,1)} %get-tuple-element.211), channel_id=1, source_target_pairs={{0,1},{1,0},{2,3},{3,2},{4,5},{5,4},{6,7},{7,6},{8,9},{9,8},{10,11... | collective-permute-start | bytes 1572872 | tf_op jit(solution)/shard_map/ppermute | solution.py:1180
  132.1 70.3 %collective-permute-start.25 = (bf16[4,512,128]{2,1,0:T(8,128)(2,1)}, bf16[4,512,128]{2,1,0:T(8,128)(2,1)}, u32[]{:S(2)}, u32[]{:S(2)}) collective-permute-start(bf16[4,512,128]{2,1,0:T(8,128)(2,1)} %get-tuple-element.265), channel_id=1, source_target_pairs={{0,4},{4,0},{8,12},{12,8},{16,20},{20,16},{24,28},{28,24},{1,5},{5... | collective-permute-start | bytes 1572872 | tf_op jit(solution)/shard_map/ppermute | solution.py:1180
  173.5 27.9 %collective-permute-start.26 = (bf16[4,768,128]{2,1,0:T(8,128)(2,1)S(1)}, bf16[4,768,128]{2,1,0:T(8,128)(2,1)S(1)}, u32[]{:S(2)}, u32[]{:S(2)}) collective-permute-start(bf16[4,768,128]{2,1,0:T(8,128)(2,1)S(1)} %get-tuple-element.277), channel_id=1, source_target_pairs={{0,4},{4,0},{8,12},{12,8},{16,20},{20,16},{24,28},{28,24},{1,5},{5... | collective-permute-start | bytes 2359304 | tf_op jit(solution)/shard_map/ppermute | solution.py:1180
  184.5 22.8 %collective-permute-start.24 = (bf16[4,528,128]{2,1,0:T(8,128)(2,1)S(1)}, bf16[4,528,128]{2,1,0:T(8,128)(2,1)S(1)}, u32[]{:S(2)}, u32[]{:S(2)}) collective-permute-start(bf16[4,528,128]{2,1,0:T(8,128)(2,1)S(1)} %get-tuple-element.284), channel_id=1, source_target_pairs={{0,4},{4,0},{8,12},{12,8},{16,20},{20,16},{24,28},{28,24},{1,5},{5... | collective-permute-start | bytes 1622024 | tf_op jit(solution)/shard_map/ppermute | solution.py:1180
  185.9 24.0 %collective-permute-start.9 = (bf16[256,1024]{1,0:T(8,128)(2,1)S(1)}, bf16[256,1024]{1,0:T(8,128)(2,1)S(1)}, u32[]{:S(2)}, u32[]{:S(2)}) collective-permute-start(bf16[256,1024]{1,0:T(8,128)(2,1)S(1)} %add_convert_fusion.3), channel_id=1, source_target_pairs={{0,2},{1,3},{2,0},{3,1},{4,6},{5,7},{6,4},{7,5},{8,10},{9,11},{10,... | collective-permute-start | bytes 1572872 | tf_op jit(solution)/shard_map/ppermute | solution.py:1180
  187.5 20.2 %collective-permute-start.23 = (f32[8,1280]{1,0:T(8,128)S(1)}, f32[8,1280]{1,0:T(8,128)S(1)}, u32[]{:S(2)}, u32[]{:S(2)}) collective-permute-start(f32[8,1280]{1,0:T(8,128)S(1)} %copy-done.55), channel_id=1, source_target_pairs={{4,0},{8,4},{12,8},{16,12},{20,16},{24,20},{28,24},{5,1},{9,5},{13... | collective-permute-start | bytes 122888 | tf_op jit(solution)/shard_map/ppermute | solution.py:1176
  211.5 13.1 %collective-permute-start.33 = (bf16[2,768,128]{2,1,0:T(8,128)(2,1)}, bf16[2,768,128]{2,1,0:T(8,128)(2,1)}, u32[]{:S(2)}, u32[]{:S(2)}) collective-permute-start(bf16[2,768,128]{2,1,0:T(8,128)(2,1)} %get-tuple-element.289), channel_id=1, source_target_pairs={{0,8},{4,12},{8,0},{12,4},{16,24},{20,28},{24,16},{28,20},{1,9},{5... | collective-permute-start | bytes 1179656 | tf_op jit(solution)/shard_map/ppermute | solution.py:1180
  215.8 62.8 %collective-permute-start.45 = (bf16[1056,1024]{1,0:T(8,128)(2,1)}, bf16[1056,1024]{1,0:T(8,128)(2,1)S(1)}, u32[]{:S(2)}, u32[]{:S(2)}) collective-permute-start(bf16[1056,1024]{1,0:T(8,128)(2,1)} %all-reduce.6.cloned.1.call-done.mine), channel_id=1, source_target_pairs={{0,4},{4,0},{8,12},{12,8},{16,20},{20,16},{24,28},{28,24},{1,5},{5... | collective-permute-start | bytes 6488072 | tf_op jit(solution)/shard_map/ppermute | solution.py:1180
  218.7 13.7 %collective-permute-start.28 = (bf16[256,1024]{1,0:T(8,128)(2,1)}, bf16[256,1024]{1,0:T(8,128)(2,1)}, u32[]{:S(2)}, u32[]{:S(2)}) collective-permute-start(bf16[256,1024]{1,0:T(8,128)(2,1)} %add_convert_fusion.mine), channel_id=1, source_target_pairs={{0,2},{1,3},{2,0},{3,1},{4,6},{5,7},{6,4},{7,5},{8,10},{9,11},{10,... | collective-permute-start | bytes 1572872 | tf_op jit(solution)/shard_map/ppermute | solution.py:1180
  222.6 25.9 %collective-permute-start.31 = (bf16[2,528,128]{2,1,0:T(8,128)(2,1)}, bf16[2,528,128]{2,1,0:T(8,128)(2,1)}, u32[]{:S(2)}, u32[]{:S(2)}) collective-permute-start(bf16[2,528,128]{2,1,0:T(8,128)(2,1)} %copy-done.47), channel_id=1, source_target_pairs={{0,8},{4,12},{8,0},{12,4},{16,24},{20,28},{24,16},{28,20},{1,9},{5... | collective-permute-start | bytes 811016 | tf_op jit(solution)/shard_map/ppermute | solution.py:1180
  222.9 19.9 %collective-permute-start.32 = (bf16[2,512,128]{2,1,0:T(8,128)(2,1)}, bf16[2,512,128]{2,1,0:T(8,128)(2,1)}, u32[]{:S(2)}, u32[]{:S(2)}) collective-permute-start(bf16[2,512,128]{2,1,0:T(8,128)(2,1)} %copy-done.48), channel_id=1, source_target_pairs={{0,8},{4,12},{8,0},{12,4},{16,24},{20,28},{24,16},{28,20},{1,9},{5... | collective-permute-start | bytes 786440 | tf_op jit(solution)/shard_map/ppermute | solution.py:1180
  225.8 16.6 %collective-permute-start.36 = (bf16[1,768,128]{2,1,0:T(8,128)(2,1)S(1)}, bf16[1,768,128]{2,1,0:T(8,128)(2,1)S(1)}, u32[]{:S(2)}, u32[]{:S(2)}) collective-permute-start(bf16[1,768,128]{2,1,0:T(8,128)(2,1)S(1)} %get-tuple-element.326), channel_id=1, source_target_pairs={{0,24},{4,28},{8,16},{12,20},{16,8},{20,12},{24,0},{28,4},{1,25},{... | collective-permute-start | bytes 589832 | tf_op jit(solution)/shard_map/ppermute | solution.py:1180
  242.4 16.1 %collective-permute-start.40 = (bf16[1,768,128]{2,1,0:T(8,128)(2,1)S(1)}, bf16[1,768,128]{2,1,0:T(8,128)(2,1)}, u32[]{:S(2)}, u32[]{:S(2)}) collective-permute-start(bf16[1,768,128]{2,1,0:T(8,128)(2,1)S(1)} %fold.15), channel_id=1, source_target_pairs={{0,24},{4,28},{8,16},{12,20},{16,8},{20,12},{24,0},{28,4},{1,25},{... | collective-permute-start | bytes 589832 | tf_op jit(solution)/shard_map/ppermute | solution.py:1180
  242.8 14.1 %collective-permute-start.30 = (f32[8,1280]{1,0:T(8,128)S(1)}, f32[8,1280]{1,0:T(8,128)S(1)}, u32[]{:S(2)}, u32[]{:S(2)}) collective-permute-start(f32[8,1280]{1,0:T(8,128)S(1)} %concatenate.37), channel_id=1, source_target_pairs={{0,8},{4,12},{8,0},{12,4},{16,24},{20,28},{24,16},{28,20},{1,9},{5... | collective-permute-start | bytes 122888 | tf_op jit(solution)/shard_map/ppermute | solution.py:1180
  254.2 17.7 %collective-permute-start.29 = (bf16[256,1024]{1,0:T(8,128)(2,1)S(1)}, bf16[256,1024]{1,0:T(8,128)(2,1)S(1)}, u32[]{:S(2)}, u32[]{:S(2)}) collective-permute-start(bf16[256,1024]{1,0:T(8,128)(2,1)S(1)} %copy-done.27), channel_id=1, source_target_pairs={{0,1},{1,0},{2,3},{3,2},{4,5},{5,4},{6,7},{7,6},{8,9},{9,8},{10,11... | collective-permute-start | bytes 1572872 | tf_op jit(solution)/shard_map/ppermute | solution.py:1180
  266.5 12.1 %collective-permute-start.44 = (bf16[2,768,128]{2,1,0:T(8,128)(2,1)S(1)}, bf16[2,768,128]{2,1,0:T(8,128)(2,1)S(1)}, u32[]{:S(2)}, u32[]{:S(2)}) collective-permute-start(bf16[2,768,128]{2,1,0:T(8,128)(2,1)S(1)} %constant_dynamic-update-slice_fusion), channel_id=1, source_target_pairs={{0,8},{4,12},{8,0},{12,4},{16,24},{20,28},{24,16},{28,20},{1,9},{5... | collective-permute-start | bytes 1179656 | tf_op jit(solution)/shard_map/ppermute | solution.py:1180
  268.5 15.1 %collective-permute-start.43 = (bf16[2,512,128]{2,1,0:T(8,128)(2,1)S(1)}, bf16[2,512,128]{2,1,0:T(8,128)(2,1)S(1)}, u32[]{:S(2)}, u32[]{:S(2)}) collective-permute-start(bf16[2,512,128]{2,1,0:T(8,128)(2,1)S(1)} %constant_dynamic-update-slice_fusion.2), channel_id=1, source_target_pairs={{0,8},{4,12},{8,0},{12,4},{16,24},{20,28},{24,16},{28,20},{1,9},{5... | collective-permute-start | bytes 786440 | tf_op jit(solution)/shard_map/ppermute | solution.py:1180
  269.7 20.4 %collective-permute-start.42 = (bf16[2,528,128]{2,1,0:T(8,128)(2,1)S(1)}, bf16[2,528,128]{2,1,0:T(8,128)(2,1)S(1)}, u32[]{:S(2)}, u32[]{:S(2)}) collective-permute-start(bf16[2,528,128]{2,1,0:T(8,128)(2,1)S(1)} %constant_dynamic-update-slice_fusion.4), channel_id=1, source_target_pairs={{0,24},{4,28},{8,16},{12,20},{16,8},{20,12},{24,0},{28,4},{1,25},{... | collective-permute-start | bytes 811016 | tf_op jit(solution)/shard_map/ppermute | solution.py:1180
  272.0 18.3 %collective-permute-start.41 = (f32[8,1280]{1,0:T(8,128)S(1)}, f32[8,1280]{1,0:T(8,128)S(1)}, u32[]{:S(2)}, u32[]{:S(2)}) collective-permute-start(f32[8,1280]{1,0:T(8,128)S(1)} %add.61), channel_id=1, source_target_pairs={{0,4},{4,0},{8,12},{12,8},{16,20},{20,16},{24,28},{28,24},{1,5},{5... | collective-permute-start | bytes 122888 | tf_op jit(solution)/shard_map/ppermute | solution.py:1180
  278.7 30.3 %collective-permute-start.47 = (bf16[4,768,128]{2,1,0:T(8,128)(2,1)S(1)}, bf16[4,768,128]{2,1,0:T(8,128)(2,1)S(1)}, u32[]{:S(2)}, u32[]{:S(2)}) collective-permute-start(bf16[4,768,128]{2,1,0:T(8,128)(2,1)S(1)} %constant_dynamic-update-slice_fusion.6.mine), channel_id=1, source_target_pairs={{0,4},{4,0},{8,12},{12,8},{16,20},{20,16},{24,28},{28,24},{1,5},{5... | collective-permute-start | bytes 2359304 | tf_op jit(solution)/shard_map/ppermute | solution.py:1180
  283.7 22.2 %collective-permute-start.49 = (bf16[4,512,128]{2,1,0:T(8,128)(2,1)S(1)}, bf16[4,512,128]{2,1,0:T(8,128)(2,1)S(1)}, u32[]{:S(2)}, u32[]{:S(2)}) collective-permute-start(bf16[4,512,128]{2,1,0:T(8,128)(2,1)S(1)} %constant_dynamic-update-slice_fusion.8.mine), channel_id=1, source_target_pairs={{0,4},{4,0},{8,12},{12,8},{16,20},{20,16},{24,28},{28,24},{1,5},{5... | collective-permute-start | bytes 1572872 | tf_op jit(solution)/shard_map/ppermute | solution.py:1180
  290.2 17.2 %collective-permute-start.48 = (bf16[4,528,128]{2,1,0:T(8,128)(2,1)S(1)}, bf16[4,528,128]{2,1,0:T(8,128)(2,1)S(1)}, u32[]{:S(2)}, u32[]{:S(2)}) collective-permute-start(bf16[4,528,128]{2,1,0:T(8,128)(2,1)S(1)} %constant_dynamic-update-slice_fusion.10.mine), channel_id=1, source_target_pairs={{0,8},{4,12},{8,0},{12,4},{16,24},{20,28},{24,16},{28,20},{1,9},{5... | collective-permute-start | bytes 1622024 | tf_op jit(solution)/shard_map/ppermute | solution.py:1180
  (77 other events, 824.2 us)
Sparse Core Ops, SparseCore 0:
  120.4 95.3 all-reduce.5

commit v5 on v4

--- a/solution.py
+++ b/solution.py
@@ -1287,7 +1287,6 @@
             q_weight, k_weight, v_weight, outgate_weight, beta_rows, decay_rows,
         )
     )
-    line.last = feed_sums
     for part in (sum_kq, sum_out, sum_v):
         part.next()
     line.last = feed_sums

time: 319 us -> 317 us (level)
    unnamed x120 -> x116, local copies, waits for them, and re-layouts: 11.9 us -> 10.2 us
where the time goes in v5:
time: 317 us; the launch traced here: 316 us
  waiting for transfers between devices  102 us (32%)
  Pallas kernels  87.6 us (28%)
  starting transfers between devices  81.1 us (26%)
  local copies, waits for them, and re-layouts  17.8 us (6%)
  between operations  14.9 us (5%)
  other arithmetic  13.1 us (4%)
    ppermute x41, waiting for transfers between devices, swapped(): lax.ppermute(value, axis, [(s, s ^ bit) for s in range(seq_size() if axis...  86.3 us
    ppermute x41, starting transfers between devices, swapped(): lax.ppermute(value, axis, [(s, s ^ bit) for s in range(seq_size() if axis...  55.2 us
    pallas_call x24, Pallas kernels, call(): pl.pallas_call(kernel, out_shape=outs, in_specs=specs(smem, pltpu.SMEM) +...  35.3 us
    pallas_call x1, Pallas kernels, mixer_back(): pl.pallas_call(functools.partial(back_kernel, heads, reach), out_shape=ou...  27.2 us
    ppermute x10, starting transfers between devices, shifted(): lax.ppermute(value, axis, [(source, source + steps) for source in range(l...  25.9 us
    pallas_call x1, Pallas kernels, mixer_prep(): pl.pallas_call(functools.partial(prep_kernel, heads), out_shape=outs, in_...  18.1 us
    ppermute x10, waiting for transfers between devices, shifted(): lax.ppermute(value, axis, [(source, source + steps) for source in range(l...  10.9 us
    unnamed x116, local copies, waits for them, and re-layouts  10.2 us
  transfers between devices with their start and end apart: 52, of which 25 were waited for; matrix products, arithmetic and copies ran while one was open for 6% of the time, Pallas kernels for 23%

profile of v5, /device:TPU:0, one launch (start us, length us, event | category | flops | bytes accessed | tf_op | source)
XLA Modules:
  0.0 316.1 jit_solution(3066911432499724925)
XLA Ops:
  7.2 7.0 %project.1 = (bf16[512,1024]{1,0:T(8,128)(2,1)}, bf16[512,1280]{1,0:T(8,128)(2,1)}, f32[512,256]{1,0:T(8,128)}, f32[512,128]{1,0:T(8,128)}, bf16[16,2304]{1,0:T(8,128)(2,1)}) custom-call(bf16[512,1024]{1,0:T(8,128)(2,1)} %x.10, f32[1,1024]{1,0:T(1,128)} %bitcast.30, bf16[1024,256]{1,0:T(8,128)(2,1)} %q_w, bf16[1024,512]{1,0:T(8,128)(2,1)} %k_w, ...), custom_call_target="tpu_custom_call" | custom-call | flops 5368709120 | bytes 4194304 | tf_op jit(solution)/shard_map/project/pallas_call | solution.py:754
  14.2 4.8 %collective-permute-start = (bf16[16,2304]{1,0:T(8,128)(2,1)}, bf16[16,2304]{1,0:T(8,128)(2,1)S(1)}, u32[]{:S(2)}, u32[]{:S(2)}) collective-permute-start(bf16[16,2304]{1,0:T(8,128)(2,1)} %get-tuple-element.199), channel_id=1, source_target_pairs={{0,4},{4,8},{8,12},{12,16},{16,20},{20,24},{24,28},{1,5},{5,9},{9,... | collective-permute-start | bytes 221192 | tf_op jit(solution)/shard_map/ppermute | solution.py:1176
  22.6 18.1 %mixer_prep.1 = (f32[2,512,256]{2,1,0:T(8,128)}, bf16[2,8,128,256]{3,2,1,0:T(8,128)(2,1)}, bf16[2,8,128,128]{3,2,1,0:T(8,128)(2,1)}, bf16[2,8,128,128]{3,2,1,0:T...) custom-call(s32[10]{0:T(128)} %starts.3, ...), custom_call_target="tpu_custom_call" | custom-call | flops 24000000000 | bytes 4000000 | tf_op jit(solution)/shard_map/mixer_prep/pallas_call | solution.py:335
  41.8 4.3 %collective-permute-start.2 = (bf16[2,2,128,128]{3,2,1,0:T(8,128)(2,1)S(1)}, bf16[2,2,128,128]{3,2,1,0:T(8,128)(2,1)S(1)}, u32[]{:S(2)}, u32[]{:S(2)}) collective-permute-start(bf16[2,2,128,128]{3,2,1,0:T(8,128)(2,1)S(1)} %pad_maximum_fusion.2), channel_id=1, source_target_pairs={{0,4},{4,8},{8,12},{12,16},{16,20},{20,24},{24,28},{1,5},{5,9},{9,... | collective-permute-start | bytes 393224 | tf_op jit(solution)/shard_map/ppermute | solution.py:1176
  46.1 3.5 %collective-permute-start.3 = (bf16[2,2,128,128]{3,2,1,0:T(8,128)(2,1)S(1)}, bf16[2,2,128,128]{3,2,1,0:T(8,128)(2,1)S(1)}, u32[]{:S(2)}, u32[]{:S(2)}) collective-permute-start(bf16[2,2,128,128]{3,2,1,0:T(8,128)(2,1)S(1)} %pad_maximum_fusion.2), channel_id=1, source_target_pairs={{0,8},{4,12},{8,16},{12,20},{16,24},{20,28},{1,9},{5,13},{9,17},{1... | collective-permute-start | bytes 393224 | tf_op jit(solution)/shard_map/ppermute | solution.py:1176
  49.6 4.9 %collective-permute-start.4 = (bf16[1,2,128,128]{3,2,1,0:T(8,128)(2,1)}, bf16[1,2,128,128]{3,2,1,0:T(8,128)(2,1)S(1)}, u32[]{:S(2)}, u32[]{:S(2)}) collective-permute-start(bf16[1,2,128,128]{3,2,1,0:T(8,128)(2,1)} %bitcast.38), channel_id=1, source_target_pairs={{0,12},{4,16},{8,20},{12,24},{16,28},{1,13},{5,17},{9,21},{13,25},... | collective-permute-start | bytes 196616 | tf_op jit(solution)/shard_map/ppermute | solution.py:1176
  63.9 12.4 %collective-permute-done.6.other = bf16[256,1024]{1,0:T(8,128)(2,1)S(1)} collective-permute-done((bf16[256,1024]{1,0:T(8,128)(2,1)S(1)}, bf16[256,1024]{1,0:T(8,128)(2,1)S(1)}, u32[]{:S(2)}, u32[]{:S(2)}) %collective-permute-start.6) | collective-permute-done | bytes 524320 | tf_op jit(solution)/shard_map/ppermute | solution.py:1180
  78.7 7.2 %feed.1 = (bf16[512,1024]{1,0:T(8,128)(2,1)S(1)}, bf16[1056,512]{1,0:T(8,128)(2,1)S(1)}, bf16[1056,512]{1,0:T(8,128)(2,1)S(1)}, bf16[256,1024]{1,0:T(8,128)(2,1)...) custom-call(bf16[256,1024]{1,0:T(8,128)(2,1)S(1)} %get-tuple-element.209.own, ...), custom_call_target="tpu_custom_call" | custom-call | flops 69206016 | bytes 199680 | tf_op jit(solution)/shard_map/feed/pallas_call | solution.py:666
  86.0 5.1 %collective-permute-done.14.normed_mine = bf16[256,1024]{1,0:T(8,128)(2,1)S(1)} collective-permute-done((bf16[256,1024]{1,0:T(8,128)(2,1)S(1)}, bf16[256,1024]{1,0:T(8,128)(2,1)S(1)}, u32[]{:S(2)}, u32[]{:S(2)}) %collective-permute-start.14) | collective-permute-done | bytes 524320 | tf_op jit(solution)/shard_map/ppermute | solution.py:1180
  94.2 11.7 %collective-permute-done.12.other = bf16[256,1024]{1,0:T(8,128)(2,1)S(1)} collective-permute-done((bf16[256,1024]{1,0:T(8,128)(2,1)S(1)}, bf16[256,1024]{1,0:T(8,128)(2,1)S(1)}, u32[]{:S(2)}, u32[]{:S(2)}) %collective-permute-start.12) | collective-permute-done | bytes 524320 | tf_op jit(solution)/shard_map/ppermute | solution.py:1180
  112.2 4.3 %collective-permute-done.15.d_near = bf16[1056,512]{1,0:T(8,128)(2,1)S(1)} collective-permute-done((bf16[1056,512]{1,0:T(8,128)(2,1)S(1)}, bf16[1056,512]{1,0:T(8,128)(2,1)S(1)}, u32[]{:S(2)}, u32[]{:S(2)}) %collective-permute-start.15) | collective-permute-done | bytes 1081376 | tf_op jit(solution)/shard_map/ppermute | solution.py:1180
  116.5 3.7 %feed_weights.1 = bf16[1056,1024]{1,0:T(8,128)(2,1)} custom-call(bf16[1056,512]{1,0:T(8,128)(2,1)S(1)} %get-tuple-element.253.d_own, bf16[512,1024]{1,0:T(8,128)(2,1)S(1)} %get-tuple-element.254.normed, bf16[512,1024]{1,0:T(8,128)(2,1)S(1)} %copy-done, bf16[1056,512]{1,0:T(8,128)(2,1)S(1)} %collective-permute-done.15.d_near, ...), custom_call_target="tpu_custom_call" | custom-call | flops 34603008 | bytes 133120 | tf_op jit(solution)/shard_map/feed_weights/pallas_call | solution.py:666
  132.0 2.7 collective-permute-start.25
  134.8 4.9 %collective-permute-done.19.rest_1_ = bf16[2,128,128]{2,1,0:T(8,128)(2,1)S(1)} collective-permute-done((bf16[2,128,128]{2,1,0:T(8,128)(2,1)S(1)}, bf16[2,128,128]{2,1,0:T(8,128)(2,1)S(1)}, u32[]{:S(2)}, u32[]{:S(2)}) %collective-permute-start.19) | collective-permute-done | bytes 65568 | tf_op jit(solution)/shard_map/ppermute | solution.py:1176
  142.2 27.2 %mixer_back.1 = (bf16[512,768]{1,0:T(8,128)(2,1)}, bf16[512,512]{1,0:T(8,128)(2,1)}, f32[16,1280]{1,0:T(8,128)}, f32[8,1280]{1,0:T(8,128)}, bf16[512,128]{1,0:T(...) custom-call(s32[10]{0:T(128)} %starts.3, f32[2]{0:T(128)} %log_rate.3, f32[2]{0:T(128)} %bias.3, ...), custom_call_target="tpu_custom_call" | custom-call | flops 2000000000 | bytes 4000000 | tf_op jit(solution)/shard_map/mixer_back/pallas_call | solution.py:639
  173.5 9.8 %collective-permute-start.26 = (bf16[4,768,128]{2,1,0:T(8,128)(2,1)S(1)}, bf16[4,768,128]{2,1,0:T(8,128)(2,1)S(1)}, u32[]{:S(2)}, u32[]{:S(2)}) collective-permute-start(bf16[4,768,128]{2,1,0:T(8,128)(2,1)S(1)} %get-tuple-element.277), channel_id=1, source_target_pairs={{0,4},{4,0},{8,12},{12,8},{16,20},{20,16},{24,28},{28,24},{1,5},{5... | collective-permute-start | bytes 2359304 | tf_op jit(solution)/shard_map/ppermute | solution.py:1180
  189.1 12.4 %collective-permute-done.26.got = bf16[4,768,128]{2,1,0:T(8,128)(2,1)S(1)} collective-permute-done((bf16[4,768,128]{2,1,0:T(8,128)(2,1)S(1)}, bf16[4,768,128]{2,1,0:T(8,128)(2,1)S(1)}, u32[]{:S(2)}, u32[]{:S(2)}) %collective-permute-start.26) | collective-permute-done | bytes 786464 | tf_op jit(solution)/shard_map/ppermute | solution.py:1180
  204.3 2.9 collective-permute-done.24.got
  211.5 4.3 %all-reduce.6.cloned.1.call-done.mine = bf16[1056,1024]{1,0:T(8,128)(2,1)} async-done(((bf16[1056,1024]{1,0:T(8,128)(2,1)}), bf16[1056,1024]{1,0:T(8,128)(2,1)}) %all-reduce.6.cloned.1.call-update) | async-done | bytes 2162704 | tf_op jit(solution)/shard_map/psum | solution.py:1257
  226.3 2.6 collective-permute-start.36
  229.7 2.8 collective-permute-done.28.other
  232.5 2.6 finish.1
  235.1 7.9 %collective-permute-done.36.got = bf16[1,768,128]{2,1,0:T(8,128)(2,1)S(1)} collective-permute-done((bf16[1,768,128]{2,1,0:T(8,128)(2,1)S(1)}, bf16[1,768,128]{2,1,0:T(8,128)(2,1)S(1)}, u32[]{:S(2)}, u32[]{:S(2)}) %collective-permute-start.36) | collective-permute-done | bytes 196640 | tf_op jit(solution)/shard_map/ppermute | solution.py:1180
  243.3 3.8 %collective-permute-start.35 = (bf16[1,512,128]{2,1,0:T(8,128)(2,1)S(1)}, bf16[1,512,128]{2,1,0:T(8,128)(2,1)S(1)}, u32[]{:S(2)}, u32[]{:S(2)}) collective-permute-start(bf16[1,512,128]{2,1,0:T(8,128)(2,1)S(1)} %get-tuple-element.329), channel_id=1, source_target_pairs={{0,24},{4,28},{8,16},{12,20},{16,8},{20,12},{24,0},{28,4},{1,25},{... | collective-permute-start | bytes 393224 | tf_op jit(solution)/shard_map/ppermute | solution.py:1180
  250.4 3.7 %collective-permute-done.35.got = bf16[1,512,128]{2,1,0:T(8,128)(2,1)S(1)} collective-permute-done((bf16[1,512,128]{2,1,0:T(8,128)(2,1)S(1)}, bf16[1,512,128]{2,1,0:T(8,128)(2,1)S(1)}, u32[]{:S(2)}, u32[]{:S(2)}) %collective-permute-start.35) | collective-permute-done | bytes 131104 | tf_op jit(solution)/shard_map/ppermute | solution.py:1180
  258.5 8.7 %collective-permute-start.37 = (f32[8,1280]{1,0:T(8,128)S(1)}, f32[8,1280]{1,0:T(8,128)S(1)}, u32[]{:S(2)}, u32[]{:S(2)}) collective-permute-start(f32[8,1280]{1,0:T(8,128)S(1)} %add.60), channel_id=1, source_target_pairs={{0,16},{4,20},{8,24},{12,28},{16,0},{20,4},{24,8},{28,12},{1,17},{... | collective-permute-start | bytes 122888 | tf_op jit(solution)/shard_map/ppermute | solution.py:1180
  269.9 2.4 collective-permute-start.42
  276.0 3.1 collective-permute-done.44
  280.8 3.0 collective-permute-done.43
  285.2 6.9 %collective-permute-done.42 = bf16[2,528,128]{2,1,0:T(8,128)(2,1)S(1)} collective-permute-done((bf16[2,528,128]{2,1,0:T(8,128)(2,1)S(1)}, bf16[2,528,128]{2,1,0:T(8,128)(2,1)S(1)}, u32[]{:S(2)}, u32[]{:S(2)}) %collective-permute-start.42) | collective-permute-done | bytes 270368 | tf_op jit(solution)/shard_map/ppermute | solution.py:1180
  294.1 3.9 %feed_out.1 = (f32[704,1024]{1,0:T(8,128)}, f32[704,1024]{1,0:T(8,128)}, f32[704,1024]{1,0:T(8,128)}) custom-call(bf16[1056,1024]{1,0:T(8,128)(2,1)S(1)} %copy-done.7, bf16[1056,1024]{1,0:T(8,128)(2,1)S(1)} %collective-permute-done.45.other), custom_call_target="tpu_custom_call" | custom-call | bytes 202752 | tf_op jit(solution)/shard_map/feed_out/pallas_call | solution.py:666
  298.7 2.9 collective-permute-done.50
  (256 shorter events, 95.6 us)
Async XLA Ops:
  7.2 208.7 %all-reduce.6.cloned.1.call-start = ((), (), s32[]{:S(2)}) async-start(), calls=%async_computation | async-start | bytes 4325376 | tf_op jit(solution)/shard_map/psum | solution.py:1257
  19.1 21.6 %collective-permute-start.1 = (bf16[256,1024]{1,0:T(8,128)(2,1)S(1)}, bf16[256,1024]{1,0:T(8,128)(2,1)S(1)}, u32[]{:S(2)}, u32[]{:S(2)}) collective-permute-start(bf16[256,1024]{1,0:T(8,128)(2,1)S(1)} %constant_dynamic-slice_fusion), channel_id=1, source_target_pairs={{0,4},{4,0},{8,12},{12,8},{16,20},{20,16},{24,28},{28,24},{1,5},{5... | collective-permute-start | bytes 1572872 | tf_op jit(solution)/shard_map/ppermute | solution.py:1180
  41.8 14.7 %collective-permute-start.2 = (bf16[2,2,128,128]{3,2,1,0:T(8,128)(2,1)S(1)}, bf16[2,2,128,128]{3,2,1,0:T(8,128)(2,1)S(1)}, u32[]{:S(2)}, u32[]{:S(2)}) collective-permute-start(bf16[2,2,128,128]{3,2,1,0:T(8,128)(2,1)S(1)} %pad_maximum_fusion.2), channel_id=1, source_target_pairs={{0,4},{4,8},{8,12},{12,16},{16,20},{20,24},{24,28},{1,5},{5,9},{9,... | collective-permute-start | bytes 393224 | tf_op jit(solution)/shard_map/ppermute | solution.py:1176
  62.3 14.0 %collective-permute-start.6 = (bf16[256,1024]{1,0:T(8,128)(2,1)S(1)}, bf16[256,1024]{1,0:T(8,128)(2,1)S(1)}, u32[]{:S(2)}, u32[]{:S(2)}) collective-permute-start(bf16[256,1024]{1,0:T(8,128)(2,1)S(1)} %add_convert_fusion.4.mine), channel_id=1, source_target_pairs={{0,2},{1,3},{2,0},{3,1},{4,6},{5,7},{6,4},{7,5},{8,10},{9,11},{10,... | collective-permute-start | bytes 1572872 | tf_op jit(solution)/shard_map/ppermute | solution.py:1180
  76.7 14.3 %collective-permute-start.14 = (bf16[256,1024]{1,0:T(8,128)(2,1)S(1)}, bf16[256,1024]{1,0:T(8,128)(2,1)S(1)}, u32[]{:S(2)}, u32[]{:S(2)}) collective-permute-start(bf16[256,1024]{1,0:T(8,128)(2,1)S(1)} %get-tuple-element.209.own), channel_id=1, source_target_pairs={{0,4},{4,0},{8,12},{12,8},{16,20},{20,16},{24,28},{28,24},{1,5},{5... | collective-permute-start | bytes 1572872 | tf_op jit(solution)/shard_map/ppermute | solution.py:1180
  91.1 25.4 %collective-permute-start.15 = (bf16[1056,512]{1,0:T(8,128)(2,1)S(1)}, bf16[1056,512]{1,0:T(8,128)(2,1)S(1)}, u32[]{:S(2)}, u32[]{:S(2)}) collective-permute-start(bf16[1056,512]{1,0:T(8,128)(2,1)S(1)} %get-tuple-element.250), channel_id=1, source_target_pairs={{0,4},{4,0},{8,12},{12,8},{16,20},{20,16},{24,28},{28,24},{1,5},{5... | collective-permute-start | bytes 3244040 | tf_op jit(solution)/shard_map/ppermute | solution.py:1180
  92.6 13.3 %collective-permute-start.12 = (bf16[256,1024]{1,0:T(8,128)(2,1)S(1)}, bf16[256,1024]{1,0:T(8,128)(2,1)S(1)}, u32[]{:S(2)}, u32[]{:S(2)}) collective-permute-start(bf16[256,1024]{1,0:T(8,128)(2,1)S(1)} %add_convert_fusion.1.mine), channel_id=1, source_target_pairs={{0,2},{1,3},{2,0},{3,1},{4,6},{5,7},{6,4},{7,5},{8,10},{9,11},{10,... | collective-permute-start | bytes 1572872 | tf_op jit(solution)/shard_map/ppermute | solution.py:1180
  124.3 15.4 %collective-permute-start.19 = (bf16[2,128,128]{2,1,0:T(8,128)(2,1)S(1)}, bf16[2,128,128]{2,1,0:T(8,128)(2,1)S(1)}, u32[]{:S(2)}, u32[]{:S(2)}) collective-permute-start(bf16[2,128,128]{2,1,0:T(8,128)(2,1)S(1)} %get-tuple-element.267), channel_id=1, source_target_pairs={{8,0},{12,4},{16,8},{20,12},{24,16},{28,20},{9,1},{13,5},{17,9},{2... | collective-permute-start | bytes 196616 | tf_op jit(solution)/shard_map/ppermute | solution.py:1176
  125.6 16.0 %collective-permute-start.20 = (bf16[2,128,128]{2,1,0:T(8,128)(2,1)S(1)}, bf16[2,128,128]{2,1,0:T(8,128)(2,1)S(1)}, u32[]{:S(2)}, u32[]{:S(2)}) collective-permute-start(bf16[2,128,128]{2,1,0:T(8,128)(2,1)S(1)} %get-tuple-element.267), channel_id=1, source_target_pairs={{12,0},{16,4},{20,8},{24,12},{28,16},{13,1},{17,5},{21,9},{25,13},... | collective-permute-start | bytes 196616 | tf_op jit(solution)/shard_map/ppermute | solution.py:1176
  131.4 53.2 %collective-permute-start.8 = (bf16[256,1024]{1,0:T(8,128)(2,1)}, bf16[256,1024]{1,0:T(8,128)(2,1)}, u32[]{:S(2)}, u32[]{:S(2)}) collective-permute-start(bf16[256,1024]{1,0:T(8,128)(2,1)} %get-tuple-element.211), channel_id=1, source_target_pairs={{0,1},{1,0},{2,3},{3,2},{4,5},{5,4},{6,7},{7,6},{8,9},{9,8},{10,11... | collective-permute-start | bytes 1572872 | tf_op jit(solution)/shard_map/ppermute | solution.py:1180
  132.0 70.3 %collective-permute-start.25 = (bf16[4,512,128]{2,1,0:T(8,128)(2,1)}, bf16[4,512,128]{2,1,0:T(8,128)(2,1)}, u32[]{:S(2)}, u32[]{:S(2)}) collective-permute-start(bf16[4,512,128]{2,1,0:T(8,128)(2,1)} %get-tuple-element.265), channel_id=1, source_target_pairs={{0,4},{4,0},{8,12},{12,8},{16,20},{20,16},{24,28},{28,24},{1,5},{5... | collective-permute-start | bytes 1572872 | tf_op jit(solution)/shard_map/ppermute | solution.py:1180
  173.5 27.9 %collective-permute-start.26 = (bf16[4,768,128]{2,1,0:T(8,128)(2,1)S(1)}, bf16[4,768,128]{2,1,0:T(8,128)(2,1)S(1)}, u32[]{:S(2)}, u32[]{:S(2)}) collective-permute-start(bf16[4,768,128]{2,1,0:T(8,128)(2,1)S(1)} %get-tuple-element.277), channel_id=1, source_target_pairs={{0,4},{4,0},{8,12},{12,8},{16,20},{20,16},{24,28},{28,24},{1,5},{5... | collective-permute-start | bytes 2359304 | tf_op jit(solution)/shard_map/ppermute | solution.py:1180
  184.5 22.8 %collective-permute-start.24 = (bf16[4,528,128]{2,1,0:T(8,128)(2,1)S(1)}, bf16[4,528,128]{2,1,0:T(8,128)(2,1)S(1)}, u32[]{:S(2)}, u32[]{:S(2)}) collective-permute-start(bf16[4,528,128]{2,1,0:T(8,128)(2,1)S(1)} %get-tuple-element.284), channel_id=1, source_target_pairs={{0,4},{4,0},{8,12},{12,8},{16,20},{20,16},{24,28},{28,24},{1,5},{5... | collective-permute-start | bytes 1622024 | tf_op jit(solution)/shard_map/ppermute | solution.py:1180
  185.9 24.0 %collective-permute-start.9 = (bf16[256,1024]{1,0:T(8,128)(2,1)S(1)}, bf16[256,1024]{1,0:T(8,128)(2,1)S(1)}, u32[]{:S(2)}, u32[]{:S(2)}) collective-permute-start(bf16[256,1024]{1,0:T(8,128)(2,1)S(1)} %add_convert_fusion.3), channel_id=1, source_target_pairs={{0,2},{1,3},{2,0},{3,1},{4,6},{5,7},{6,4},{7,5},{8,10},{9,11},{10,... | collective-permute-start | bytes 1572872 | tf_op jit(solution)/shard_map/ppermute | solution.py:1180
  187.5 20.2 %collective-permute-start.23 = (f32[8,1280]{1,0:T(8,128)S(1)}, f32[8,1280]{1,0:T(8,128)S(1)}, u32[]{:S(2)}, u32[]{:S(2)}) collective-permute-start(f32[8,1280]{1,0:T(8,128)S(1)} %copy-done.53), channel_id=1, source_target_pairs={{4,0},{8,4},{12,8},{16,12},{20,16},{24,20},{28,24},{5,1},{9,5},{13... | collective-permute-start | bytes 122888 | tf_op jit(solution)/shard_map/ppermute | solution.py:1176
  211.5 13.6 %collective-permute-start.33 = (bf16[2,768,128]{2,1,0:T(8,128)(2,1)}, bf16[2,768,128]{2,1,0:T(8,128)(2,1)}, u32[]{:S(2)}, u32[]{:S(2)}) collective-permute-start(bf16[2,768,128]{2,1,0:T(8,128)(2,1)} %get-tuple-element.289), channel_id=1, source_target_pairs={{0,8},{4,12},{8,0},{12,4},{16,24},{20,28},{24,16},{28,20},{1,9},{5... | collective-permute-start | bytes 1179656 | tf_op jit(solution)/shard_map/ppermute | solution.py:1180
  215.9 63.3 %collective-permute-start.45 = (bf16[1056,1024]{1,0:T(8,128)(2,1)}, bf16[1056,1024]{1,0:T(8,128)(2,1)S(1)}, u32[]{:S(2)}, u32[]{:S(2)}) collective-permute-start(bf16[1056,1024]{1,0:T(8,128)(2,1)} %all-reduce.6.cloned.1.call-done.mine), channel_id=1, source_target_pairs={{0,4},{4,0},{8,12},{12,8},{16,20},{20,16},{24,28},{28,24},{1,5},{5... | collective-permute-start | bytes 6488072 | tf_op jit(solution)/shard_map/ppermute | solution.py:1180
  218.8 13.7 %collective-permute-start.28 = (bf16[256,1024]{1,0:T(8,128)(2,1)}, bf16[256,1024]{1,0:T(8,128)(2,1)}, u32[]{:S(2)}, u32[]{:S(2)}) collective-permute-start(bf16[256,1024]{1,0:T(8,128)(2,1)} %add_convert_fusion.mine), channel_id=1, source_target_pairs={{0,2},{1,3},{2,0},{3,1},{4,6},{5,7},{6,4},{7,5},{8,10},{9,11},{10,... | collective-permute-start | bytes 1572872 | tf_op jit(solution)/shard_map/ppermute | solution.py:1180
  223.1 24.0 %collective-permute-start.31 = (bf16[2,528,128]{2,1,0:T(8,128)(2,1)}, bf16[2,528,128]{2,1,0:T(8,128)(2,1)S(1)}, u32[]{:S(2)}, u32[]{:S(2)}) collective-permute-start(bf16[2,528,128]{2,1,0:T(8,128)(2,1)} %copy-done.45), channel_id=1, source_target_pairs={{0,8},{4,12},{8,0},{12,4},{16,24},{20,28},{24,16},{28,20},{1,9},{5... | collective-permute-start | bytes 811016 | tf_op jit(solution)/shard_map/ppermute | solution.py:1180
  223.6 19.6 %collective-permute-start.32 = (bf16[2,512,128]{2,1,0:T(8,128)(2,1)}, bf16[2,512,128]{2,1,0:T(8,128)(2,1)S(1)}, u32[]{:S(2)}, u32[]{:S(2)}) collective-permute-start(bf16[2,512,128]{2,1,0:T(8,128)(2,1)} %copy-done.46), channel_id=1, source_target_pairs={{0,8},{4,12},{8,0},{12,4},{16,24},{20,28},{24,16},{28,20},{1,9},{5... | collective-permute-start | bytes 786440 | tf_op jit(solution)/shard_map/ppermute | solution.py:1180
  226.3 16.7 %collective-permute-start.36 = (bf16[1,768,128]{2,1,0:T(8,128)(2,1)S(1)}, bf16[1,768,128]{2,1,0:T(8,128)(2,1)S(1)}, u32[]{:S(2)}, u32[]{:S(2)}) collective-permute-start(bf16[1,768,128]{2,1,0:T(8,128)(2,1)S(1)} %get-tuple-element.326), channel_id=1, source_target_pairs={{0,24},{4,28},{8,16},{12,20},{16,8},{20,12},{24,0},{28,4},{1,25},{... | collective-permute-start | bytes 589832 | tf_op jit(solution)/shard_map/ppermute | solution.py:1180
  243.0 15.5 %collective-permute-start.40 = (bf16[1,768,128]{2,1,0:T(8,128)(2,1)S(1)}, bf16[1,768,128]{2,1,0:T(8,128)(2,1)S(1)}, u32[]{:S(2)}, u32[]{:S(2)}) collective-permute-start(bf16[1,768,128]{2,1,0:T(8,128)(2,1)S(1)} %fold.15), channel_id=1, source_target_pairs={{0,24},{4,28},{8,16},{12,20},{16,8},{20,12},{24,0},{28,4},{1,25},{... | collective-permute-start | bytes 589832 | tf_op jit(solution)/shard_map/ppermute | solution.py:1180
  254.1 18.3 %collective-permute-start.29 = (bf16[256,1024]{1,0:T(8,128)(2,1)}, bf16[256,1024]{1,0:T(8,128)(2,1)S(1)}, u32[]{:S(2)}, u32[]{:S(2)}) collective-permute-start(bf16[256,1024]{1,0:T(8,128)(2,1)} %get-tuple-element.315), channel_id=1, source_target_pairs={{0,1},{1,0},{2,3},{3,2},{4,5},{5,4},{6,7},{7,6},{8,9},{9,8},{10,11... | collective-permute-start | bytes 1572872 | tf_op jit(solution)/shard_map/ppermute | solution.py:1180
  255.5 11.8 %collective-permute-start.39 = (bf16[1,512,128]{2,1,0:T(8,128)(2,1)S(1)}, bf16[1,512,128]{2,1,0:T(8,128)(2,1)S(1)}, u32[]{:S(2)}, u32[]{:S(2)}) collective-permute-start(bf16[1,512,128]{2,1,0:T(8,128)(2,1)S(1)} %fold.16), channel_id=1, source_target_pairs={{0,24},{4,28},{8,16},{12,20},{16,8},{20,12},{24,0},{28,4},{1,25},{... | collective-permute-start | bytes 393224 | tf_op jit(solution)/shard_map/ppermute | solution.py:1180
  257.0 12.6 %collective-permute-start.38 = (bf16[1,528,128]{2,1,0:T(8,128)(2,1)S(1)}, bf16[1,528,128]{2,1,0:T(8,128)(2,1)S(1)}, u32[]{:S(2)}, u32[]{:S(2)}) collective-permute-start(bf16[1,528,128]{2,1,0:T(8,128)(2,1)S(1)} %fold.17), channel_id=1, source_target_pairs={{0,4},{4,0},{8,12},{12,8},{16,20},{20,16},{24,28},{28,24},{1,5},{5... | collective-permute-start | bytes 405512 | tf_op jit(solution)/shard_map/ppermute | solution.py:1180
  267.3 11.8 %collective-permute-start.44 = (bf16[2,768,128]{2,1,0:T(8,128)(2,1)S(1)}, bf16[2,768,128]{2,1,0:T(8,128)(2,1)S(1)}, u32[]{:S(2)}, u32[]{:S(2)}) collective-permute-start(bf16[2,768,128]{2,1,0:T(8,128)(2,1)S(1)} %constant_dynamic-update-slice_fusion), channel_id=1, source_target_pairs={{0,8},{4,12},{8,0},{12,4},{16,24},{20,28},{24,16},{28,20},{1,9},{5... | collective-permute-start | bytes 1179656 | tf_op jit(solution)/shard_map/ppermute | solution.py:1180
  269.6 14.2 %collective-permute-start.43 = (bf16[2,512,128]{2,1,0:T(8,128)(2,1)S(1)}, bf16[2,512,128]{2,1,0:T(8,128)(2,1)S(1)}, u32[]{:S(2)}, u32[]{:S(2)}) collective-permute-start(bf16[2,512,128]{2,1,0:T(8,128)(2,1)S(1)} %constant_dynamic-update-slice_fusion.2), channel_id=1, source_target_pairs={{0,8},{4,12},{8,0},{12,4},{16,24},{20,28},{24,16},{28,20},{1,9},{5... | collective-permute-start | bytes 786440 | tf_op jit(solution)/shard_map/ppermute | solution.py:1180
  269.9 22.2 %collective-permute-start.42 = (bf16[2,528,128]{2,1,0:T(8,128)(2,1)S(1)}, bf16[2,528,128]{2,1,0:T(8,128)(2,1)S(1)}, u32[]{:S(2)}, u32[]{:S(2)}) collective-permute-start(bf16[2,528,128]{2,1,0:T(8,128)(2,1)S(1)} %constant_dynamic-update-slice_fusion.4), channel_id=1, source_target_pairs={{0,24},{4,28},{8,16},{12,20},{16,8},{20,12},{24,0},{28,4},{1,25},{... | collective-permute-start | bytes 811016 | tf_op jit(solution)/shard_map/ppermute | solution.py:1180
  272.3 19.9 %collective-permute-start.41 = (f32[8,1280]{1,0:T(8,128)S(1)}, f32[8,1280]{1,0:T(8,128)S(1)}, u32[]{:S(2)}, u32[]{:S(2)}) collective-permute-start(f32[8,1280]{1,0:T(8,128)S(1)} %add.61), channel_id=1, source_target_pairs={{0,4},{4,0},{8,12},{12,8},{16,20},{20,16},{24,28},{28,24},{1,5},{5... | collective-permute-start | bytes 122888 | tf_op jit(solution)/shard_map/ppermute | solution.py:1180
  279.2 28.1 %collective-permute-start.47 = (bf16[4,768,128]{2,1,0:T(8,128)(2,1)S(1)}, bf16[4,768,128]{2,1,0:T(8,128)(2,1)S(1)}, u32[]{:S(2)}, u32[]{:S(2)}) collective-permute-start(bf16[4,768,128]{2,1,0:T(8,128)(2,1)S(1)} %constant_dynamic-update-slice_fusion.6.mine), channel_id=1, source_target_pairs={{0,4},{4,0},{8,12},{12,8},{16,20},{20,16},{24,28},{28,24},{1,5},{5... | collective-permute-start | bytes 2359304 | tf_op jit(solution)/shard_map/ppermute | solution.py:1180
  283.8 20.3 %collective-permute-start.49 = (bf16[4,512,128]{2,1,0:T(8,128)(2,1)S(1)}, bf16[4,512,128]{2,1,0:T(8,128)(2,1)S(1)}, u32[]{:S(2)}, u32[]{:S(2)}) collective-permute-start(bf16[4,512,128]{2,1,0:T(8,128)(2,1)S(1)} %constant_dynamic-update-slice_fusion.8.mine), channel_id=1, source_target_pairs={{0,4},{4,0},{8,12},{12,8},{16,20},{20,16},{24,28},{28,24},{1,5},{5... | collective-permute-start | bytes 1572872 | tf_op jit(solution)/shard_map/ppermute | solution.py:1180
  292.2 13.5 %collective-permute-start.48 = (bf16[4,528,128]{2,1,0:T(8,128)(2,1)S(1)}, bf16[4,528,128]{2,1,0:T(8,128)(2,1)S(1)}, u32[]{:S(2)}, u32[]{:S(2)}) collective-permute-start(bf16[4,528,128]{2,1,0:T(8,128)(2,1)S(1)} %constant_dynamic-update-slice_fusion.10.mine), channel_id=1, source_target_pairs={{0,8},{4,12},{8,0},{12,4},{16,24},{20,28},{24,16},{28,20},{1,9},{5... | collective-permute-start | bytes 1622024 | tf_op jit(solution)/shard_map/ppermute | solution.py:1180
  (75 other events, 829.9 us)
Sparse Core Ops, SparseCore 0:
  120.4 95.3 all-reduce.5
